TPU v7x, 32 devices: a whole 2x2x4 slice. The times are simulated.
32 devices in a mesh: groups: 2 (over x), tm: 16 (over z, y, core).
Axes of the slice: x: 2, y: 2, z: 4, core: 2. Of those that a mesh axis runs over, the one named last changes fastest.
Arguments:
- token_ids: int32 [4096, 8], P(('groups', 'tm')), parts along dimension 0, may hold values from 0 to 127
- field_offsets: int32 [16], P('groups'), parts along dimension 0, may hold values from 0 to 896
- embed_table: bfloat16 [1024, 1024], replicated, may hold values from -2.09375 to 2.09375
- w_in: bfloat16 [1024, 3072], P('tm'), may hold values from -0.1875 to 0.1875
- short_taps: float32 [3, 3072], replicated, may hold values from -1 to 1
- filters: bfloat16 [2, 1024, 2048], P(None, 'tm'), may hold values from -1.1 to 1.1
- cotangent: bfloat16 [4096, 1024], P(('groups', 'tm')), parts along dimension 0, may hold values from -0.125 to 0.125
Outputs:
- mixer_out: bfloat16 [4096, 1024], P(('groups', 'tm')), parts along dimension 0
- weight_grads: float32 [2048, 3072], P(('groups', 'tm')), parts along dimension 0
- tap_grads: float32 [6, 3072], P('groups'), parts along dimension 0
- filter_grads: float32 [4, 1024, 2048], P('groups', 'tm'), parts along dimension 0
There are 2 independent parts, one for each index of `groups`. A program takes and returns all parts, laid end to end along the dimension named above; an argument that names none is the same for every part. Nothing has to cross between parts.
All inputs are finite; a program needn't handle non-finite values.
Results may differ from a plain program's by a relative error of at most 0.035.
Values may be sent and summed in bfloat16 or wider, within the bound.
No kernel may reach another device: no remote copies, remote signals or barrier semaphores. Data moves between devices by JAX's collectives and lax.ppermute only.
A program may use at most 128 MiB of HBM per device.

v0:
```python
import math

import jax
import jax.numpy as jnp
from jax import lax
from jax.sharding import PartitionSpec as P

HIGHEST = lax.Precision.HIGHEST


def shifted(value, axis, steps):
    count = lax.axis_size(axis)
    initial, last = (max(0, -steps), min(count, count - steps))
    return lax.ppermute(value, axis, [(source, source + steps) for source in range(initial, last)])


def cis_tables(count_a, count_b, modulus):
    left = jnp.arange(count_a, dtype=jnp.int32)[:, None]
    right = jnp.arange(count_b, dtype=jnp.int32)[None, :]
    angle = 2.0 * math.pi / modulus * (left * right % modulus).astype(jnp.float32)
    return (jnp.cos(angle), jnp.sin(angle))


def build_tables(first_len, second_len, total):
    first_cos, first_sin = cis_tables(first_len, first_len // 2, first_len)
    twist_cos, twist_sin = cis_tables(first_len, second_len, total)
    second_cos, second_sin = cis_tables(second_len, second_len, second_len)
    first_both = jnp.concatenate([first_cos, -first_sin], axis=0)
    forward_second = jnp.concatenate(
        [
            jnp.concatenate([second_cos, -second_sin], axis=1),
            jnp.concatenate([second_sin, second_cos], axis=1),
        ],
        axis=0,
    )
    inverse_second = jnp.concatenate(
        [
            jnp.concatenate([second_cos, second_sin], axis=1),
            jnp.concatenate([-second_sin, second_cos], axis=1),
        ],
        axis=0,
    )
    return (first_both, twist_cos, twist_sin, forward_second, inverse_second)


def spectrum(series, tables):
    first_both, twist_cos, twist_sin, forward_second, inverse_second = tables
    channels, length = series.shape
    rows_k = twist_cos.shape[0]
    half = first_both.shape[1]
    second_len = twist_cos.shape[1]
    blocks = series.reshape(channels, half, length // half)
    part = jnp.einsum("ka,cab->ckb", first_both, blocks, precision=HIGHEST)
    part_re = part[:, :rows_k]
    part_im = part[:, rows_k:]
    turn_re = part_re * twist_cos + part_im * twist_sin
    turn_im = part_im * twist_cos - part_re * twist_sin
    turned = jnp.concatenate([turn_re, turn_im], axis=2)
    result = jnp.einsum("ckb,bm->ckm", turned, forward_second, precision=HIGHEST)
    return (result[:, :, :second_len], result[:, :, second_len:])


def signal_of(pair, tables):
    first_both, twist_cos, twist_sin, forward_second, inverse_second = tables
    spec_re, spec_im = pair
    channels = spec_re.shape[0]
    second_len = twist_cos.shape[1]
    total = twist_cos.shape[0] * second_len
    joined = jnp.concatenate([spec_re, spec_im], axis=2)
    back = jnp.einsum("ckm,mb->ckb", joined, inverse_second, precision=HIGHEST)
    back_re = back[:, :, :second_len]
    back_im = back[:, :, second_len:]
    turn_re = back_re * twist_cos - back_im * twist_sin
    turn_im = back_im * twist_cos + back_re * twist_sin
    turned = jnp.concatenate([turn_re, turn_im], axis=1)
    blocks = jnp.einsum("ka,ckb->cab", first_both, turned, precision=HIGHEST)
    return blocks.reshape(channels, -1) * (1.0 / total)


def product(left, right, conjugate):
    left_re, left_im = left
    right_re, right_im = right
    if conjugate:
        right_im = -right_im
    return (left_re * right_re - left_im * right_im, left_re * right_im + left_im * right_re)


def widen(array):
    return array.astype(jnp.float32)


def local(token_ids, field_offsets, embed_table, w_in, short_taps, filters, cotangent):
    tok_rows, width = cotangent.shape
    peers = lax.axis_size("tm")
    row_index = token_ids + field_offsets[None, :]
    embedded = jnp.sum(jnp.take(embed_table, row_index, axis=0).astype(jnp.float32), axis=1).astype(
        jnp.bfloat16
    )
    block = embedded
    proj = jnp.dot(
        block, lax.all_gather(w_in, "tm", axis=0, tiled=True), preferred_element_type=jnp.float32
    ).astype(jnp.bfloat16)
    before = shifted(proj[tok_rows - 2 :], "tm", 1)
    padded = jnp.concatenate([widen(before), widen(proj)], axis=0)
    mixed = (
        short_taps[0] * padded[2:]
        + short_taps[1] * padded[1 : tok_rows + 1]
        + short_taps[2] * padded[:tok_rows]
    ).astype(jnp.bfloat16)
    values = mixed[:, :width]
    first_gate = mixed[:, width : 2 * width]
    second_gate = mixed[:, 2 * width :]
    total = 2 * tok_rows * peers
    bits = total.bit_length() - 1
    first_len = 1 << (bits + 1) // 2
    second_len = total // first_len
    tables = build_tables(first_len, second_len, total)
    first_spec = spectrum(widen(filters[0]), tables)
    second_spec = spectrum(widen(filters[1]), tables)

    def split_time(series):
        return series.reshape(tok_rows, peers, -1)

    def channel_major(moved):
        return moved.reshape(moved.shape[0], -1).T

    def time_major(block):
        return block.T.reshape(block.shape[1], 1, block.shape[0])

    def to_channels(series):
        moved = lax.all_to_all(split_time(series), "tm", split_axis=1, concat_axis=0, tiled=True)
        return channel_major(moved)

    def to_time(block):
        moved = lax.all_to_all(time_major(block), "tm", split_axis=0, concat_axis=1, tiled=True)
        return moved.reshape(tok_rows, -1)

    value_spec = spectrum(widen(to_channels(values)), tables)
    first_conv = to_time(
        signal_of(product(value_spec, first_spec, False), tables).astype(jnp.bfloat16)
    )
    first_mix = (widen(first_gate) * widen(first_conv)).astype(jnp.bfloat16)
    mix_spec = spectrum(widen(to_channels(first_mix)), tables)
    second_conv = to_time(
        signal_of(product(mix_spec, second_spec, False), tables).astype(jnp.bfloat16)
    )
    mixer_out = (widen(second_gate) * widen(second_conv)).astype(jnp.bfloat16)
    upstream = widen(cotangent)
    grad_conv2 = (upstream * widen(second_gate)).astype(jnp.bfloat16)
    grad_gate2 = (upstream * widen(second_conv)).astype(jnp.bfloat16)
    grad_spec2 = spectrum(widen(to_channels(grad_conv2)), tables)
    grad_mix = to_time(
        signal_of(product(grad_spec2, second_spec, True), tables).astype(jnp.bfloat16)
    )
    filter_two = signal_of(product(grad_spec2, mix_spec, True), tables)
    grad_gate1 = (widen(grad_mix) * widen(first_conv)).astype(jnp.bfloat16)
    grad_conv1 = (widen(grad_mix) * widen(first_gate)).astype(jnp.bfloat16)
    grad_spec1 = spectrum(widen(to_channels(grad_conv1)), tables)
    grad_values = to_time(
        signal_of(product(grad_spec1, first_spec, True), tables).astype(jnp.bfloat16)
    )
    filter_one = signal_of(product(grad_spec1, value_spec, True), tables)
    filter_grads = jnp.stack([filter_one, filter_two], axis=0)
    grad_mixed = jnp.concatenate([grad_values, grad_gate1, grad_gate2], axis=1)
    after = shifted(grad_mixed[:2], "tm", -1)
    grad_wide = widen(grad_mixed)
    grad_padded = jnp.concatenate([grad_wide, widen(after)], axis=0)
    grad_proj = (
        short_taps[0] * grad_wide
        + short_taps[1] * grad_padded[1 : tok_rows + 1]
        + short_taps[2] * grad_padded[2:]
    ).astype(jnp.bfloat16)
    tap_terms = jnp.stack(
        [
            jnp.sum(grad_wide * padded[2:], axis=0),
            jnp.sum(grad_wide * padded[1 : tok_rows + 1], axis=0),
            jnp.sum(grad_wide * padded[:tok_rows], axis=0),
        ],
        axis=0,
    )
    tap_grads = lax.psum(tap_terms, "tm")
    block = embedded
    weight_grads = lax.psum_scatter(
        jnp.einsum("tr,tc->rc", block, grad_proj, preferred_element_type=jnp.float32),
        "tm",
        scatter_dimension=0,
        tiled=True,
    )
    return (mixer_out, weight_grads, tap_grads, filter_grads)


def solution(mesh):
    return jax.shard_map(
        local,
        mesh=mesh,
        in_specs=(
            P(("groups", "tm"), None),
            P("groups"),
            P(),
            P("tm", None),
            P(),
            P(None, "tm", None),
            P(("groups", "tm"), None),
        ),
        out_specs=(
            P(("groups", "tm"), None),
            P(("groups", "tm"), None),
            P("groups", None),
            P("groups", "tm", None),
        ),
        check_vma=False,
    )
```

profile of v0, /device:TPU:0, one launch (start us, length us, event | category | flops | bytes accessed | tf_op | source)
XLA Modules:
  0.0 535.3 jit_solution(3606033595169535217)
XLA Ops:
  9.0 5.4 %gather_fusion = bf16[1024,1024]{1,0:T(8,128)(2,1)} fusion(bf16[1024,1024]{1,0:T(8,128)(2,1)S(1)} %copy-done, s32[1024]{0:T(1024)S(1)} %broadcast_clamp_fusion), kind=kCustom, calls=%fused_computation | custom fusion | bytes 4198400 | tf_op jit(solution)/shard_map/jit(_take)/gather | solution.py:96
  16.3 2.7 fusion.72
  19.8 55.1 %all-gather.2.cloned.1.call-done = bf16[1024,3072]{1,0:T(8,128)(2,1)} async-done(((bf16[64,3072]{1,0:T(8,128)(2,1)}), bf16[1024,3072]{1,0:T(8,128)(2,1)}) %all-gather.2.cloned.1.call-update) | async-done | bytes 6291472 | tf_op jit(solution)/shard_map/all_gather | solution.py:101
  74.9 3.8 fusion.187
  85.8 5.3 all-to-all-start.4
  93.4 7.6 %all-to-all-done.4 = bf16[128,16,64]{0,2,1:T(8,128)(2,1)} async-done(((bf16[128,16,64]{0,2,1:T(8,128)(2,1)}), bf16[128,16,64]{0,2,1:T(8,128)(2,1)}, u32[]{:S(2)}, u32[]{:S(2)}) %all-to-all-start.4) | async-done | bytes 262176 | tf_op jit(solution)/shard_map/all_to_all | solution.py:131
  107.2 6.7 %fusion.16 = f32[64,64,128]{2,1,0:T(8,128)S(1)} fusion(f32[128,128,1]{1,0,2:T(8,128)S(1)} %get-tuple-element.57, f32[64,64,64]{1,2,0:T(8,128)S(1)} %get-tuple-element.36, f32[64,64,64]{1,2,0:T(8,128)S(1)} %get-tuple-element.35), kind=kOutput, calls=%fused_computation.17 | convolution fusion | flops 805830656 | bytes 4259840 | tf_op jit(solution)/shard_map/ckb,bm->ckm/dot_general | solution.py:59
  113.9 7.2 %fusion.12 = f32[64,64,128]{2,1,0:T(8,128)S(1)} fusion(f32[128,128,1]{1,0,2:T(8,128)S(1)} %get-tuple-element.57, f32[64,64,64]{1,2,0:T(8,128)S(1)} %get-tuple-element.69, f32[64,64,64]{1,2,0:T(8,128)S(1)} %get-tuple-element.70), kind=kOutput, calls=%fused_computation.13 | convolution fusion | flops 805830656 | bytes 4259840 | tf_op jit(solution)/shard_map/ckb,bm->ckm/dot_general | solution.py:59
  122.5 6.2 %fusion.40 = f32[64,64,128]{1,2,0:T(8,128)S(1)} fusion(f32[128,128,1]{1,0,2:T(8,128)S(1)} %get-tuple-element.58, f32[64,64,64]{2,1,0:T(8,128)S(1)} %get-tuple-element.28, f32[64,64,64]{2,1,0:T(8,128)S(1)} %get-tuple-element.27), kind=kOutput, calls=%fused_computation.42 | convolution fusion | flops 805830656 | bytes 4259840 | tf_op jit(solution)/shard_map/ckm,mb->ckb/dot_general | solution.py:70
  129.8 5.8 %fusion.119 = bf16[64,32,64]{2,1,0:T(8,128)(2,1)S(1)} fusion(f32[128,32,1]{0,1,2:T(8,128)S(1)} %maximum_bitcast_fusion, f32[64,64,64]{1,2,0:T(8,128)S(1)} %get-tuple-element.16, f32[64,64,64]{1,2,0:T(8,128)S(1)} %get-tuple-element.15), kind=kOutput, calls=%fused_computation.148 | convolution fusion | flops 202113024 | bytes 2375680 | tf_op jit(solution)/shard_map/ka,ckb->cab/dot_general | solution.py:76
  142.0 3.5 all-to-all-start.5
  148.7 6.8 %all-to-all-done.5 = bf16[16,2,4096]{2,1,0:T(2,128)(2,1)S(1)} async-done(((bf16[16,2,4096]{2,1,0:T(2,128)(2,1)}), bf16[16,2,4096]{2,1,0:T(2,128)(2,1)S(1)}, u32[]{:S(2)}, u32[]{:S(2)}) %all-to-all-start.5) | async-done | bytes 262176 | tf_op jit(solution)/shard_map/all_to_all | solution.py:135
  155.6 4.2 all-to-all-start
  161.7 3.4 copy.242
  170.9 6.0 %all-to-all-start.6 = ((bf16[128,16,64]{0,2,1:T(8,128)(2,1)}), bf16[128,16,64]{0,2,1:T(8,128)(2,1)}, u32[]{:S(2)}, u32[]{:S(2)}) async-start(bf16[128,16,64]{0,2,1:T(8,128)(2,1)} %bitcast.197), calls=%async_computation.6 | async-start | bytes 524288 | tf_op jit(solution)/shard_map/all_to_all | solution.py:131
  176.9 3.6 convolution_bitcast_fusion.4
  184.6 3.6 convolution_bitcast_fusion.5
  194.8 4.4 multiply_add_fusion.6
  199.3 6.7 %fusion.20 = f32[64,64,128]{2,1,0:T(8,128)S(1)} fusion(f32[128,128,1]{1,0,2:T(8,128)S(1)} %get-tuple-element.57, f32[64,64,64]{1,2,0:T(8,128)S(1)} %get-tuple-element.34, f32[64,64,64]{1,2,0:T(8,128)S(1)} %get-tuple-element.33), kind=kOutput, calls=%fused_computation.21 | convolution fusion | flops 805830656 | bytes 4259840 | tf_op jit(solution)/shard_map/ckb,bm->ckm/dot_general | solution.py:59
  206.0 7.1 %fusion.4 = f32[64,64,128]{2,1,0:T(8,128)S(1)} fusion(f32[128,128,1]{1,0,2:T(8,128)S(1)} %get-tuple-element.57, f32[64,64,64]{1,2,0:T(8,128)S(1)} %get-tuple-element.65, f32[64,64,64]{1,2,0:T(8,128)S(1)} %get-tuple-element.66), kind=kOutput, calls=%fused_computation.5 | convolution fusion | flops 805830656 | bytes 4259840 | tf_op jit(solution)/shard_map/ckb,bm->ckm/dot_general | solution.py:59
  213.0 6.7 %fusion = f32[64,64,128]{2,1,0:T(8,128)S(1)} fusion(f32[128,128,1]{1,0,2:T(8,128)S(1)} %get-tuple-element.57, f32[64,64,64]{1,2,0:T(8,128)S(1)} %get-tuple-element.67, f32[64,64,64]{1,2,0:T(8,128)S(1)} %get-tuple-element.68), kind=kOutput, calls=%fused_computation.1 | convolution fusion | flops 805830656 | bytes 4259840 | tf_op jit(solution)/shard_map/ckb,bm->ckm/dot_general | solution.py:59
  219.7 3.2 multiply_subtract_fusion.5
  222.9 4.1 multiply_subtract_fusion.3
  227.0 8.3 %fusion.48 = f32[64,64,128]{1,2,0:T(8,128)S(1)} fusion(f32[128,128,1]{1,0,2:T(8,128)S(1)} %get-tuple-element.58, f32[64,64,64]{2,1,0:T(8,128)} %get-tuple-element.26, f32[64,64,64]{2,1,0:T(8,128)} %get-tuple-element.25), kind=kOutput, calls=%fused_computation.50 | convolution fusion | flops 805830656 | bytes 4259840 | tf_op jit(solution)/shard_map/ckm,mb->ckb/dot_general | solution.py:70
  235.3 6.2 %fusion.56 = f32[64,64,128]{1,2,0:T(8,128)S(1)} fusion(f32[128,128,1]{1,0,2:T(8,128)S(1)} %get-tuple-element.58, f32[64,64,64]{2,1,0:T(8,128)S(1)} %copy-done.9, f32[64,64,64]{2,1,0:T(8,128)S(1)} %copy-done.8), kind=kOutput, calls=%fused_computation.58 | convolution fusion | flops 805830656 | bytes 4259840 | tf_op jit(solution)/shard_map/ckm,mb->ckb/dot_general | solution.py:70
  241.5 6.2 %fusion.24 = f32[64,64,128]{1,2,0:T(8,128)S(1)} fusion(f32[128,128,1]{1,0,2:T(8,128)S(1)} %get-tuple-element.58, f32[64,64,64]{2,1,0:T(8,128)S(1)} %get-tuple-element.45, f32[64,64,64]{2,1,0:T(8,128)S(1)} %get-tuple-element.46), kind=kOutput, calls=%fused_computation.26 | convolution fusion | flops 805830656 | bytes 4259840 | tf_op jit(solution)/shard_map/ckm,mb->ckb/dot_general | solution.py:70
  247.7 4.6 multiply_subtract_fusion.2
  252.3 6.6 %fusion.125 = bf16[64,32,64]{2,1,0:T(8,128)(2,1)} fusion(f32[128,32,1]{0,1,2:T(8,128)S(1)} %maximum_bitcast_fusion, f32[64,64,64]{1,2,0:T(8,128)S(1)} %get-tuple-element.59, f32[64,64,64]{1,2,0:T(8,128)S(1)} %get-tuple-element.60), kind=kOutput, calls=%fused_computation.150 | convolution fusion | flops 202113024 | bytes 2375680 | tf_op jit(solution)/shard_map/ka,ckb->cab/dot_general | solution.py:76
  267.6 16.1 %all_to_all.102 = bf16[16,2,4096]{2,1,0:T(2,128)(2,1)} all-to-all(bf16[16,2,4096]{2,1,0:T(2,128)(2,1)} %reshape.212), channel_id=1, replica_groups=mesh['groups'=2,'tm'=16] {'tm'}, dimensions={0} | all-to-all | bytes 524288 | tf_op jit(solution)/shard_map/all_to_all | solution.py:135
  283.7 3.4 reshape.213
  287.1 3.4 copy.223
  298.3 4.2 all-to-all-start.2
  302.5 8.0 %fusion.116 = bf16[64,32,64]{2,1,0:T(8,128)(2,1)S(1)} fusion(f32[128,32,1]{0,1,2:T(8,128)S(1)} %maximum_bitcast_fusion, f32[64,64,64]{1,2,0:T(8,128)} %get-tuple-element.61, f32[64,64,64]{1,2,0:T(8,128)} %get-tuple-element.62), kind=kOutput, calls=%fused_computation.147 | convolution fusion | flops 202113024 | bytes 2375680 | tf_op jit(solution)/shard_map/ka,ckb->cab/dot_general | solution.py:76
  316.5 6.4 %all-to-all-start.7 = ((bf16[16,2,4096]{2,1,0:T(2,128)(2,1)}), bf16[16,2,4096]{2,1,0:T(2,128)(2,1)}, u32[]{:S(2)}, u32[]{:S(2)}) async-start(bf16[16,2,4096]{2,1,0:T(2,128)(2,1)} %reshape.218), calls=%async_computation.7 | async-start | bytes 524288 | tf_op jit(solution)/shard_map/all_to_all | solution.py:135
  328.3 6.7 %fusion.8 = f32[64,64,128]{2,1,0:T(8,128)S(1)} fusion(f32[128,128,1]{1,0,2:T(8,128)S(1)} %get-tuple-element.57, f32[64,64,64]{1,2,0:T(8,128)S(1)} %get-tuple-element.38, f32[64,64,64]{1,2,0:T(8,128)S(1)} %get-tuple-element.37), kind=kOutput, calls=%fused_computation.9 | convolution fusion | flops 805830656 | bytes 4259840 | tf_op jit(solution)/shard_map/ckb,bm->ckm/dot_general | solution.py:59
  335.0 3.2 multiply_subtract_fusion.1
  338.2 8.0 %fusion.64 = f32[64,64,128]{1,2,0:T(8,128)S(1)} fusion(f32[128,128,1]{1,0,2:T(8,128)S(1)} %get-tuple-element.58, f32[64,64,64]{2,1,0:T(8,128)} %get-tuple-element.24, f32[64,64,64]{2,1,0:T(8,128)S(1)} %get-tuple-element.23), kind=kOutput, calls=%fused_computation.66 | convolution fusion | flops 805830656 | bytes 4259840 | tf_op jit(solution)/shard_map/ckm,mb->ckb/dot_general | solution.py:70
  346.2 6.2 %fusion.32 = f32[64,64,128]{1,2,0:T(8,128)S(1)} fusion(f32[128,128,1]{1,0,2:T(8,128)S(1)} %get-tuple-element.58, f32[64,64,64]{2,1,0:T(8,128)S(1)} %get-tuple-element.47, f32[64,64,64]{2,1,0:T(8,128)S(1)} %get-tuple-element.48), kind=kOutput, calls=%fused_computation.34 | convolution fusion | flops 805830656 | bytes 4259840 | tf_op jit(solution)/shard_map/ckm,mb->ckb/dot_general | solution.py:70
  352.3 3.2 multiply_subtract_fusion
  355.6 6.0 %fusion.122 = bf16[64,32,64]{2,1,0:T(8,128)(2,1)S(1)} fusion(f32[128,32,1]{0,1,2:T(8,128)S(1)} %maximum_bitcast_fusion, f32[64,64,64]{1,2,0:T(8,128)S(1)} %get-tuple-element.63, f32[64,64,64]{1,2,0:T(8,128)S(1)} %get-tuple-element.64), kind=kOutput, calls=%fused_computation.149 | convolution fusion | flops 202113024 | bytes 2375680 | tf_op jit(solution)/shard_map/ka,ckb->cab/dot_general | solution.py:76
  364.2 5.9 %all-to-all-start.3 = ((bf16[16,2,4096]{2,1,0:T(2,128)(2,1)}), bf16[16,2,4096]{2,1,0:T(2,128)(2,1)S(1)}, u32[]{:S(2)}, u32[]{:S(2)}) async-start(bf16[16,2,4096]{2,1,0:T(2,128)(2,1)} %reshape.214), calls=%async_computation.3 | async-start | bytes 524288 | tf_op jit(solution)/shard_map/all_to_all | solution.py:135
  373.3 6.9 %all-to-all-done.3 = bf16[16,2,4096]{2,1,0:T(2,128)(2,1)S(1)} async-done(((bf16[16,2,4096]{2,1,0:T(2,128)(2,1)}), bf16[16,2,4096]{2,1,0:T(2,128)(2,1)S(1)}, u32[]{:S(2)}, u32[]{:S(2)}) %all-to-all-start.3) | async-done | bytes 262176 | tf_op jit(solution)/shard_map/all_to_all | solution.py:135
  386.6 6.4 %fusion.128 = f32[1024,3072]{1,0:T(8,128)} fusion(bf16[128,1024]{1,0:T(8,128)(2,1)S(1)} %copy-done.11, f32[128,3072]{1,0:T(8,128)S(1)} %get-tuple-element.50, f32[2,3072]{1,0:T(2,128)S(1)} %convert_element_type.300, f32[3072]{0:T(1024)S(1)} %bitcast.207, f32[3072]{0:T(1024)S(1)} %bitcast.209, f32[3072]{0:T(1024)S(1)} %bitcast.205), kind=kOutput, calls=%fused_computation.152 | convolution fusion | flops 808452096 | bytes 14479360 | tf_op jit(solution)/shard_map/tr,tc->rc/dot_general | solution.py:184
  394.7 7.4 %fusion.89 = f32[64,32,64]{2,1,0:T(8,128)S(1)} fusion(f32[128,32,1]{0,1,2:T(8,128)S(1)} %maximum_bitcast_fusion, f32[64,64,64]{1,2,0:T(8,128)} %get-tuple-element.10, f32[64,64,64]{1,2,0:T(8,128)S(1)} %copy-done.7), kind=kOutput, calls=%fused_computation.138 | convolution fusion | flops 201981952 | bytes 2637824 | tf_op jit(solution)/shard_map/ka,ckb->cab/dot_general | solution.py:76
  403.3 8.6 %fusion.83 = f32[64,32,64]{2,1,0:T(8,128)S(1)} fusion(f32[128,32,1]{0,1,2:T(8,128)S(1)} %maximum_bitcast_fusion, f32[64,64,64]{1,2,0:T(8,128)} %get-tuple-element.12, f32[64,64,64]{1,2,0:T(8,128)} %get-tuple-element.11), kind=kOutput, calls=%fused_computation.136 | convolution fusion | flops 201981952 | bytes 2637824 | tf_op jit(solution)/shard_map/ka,ckb->cab/dot_general | solution.py:76
  413.1 2.5 pad_maximum_fusion.2
  416.4 63.6 %psum.7 = f32[3,3072]{1,0:T(4,128)} all-reduce(f32[3,3072]{1,0:T(4,128)S(1)} %pad_maximum_fusion.8), channel_id=1, replica_groups=mesh['groups'=2,'tm'=16] {'tm'}, use_global_device_ids=true, to_apply=%region_5.6 | all-reduce | flops 9216 | bytes 73728 | tf_op jit(solution)/shard_map/psum | solution.py:181
  480.1 48.2 %reduce-scatter.2.cloned.1.call-done = f32[64,3072]{1,0:T(8,128)} async-done(((f32[1024,3072]{1,0:T(8,128)}), f32[64,3072]{1,0:T(8,128)}) %reduce-scatter.2.cloned.1.call-update) | async-done | bytes 786448 | tf_op jit(solution)/shard_map/reduce_scatter | solution.py:183
  (180 shorter events, 94.8 us)
Async XLA Ops:
  7.2 1.9 copy-start
  7.2 67.7 %all-gather.2.cloned.1.call-start = ((), (), s32[]{:S(2)}) async-start(), calls=%async_computation.9 | async-start | bytes 6684672 | tf_op jit(solution)/shard_map/all_gather | solution.py:101
  14.4 4.5 copy-start.27
  14.4 5.3 copy-start.36
  19.0 59.7 %copy-start.10 = (bf16[128,1024]{1,0:T(8,128)(2,1)}, bf16[128,1024]{1,0:T(8,128)(2,1)S(1)}, u32[]{:S(2)}) copy-start(bf16[128,1024]{1,0:T(8,128)(2,1)S(1)} %fusion.72) | copy-start | bytes 786436
  19.8 64.0 %copy-start.30 = (f32[1,3072]{1,0:T(1,128)}, f32[1,3072]{1,0:T(1,128)S(1)}, u32[]{:S(2)}) copy-start(f32[1,3072]{1,0:T(1,128)S(1)} %get-tuple-element.71) | copy-start | bytes 36868
  19.8 64.0 %copy-start.32 = (f32[1,3072]{1,0:T(1,128)}, f32[1,3072]{1,0:T(1,128)S(1)}, u32[]{:S(2)}) copy-start(f32[1,3072]{1,0:T(1,128)S(1)} %get-tuple-element.72) | copy-start | bytes 36868
  19.8 64.0 %copy-start.34 = (f32[1,3072]{1,0:T(1,128)}, f32[1,3072]{1,0:T(1,128)S(1)}, u32[]{:S(2)}) copy-start(f32[1,3072]{1,0:T(1,128)S(1)} %get-tuple-element.73) | copy-start | bytes 36868
  78.7 0.9 copy-start.12
  78.7 6.3 %copy-start.5 = (f32[128,3072]{1,0:T(8,128)}, f32[128,3072]{1,0:T(8,128)S(1)}, u32[]{:S(2)}) copy-start(f32[128,3072]{1,0:T(8,128)S(1)} %get-tuple-element.74) | copy-start | bytes 4718596
  78.7 6.2 %copy-start.25 = (bf16[128,1024]{1,0:T(8,128)(2,1)S(1)}, bf16[128,1024]{1,0:T(8,128)(2,1)}, u32[]{:S(2)}) copy-start(bf16[128,1024]{1,0:T(8,128)(2,1)} %param.13) | copy-start | bytes 786436
  79.6 4.2 collective-permute-start
  83.8 0.6 copy-start.28
  85.8 15.2 %all-to-all-start.4 = ((bf16[128,16,64]{0,2,1:T(8,128)(2,1)}), bf16[128,16,64]{0,2,1:T(8,128)(2,1)}, u32[]{:S(2)}, u32[]{:S(2)}) async-start(bf16[128,16,64]{0,2,1:T(8,128)(2,1)} %bitcast.31), calls=%async_computation.4 | async-start | bytes 524288 | tf_op jit(solution)/shard_map/all_to_all | solution.py:131
  104.4 1.3 copy-start.19
  104.4 1.3 copy-start.22
  121.1 1.4 copy-start.2
  142.0 13.5 %all-to-all-start.5 = ((bf16[16,2,4096]{2,1,0:T(2,128)(2,1)}), bf16[16,2,4096]{2,1,0:T(2,128)(2,1)S(1)}, u32[]{:S(2)}, u32[]{:S(2)}) async-start(bf16[16,2,4096]{2,1,0:T(2,128)(2,1)} %reshape.216), calls=%async_computation.5 | async-start | bytes 524288 | tf_op jit(solution)/shard_map/all_to_all | solution.py:135
  155.6 15.3 %all-to-all-start = ((bf16[128,16,64]{0,2,1:T(8,128)(2,1)}), bf16[128,16,64]{0,2,1:T(8,128)(2,1)}, u32[]{:S(2)}, u32[]{:S(2)}) async-start(bf16[128,16,64]{0,2,1:T(8,128)(2,1)} %bitcast.6), calls=%async_computation | async-start | bytes 524288 | tf_op jit(solution)/shard_map/all_to_all | solution.py:131
  170.9 17.3 %all-to-all-start.6 = ((bf16[128,16,64]{0,2,1:T(8,128)(2,1)}), bf16[128,16,64]{0,2,1:T(8,128)(2,1)}, u32[]{:S(2)}, u32[]{:S(2)}) async-start(bf16[128,16,64]{0,2,1:T(8,128)(2,1)} %bitcast.197), calls=%async_computation.6 | async-start | bytes 524288 | tf_op jit(solution)/shard_map/all_to_all | solution.py:131
  192.4 2.4 copy-start.4
  192.4 2.4 copy-start.20
  192.4 2.4 copy-start.23
  227.0 8.3 %copy-start.8 = (f32[64,64,64]{2,1,0:T(8,128)S(1)}, f32[64,64,64]{2,1,0:T(8,128)}, u32[]{:S(2)}) copy-start(f32[64,64,64]{2,1,0:T(8,128)} %get-tuple-element.21) | copy-start | bytes 3145732
  227.0 8.3 %copy-start.9 = (f32[64,64,64]{2,1,0:T(8,128)S(1)}, f32[64,64,64]{2,1,0:T(8,128)}, u32[]{:S(2)}) copy-start(f32[64,64,64]{2,1,0:T(8,128)} %get-tuple-element.22) | copy-start | bytes 3145732
  298.3 18.1 %all-to-all-start.2 = ((bf16[128,16,64]{0,2,1:T(8,128)(2,1)}), bf16[128,16,64]{0,2,1:T(8,128)(2,1)}, u32[]{:S(2)}, u32[]{:S(2)}) async-start(bf16[128,16,64]{0,2,1:T(8,128)(2,1)} %bitcast.20), calls=%async_computation.2 | async-start | bytes 524288 | tf_op jit(solution)/shard_map/all_to_all | solution.py:131
  316.5 47.8 %all-to-all-start.7 = ((bf16[16,2,4096]{2,1,0:T(2,128)(2,1)}), bf16[16,2,4096]{2,1,0:T(2,128)(2,1)}, u32[]{:S(2)}, u32[]{:S(2)}) async-start(bf16[16,2,4096]{2,1,0:T(2,128)(2,1)} %reshape.218), calls=%async_computation.7 | async-start | bytes 524288 | tf_op jit(solution)/shard_map/all_to_all | solution.py:135
  326.2 1.2 copy-start.21
  326.2 1.2 copy-start.24
  328.3 6.7 %copy-start.3 = (f32[64,64,128]{2,1,0:T(8,128)S(1)}, f32[64,64,128]{2,1,0:T(8,128)}, u32[]{:S(2)}) copy-start(f32[64,64,128]{2,1,0:T(8,128)} %copy-done.2) | copy-start | bytes 6291460
  364.2 16.0 %all-to-all-start.3 = ((bf16[16,2,4096]{2,1,0:T(2,128)(2,1)}), bf16[16,2,4096]{2,1,0:T(2,128)(2,1)S(1)}, u32[]{:S(2)}, u32[]{:S(2)}) async-start(bf16[16,2,4096]{2,1,0:T(2,128)(2,1)} %reshape.214), calls=%async_computation.3 | async-start | bytes 524288 | tf_op jit(solution)/shard_map/all_to_all | solution.py:135
  370.2 158.0 %reduce-scatter.2.cloned.1.call-start = ((), (), s32[]{:S(2)}) async-start(), calls=%async_computation.10 | async-start | bytes 13369344 | tf_op jit(solution)/shard_map/reduce_scatter | solution.py:183
  373.3 10.0 %copy-start.15 = (bf16[128,1024]{1,0:T(8,128)(2,1)}, bf16[128,1024]{1,0:T(8,128)(2,1)S(1)}, u32[]{:S(2)}) copy-start(bf16[128,1024]{1,0:T(8,128)(2,1)S(1)} %copy.256) | copy-start | bytes 786436
  381.5 1.0 copy-start.26
  381.6 1.7 copy-start.14
  382.4 4.2 copy-start.11
  382.4 4.2 copy-start.31
  382.4 4.2 copy-start.33
  382.4 4.2 copy-start.35
  383.3 9.8 %copy-start.17 = (bf16[128,1024]{1,0:T(8,128)(2,1)}, bf16[128,1024]{1,0:T(8,128)(2,1)S(1)}, u32[]{:S(2)}) copy-start(bf16[128,1024]{1,0:T(8,128)(2,1)S(1)} %get-tuple-element.53) | copy-start | bytes 786436
  383.5 3.1 collective-permute-start.1
  393.1 1.6 copy-start.7
  411.9 3.7 copy-start.13
  411.9 3.7 copy-start.16
  411.9 3.7 copy-start.29
  413.1 2.5 copy-start.6
  413.1 2.6 copy-start.18
  413.1 115.1 %copy-start.1 = (bf16[1024,1024]{1,0:T(8,128)(2,1)S(1)}, bf16[1024,1024]{1,0:T(8,128)(2,1)}, u32[]{:S(2)}) copy-start(bf16[1024,1024]{1,0:T(8,128)(2,1)} %param.9) | copy-start | bytes 6291460
Sparse Core Ops, SparseCore 0:
  10.3 64.5 all-gather.1
  393.2 134.9 reduce-scatter.1
where the time goes:
time: 542 us; the launch traced here: 535 us
  matrix products  148 us (27%)
  waiting for transfers between devices  127 us (23%)
  blocking collectives  79.7 us (15%)
  local copies, waits for them, and re-layouts  74.7 us (14%)
  other arithmetic  51.6 us (10%)
  starting transfers between devices  39 us (7%)
  between operations  15.2 us (3%)
    psum x1, blocking collectives, local(): tap_grads = lax.psum(tap_terms, 'tm')  63.6 us
    all_gather x1, waiting for transfers between devices, local(): lax.all_gather(w_in, 'tm', axis=0, tiled=True)  55.1 us
    reduce_scatter x1, waiting for transfers between devices, local(): lax.psum_scatter(jnp.einsum('tr,tc->rc', block, grad_proj, preferred_elem...  48.2 us
    dot_general x6, matrix products, signal_of(): blocks = jnp.einsum('ka,ckb->cab', first_both, turned, precision=HIGHEST)  42.6 us
    dot_general x6, matrix products, signal_of(): back = jnp.einsum('ckm,mb->ckb', joined, inverse_second, precision=HIGHEST)  41 us
    dot_general x6, matrix products, spectrum(): jnp.einsum('ckb,bm->ckm', turned, forward_second, precision=HIGHEST)  40.9 us
    unnamed x94, local copies, waits for them, and re-layouts  25.1 us
    all_to_all x4, starting transfers between devices, to_channels(): lax.all_to_all(split_time(series), 'tm', split_axis=1, concat_axis=0, til...  19.6 us
  transfers between devices with their start and end apart: 11, of which 6 were waited for; matrix products, arithmetic and copies ran while one was open for 23% of the time, Pallas kernels for 0%

commit v1 on v0

v1 whole, which is shorter than its diff:
```python
import jax
import jax.numpy as jnp
import ml_dtypes
import numpy as np
from jax import lax
from jax.experimental import pallas as pl
from jax.experimental.pallas import tpu as pltpu
from jax.sharding import PartitionSpec as P

F32 = jnp.float32
BF16 = jnp.bfloat16
LANES = 128
GROUP = 16
PARAMS = pltpu.CompilerParams(vmem_limit_bytes=48 * 1024 * 1024)


def widen(array):
    return array.astype(F32)


def rounded(array):
    return array.astype(BF16).astype(F32)


def transform_tables(blocks):
    total = 2 * blocks * LANES
    row = np.arange(blocks) + 0.5
    first = np.exp(-2j * np.pi * np.outer(row, np.arange(blocks)) / (2 * blocks))
    turn = np.exp(-2j * np.pi * np.outer(row, np.arange(LANES)) / total)
    second = np.exp(-2j * np.pi * np.outer(np.arange(LANES), np.arange(LANES)) / LANES)
    same = np.eye(GROUP)
    first_rows = np.concatenate([first.real, first.imag], axis=0)
    back_rows = np.concatenate([first.real.T, first.imag.T], axis=1) * (2.0 / total)
    forward = np.block([[second.real, second.imag], [-second.imag, second.real]])
    inverse = np.block([[second.real, -second.imag], [second.imag, second.real]])
    narrow = ml_dtypes.bfloat16
    return (
        np.kron(first_rows, same).astype(narrow),
        np.kron(back_rows, same).astype(narrow),
        forward.astype(narrow),
        inverse.astype(narrow),
        np.repeat(turn.real, GROUP, axis=0).astype(np.float32),
        np.repeat(turn.imag, GROUP, axis=0).astype(np.float32),
    )


def dot(left, right):
    return jnp.dot(left, right, preferred_element_type=F32)


def joined(parts, axis):
    return parts[0] if len(parts) == 1 else jnp.concatenate(parts, axis=axis)


def forward(series, tables):
    first, _, second, _, turn_re, turn_im = tables
    rows = turn_re.shape[0]
    part = dot(first[...], joined(series, 1))
    spectra = []
    for place in range(len(series)):
        lanes = slice(place * LANES, (place + 1) * LANES)
        part_re = part[:rows, lanes]
        part_im = part[rows:, lanes]
        turned = jnp.concatenate(
            [
                part_re * turn_re[...] - part_im * turn_im[...],
                part_re * turn_im[...] + part_im * turn_re[...],
            ],
            axis=1,
        )
        spectra.append(dot(turned.astype(BF16), second[...]))
    return spectra


def inverse(spectra, tables):
    _, last, _, second, turn_re, turn_im = tables
    turned = []
    for spectrum in spectra:
        back = dot(spectrum.astype(BF16), second[...])
        back_re = back[:, :LANES]
        back_im = back[:, LANES:]
        turned.append(
            jnp.concatenate(
                [
                    back_re * turn_re[...] + back_im * turn_im[...],
                    back_im * turn_re[...] - back_re * turn_im[...],
                ],
                axis=0,
            ).astype(BF16)
        )
    signal = dot(last[...], joined(turned, 1))
    return [signal[:, place * LANES : (place + 1) * LANES] for place in range(len(spectra))]


def product(left, right, conjugate):
    left_re, left_im = left[:, :LANES], left[:, LANES:]
    right_re, right_im = right[:, :LANES], right[:, LANES:]
    if conjugate:
        return jnp.concatenate(
            [
                left_re * right_re + left_im * right_im,
                left_im * right_re - left_re * right_im,
            ],
            axis=1,
        )
    return jnp.concatenate(
        [
            left_re * right_re - left_im * right_im,
            left_re * right_im + left_im * right_re,
        ],
        axis=1,
    )


def batches(chans):
    groups = chans // GROUP
    size = 2 if groups % 2 == 0 else 1
    return [range(start, start + size) for start in range(0, groups, size)]


def channel_rows(group, offset=0):
    return slice(offset + group * GROUP, offset + (group + 1) * GROUP)


def flat(block):
    return block.reshape(block.shape[0] * block.shape[1], block.shape[2])


def one_hot(ids, codes):
    fields, lanes = ids.shape
    code = lax.broadcasted_iota(jnp.int32, (codes, lanes), 0).astype(F32)
    return jnp.concatenate(
        [
            jnp.where(code == ids[field : field + 1], 1.0, 0.0).astype(BF16)
            for field in range(fields)
        ],
        axis=0,
    )


def filter_kernel(filters, *rest):
    tables, spectra = rest[:6], rest[6]
    chans, steps = filters.shape[1:]
    blocks = steps // LANES
    for which in range(2):
        for batch in batches(chans):
            series = [
                jnp.concatenate(
                    [
                        filters[which, channel_rows(group), t * LANES : (t + 1) * LANES]
                        for t in range(blocks)
                    ],
                    axis=0,
                )
                for group in batch
            ]
            for group, spectrum in zip(batch, forward(series, tables)):
                spectra[which, group] = spectrum


def forward_kernel(ids, entries, w_cols, taps, filter_spec, *rest):
    tables = rest[:6]
    proj, mixed, first_conv, second_conv, value_spec, mix_spec, mixer_out = rest[6:]
    blocks, fields, _ = ids.shape
    codes = entries.shape[0] // fields
    chans = w_cols.shape[1] // 3
    coded = dot(entries[...], w_cols[...]).T.astype(BF16)
    lane = lax.broadcasted_iota(jnp.int32, (3 * chans, LANES), 1)
    last1 = jnp.zeros((3 * chans, LANES), F32)
    last2 = last1
    for pair in range(blocks // 2):
        hot = jnp.concatenate(
            [one_hot(widen(ids[2 * pair + side]), codes) for side in range(2)], axis=1
        )
        both = dot(coded, hot).astype(BF16)
        for side in range(2):
            block = 2 * pair + side
            now = both[:, side * LANES : (side + 1) * LANES]
            proj[block] = now
            now = widen(now)
            turn1 = pltpu.roll(now, 1, 1)
            turn2 = pltpu.roll(now, 2, 1)
            late1 = jnp.where(lane < 1, last1, turn1)
            late2 = jnp.where(lane < 2, last2, turn2)
            last1, last2 = turn1, turn2
            mixed[block] = (taps[0] * now + taps[1] * late1 + taps[2] * late2).astype(BF16)
    for batch in batches(chans):
        spectra = forward([flat(mixed[:, channel_rows(group), :]) for group in batch], tables)
        turned = []
        for group, spectrum in zip(batch, spectra):
            value_spec[group] = spectrum
            turned.append(product(spectrum, filter_spec[0, group], False))
        series = []
        for group, signal in zip(batch, inverse(turned, tables)):
            conv = signal.astype(BF16)
            first_conv[:, channel_rows(group), :] = conv.reshape(blocks, GROUP, LANES)
            gate = flat(mixed[:, channel_rows(group, chans), :])
            series.append((widen(gate) * widen(conv)).astype(BF16))
        turned = []
        for group, spectrum in zip(batch, forward(series, tables)):
            mix_spec[group] = spectrum
            turned.append(product(spectrum, filter_spec[1, group], False))
        for group, signal in zip(batch, inverse(turned, tables)):
            conv = signal.astype(BF16)
            second_conv[:, channel_rows(group), :] = conv.reshape(blocks, GROUP, LANES)
            gate = flat(mixed[:, channel_rows(group, 2 * chans), :])
            result = (widen(gate) * widen(conv)).astype(BF16)
            mixer_out[:, channel_rows(group), :] = result.reshape(blocks, GROUP, LANES)


def backward_kernel(
    ids, entries, taps, filter_spec, cotangent, proj, mixed, first_conv, second_conv, *rest
):
    tables = rest[:6]
    weight_part, tap_terms, grad_spec, grad_mixed, grad_proj, hot = rest[6:]
    blocks, fields, _ = ids.shape
    codes = entries.shape[0] // fields
    chans = cotangent.shape[1]
    for batch in batches(chans):
        series = []
        for group in batch:
            upstream = widen(flat(cotangent[:, channel_rows(group), :]))
            gate = widen(flat(mixed[:, channel_rows(group, 2 * chans), :]))
            conv = widen(flat(second_conv[:, channel_rows(group), :]))
            series.append((upstream * gate).astype(BF16))
            grad_mixed[:, channel_rows(group, 2 * chans), :] = (
                (upstream * conv).astype(BF16).reshape(blocks, GROUP, LANES)
            )
        turned = []
        for group, spectrum in zip(batch, forward(series, tables)):
            grad_spec[1, group] = spectrum
            turned.append(product(spectrum, filter_spec[1, group], True))
        series = []
        for group, signal in zip(batch, inverse(turned, tables)):
            grad_mix = rounded(signal)
            gate = widen(flat(mixed[:, channel_rows(group, chans), :]))
            conv = widen(flat(first_conv[:, channel_rows(group), :]))
            series.append((grad_mix * gate).astype(BF16))
            grad_mixed[:, channel_rows(group, chans), :] = (
                (grad_mix * conv).astype(BF16).reshape(blocks, GROUP, LANES)
            )
        turned = []
        for group, spectrum in zip(batch, forward(series, tables)):
            grad_spec[0, group] = spectrum
            turned.append(product(spectrum, filter_spec[0, group], True))
        for group, signal in zip(batch, inverse(turned, tables)):
            grad_mixed[:, channel_rows(group), :] = signal.astype(BF16).reshape(
                blocks, GROUP, LANES
            )
    lane = lax.broadcasted_iota(jnp.int32, (3 * chans, LANES), 1)
    next1 = jnp.zeros((3 * chans, LANES), F32)
    next2 = next1
    sums = [next1] * 3
    for block in reversed(range(blocks)):
        lanes = slice(block * LANES, (block + 1) * LANES)
        hot[:, lanes] = one_hot(widen(ids[block]), codes)
        now = widen(grad_mixed[block])
        turn1 = pltpu.roll(now, LANES - 1, 1)
        turn2 = pltpu.roll(now, LANES - 2, 1)
        soon1 = jnp.where(lane >= LANES - 1, next1, turn1)
        soon2 = jnp.where(lane >= LANES - 2, next2, turn2)
        next1, next2 = turn1, turn2
        grad_proj[:, lanes] = (taps[0] * now + taps[1] * soon1 + taps[2] * soon2).astype(BF16)
        held = widen(proj[block])
        sums = [total + held * moved for total, moved in zip(sums, (now, soon1, soon2))]
    for tap in range(3):
        tap_terms[tap] = jnp.sum(sums[tap], axis=1, keepdims=True)
    coded = lax.dot_general(
        grad_proj[...], hot[...], (((1,), (1,)), ((), ())), preferred_element_type=F32
    )
    weight_part[...] = dot(coded.astype(BF16), entries[...]).T.astype(BF16)


def lagged_kernel(grad_spec, value_spec, mix_spec, *rest):
    tables, filter_grads = rest[:6], rest[6]
    chans, steps = filter_grads.shape[1:]
    blocks = steps // LANES
    for which, other in enumerate((value_spec, mix_spec)):
        for batch in batches(chans):
            turned = [product(grad_spec[which, group], other[group], True) for group in batch]
            for group, signal in zip(batch, inverse(turned, tables)):
                for t in range(blocks):
                    filter_grads[which, channel_rows(group), t * LANES : (t + 1) * LANES] = signal[
                        t * GROUP : (t + 1) * GROUP
                    ]


def shape(dims, kind):
    return jax.ShapeDtypeStruct(dims, kind)


def exchange(blocks):
    return lax.all_to_all(blocks, "tm", split_axis=0, concat_axis=0, tiled=True)


def local(token_ids, field_offsets, embed_table, w_in, short_taps, filters, cotangent):
    tok_rows, width = cotangent.shape
    peers = lax.axis_size("tm")
    fields = token_ids.shape[1]
    codes = embed_table.shape[0] // fields
    rows = w_in.shape[0]
    chans = width // peers
    steps = tok_rows * peers
    groups = chans // GROUP
    tables = transform_tables(peers)

    w_send = w_in.reshape(rows, 3, peers, chans).transpose(2, 0, 1, 3)
    w_send = w_send.reshape(peers, rows * 3 * chans // LANES, LANES)
    ids_send = jnp.broadcast_to(token_ids.T.astype(BF16)[None], (peers, fields, tok_rows))
    arrived = exchange(jnp.concatenate([w_send, ids_send], axis=1))
    w_cols = arrived[:, : w_send.shape[1]].reshape(width, 3 * chans)
    ids = arrived[:, w_send.shape[1] :]
    upstream = exchange(cotangent.T.reshape(peers, chans, tok_rows))

    entries = jnp.concatenate(
        [
            lax.dynamic_slice_in_dim(embed_table, field_offsets[f], codes, axis=0)
            for f in range(fields)
        ],
        axis=0,
    )
    taps = short_taps.reshape(3, 3, peers, chans)
    taps = lax.dynamic_index_in_dim(taps, lax.axis_index("tm"), axis=2, keepdims=False)
    taps = jnp.broadcast_to(taps.reshape(3, 3 * chans, 1), (3, 3 * chans, LANES))

    spec = (groups, peers * GROUP, 2 * LANES)
    moved = (peers, chans, LANES)
    wide = (peers, 3 * chans, LANES)
    filter_spec = pl.pallas_call(
        filter_kernel, out_shape=shape((2,) + spec, F32), compiler_params=PARAMS
    )(filters, *tables)
    proj, mixed, first_conv, second_conv, value_spec, mix_spec, mixer_out = pl.pallas_call(
        forward_kernel,
        out_shape=(
            shape(wide, BF16),
            shape(wide, BF16),
            shape(moved, BF16),
            shape(moved, BF16),
            shape(spec, F32),
            shape(spec, F32),
            shape(moved, BF16),
        ),
        compiler_params=PARAMS,
    )(ids, entries, w_cols, taps, filter_spec, *tables)
    mixer_out = exchange(mixer_out).reshape(width, tok_rows).T
    weight_part, tap_terms, grad_spec = pl.pallas_call(
        backward_kernel,
        out_shape=(
            shape((width, 3 * chans), BF16),
            shape((3, 3 * chans, 1), F32),
            shape((2,) + spec, F32),
        ),
        scratch_shapes=[
            pltpu.VMEM(wide, BF16),
            pltpu.VMEM((3 * chans, steps), BF16),
            pltpu.VMEM((fields * codes, steps), BF16),
        ],
        compiler_params=PARAMS,
    )(ids, entries, taps, filter_spec, upstream, proj, mixed, first_conv, second_conv, *tables)
    filter_grads = pl.pallas_call(
        lagged_kernel, out_shape=shape((2, chans, steps), F32), compiler_params=PARAMS
    )(grad_spec, value_spec, mix_spec, *tables)

    tap_terms = tap_terms.reshape(1, 3 * 3 * chans)
    tap_high = tap_terms.astype(BF16)
    tap_low = (tap_terms - widen(tap_high)).astype(BF16)
    tap_send = jnp.concatenate([tap_high, tap_low], axis=1)
    space = -tap_send.shape[1] % LANES
    tap_send = jnp.pad(tap_send, ((0, 0), (0, space))).reshape(1, -1, LANES)
    tap_send = jnp.broadcast_to(tap_send, (peers,) + tap_send.shape[1:])
    weight_send = weight_part.reshape(peers, rows * 3 * chans // LANES, LANES)
    arrived = exchange(jnp.concatenate([weight_send, tap_send], axis=1))
    weight_grads = arrived[:, : weight_send.shape[1]].reshape(peers, rows, 3, chans)
    weight_grads = widen(weight_grads).transpose(1, 2, 0, 3).reshape(rows, 3 * width)
    taps_moved = arrived[:, weight_send.shape[1] :].reshape(peers, -1)
    count = 3 * 3 * chans
    tap_grads = widen(taps_moved[:, :count]) + widen(taps_moved[:, count : 2 * count])
    tap_grads = tap_grads.reshape(peers, 3, 3, chans).transpose(1, 2, 0, 3)
    return (mixer_out, weight_grads, tap_grads.reshape(3, 3 * width), filter_grads)


def solution(mesh):
    return jax.shard_map(
        local,
        mesh=mesh,
        in_specs=(
            P(("groups", "tm"), None),
            P("groups"),
            P(),
            P("tm", None),
            P(),
            P(None, "tm", None),
            P(("groups", "tm"), None),
        ),
        out_specs=(
            P(("groups", "tm"), None),
            P(("groups", "tm"), None),
            P("groups", None),
            P("groups", "tm", None),
        ),
        check_vma=False,
    )
```

time: 542 us -> 112 us (0.21); the launches traced: 535 us -> 111 us
  matrix products: 148 us -> 0 us
  waiting for transfers between devices: 127 us -> 7.14 us
  blocking collectives: 79.7 us -> 0 us
  other arithmetic: 51.6 us -> 4.71 us
  local copies, waits for them, and re-layouts: 74.7 us -> 37.7 us
  Pallas kernels: 0 us -> 19.7 us
  starting transfers between devices: 39 us -> 25.6 us
    dot_general x26 -> x0, matrix products: 148 us -> none  [the longest x6 42.6 us: signal_of(): blocks = jnp.einsum('ka,ckb->cab', first_both, turned, precision=HIGHEST)]
    psum x1 -> x0, blocking collectives: 63.6 us -> none  [local(): tap_grads = lax.psum(tap_terms, 'tm')]
    all_gather x1 -> x0, waiting for transfers between devices: 55.1 us -> none  [local(): lax.all_gather(w_in, 'tm', axis=0, tiled=True)]
    reduce_scatter x1 -> x0, waiting for transfers between devices: 48.2 us -> none  [local(): lax.psum_scatter(jnp.einsum('tr,tc->rc', block, grad_proj, preferred_elem...]
    sub x7 -> x0, other arithmetic: 20.7 us -> none  [the longest x4 11.8 us: product(): left_re * right_re - left_im * right_im]
    pallas_call x0 -> x4, Pallas kernels: none -> 19.7 us  [the longest x1 8.7 us: local(): pl.pallas_call(forward_kernel, out_shape=(shape(wide, BF16), shape(wide,...]
    all_to_all x1 -> x0, blocking collectives: 16.1 us -> none  [to_time(): lax.all_to_all(time_major(block), 'tm', split_axis=0, concat_axis=1, tile...]
    convert_element_type x13 -> x0, local copies, waits for them, and re-layouts: 15 us -> none  [the longest x6 5.55 us: widen(): return array.astype(jnp.float32)]
  transfers between devices with their start and end apart: 11 -> 4, of which waited for: 6 -> 1; matrix products, arithmetic and copies ran while one was open for 23% -> 17% of each run, Pallas kernels for 0% -> 18%
where the time goes in v1:
time: 112 us; the launch traced here: 111 us
  local copies, waits for them, and re-layouts  37.7 us (34%)
  starting transfers between devices  25.6 us (23%)
  Pallas kernels  19.7 us (18%)
  between operations  16.2 us (14%)
  waiting for transfers between devices  7.14 us (6%)
  other arithmetic  4.71 us (4%)
    all_to_all x4, starting transfers between devices, exchange(): return lax.all_to_all(blocks, 'tm', split_axis=0, concat_axis=0, tiled=True)  25.6 us
    unnamed x54, local copies, waits for them, and re-layouts  20.2 us
    pallas_call x1, Pallas kernels, local(): pl.pallas_call(forward_kernel, out_shape=(shape(wide, BF16), shape(wide,...  8.7 us
    pallas_call x1, Pallas kernels, local(): pl.pallas_call(backward_kernel, out_shape=(shape((width, 3 * chans), BF16...  8.15 us
    all_to_all x4, waiting for transfers between devices, exchange(): return lax.all_to_all(blocks, 'tm', split_axis=0, concat_axis=0, tiled=True)  7.14 us
    reshape x3, local copies, waits for them, and re-layouts, local(): widen(weight_grads).transpose(1, 2, 0, 3).reshape(rows, 3 * width)  5.68 us
    reshape x1, local copies, waits for them, and re-layouts, local(): weight_send = weight_part.reshape(peers, rows * 3 * chans // LANES, LANES)  2.56 us
  transfers between devices with their start and end apart: 4, of which 1 were waited for; matrix products, arithmetic and copies ran while one was open for 17% of the time, Pallas kernels for 18%

profile of v1, /device:TPU:0, one launch (start us, length us, event | category | flops | bytes accessed | tf_op | source)
XLA Modules:
  0.0 111.0 jit_solution(18360617786008220155)
XLA Ops:
  0.6 0.7 convert_bitcast_fusion
  1.3 1.5 %reshape.92 = bf16[64,3,16,64]{3,2,1,0:T(8,128)(2,1)S(1)} reshape(bf16[64,3072]{1,0:T(8,128)(2,1)} %param.16) | data formatting | bytes 786432 | tf_op jit(solution)/shard_map/reshape | solution.py:307
  2.9 0.5 copy.32
  3.4 0.6 reshape.93
  4.0 0.8 pad_maximum_fusion.1
  4.9 7.5 %all-to-all-start = ((bf16[16,104,128]{2,1,0:T(8,128)(2,1)}), bf16[16,104,128]{2,1,0:T(8,128)(2,1)S(1)}, u32[]{:S(2)}, u32[]{:S(2)}) async-start(bf16[16,104,128]{2,1,0:T(8,128)(2,1)} %pad_maximum_fusion.1), calls=%async_computation | async-start | bytes 851968 | tf_op jit(solution)/shard_map/all_to_all | solution.py:293
  12.4 0.7 fusion.1
  18.3 0.8 copy.26
  21.7 1.7 %dynamic-slice_dynamic-update-slice_fusion.7 = bf16[1024,1024]{1,0:T(8,128)(2,1)} fusion(bf16[1024,1024]{1,0:T(8,128)(2,1)} %param.15, s32[]{:T(128)S(6)} %select_n.28), kind=kLoop, calls=%fused_computation.11 | loop fusion | bytes 524292
  23.4 1.7 %dynamic-slice_dynamic-update-slice_fusion.6 = bf16[1024,1024]{1,0:T(8,128)(2,1)} fusion(bf16[1024,1024]{1,0:T(8,128)(2,1)} %dynamic-slice_dynamic-update-slice_fusion.7, bf16[1024,1024]{1,0:T(8,128)(2,1)} %param.15, s32[]{:T(128)S(6)} %select_n.29), kind=kLoop, calls=%fused_computation.10 | loop fusion | bytes 524292
  25.1 1.7 %dynamic-slice_dynamic-update-slice_fusion.5 = bf16[1024,1024]{1,0:T(8,128)(2,1)} fusion(bf16[1024,1024]{1,0:T(8,128)(2,1)} %dynamic-slice_dynamic-update-slice_fusion.6, bf16[1024,1024]{1,0:T(8,128)(2,1)} %param.15, s32[]{:T(128)S(6)} %select_n.30), kind=kLoop, calls=%fused_computation.9 | loop fusion | bytes 524292
  26.9 6.0 %all-to-all-start.2 = ((bf16[16,64,128]{2,1,0:T(8,128)(2,1)}), bf16[16,64,128]{2,1,0:T(8,128)(2,1)S(1)}, u32[]{:S(2)}, u32[]{:S(2)}) async-start(bf16[16,64,128]{2,1,0:T(8,128)(2,1)} %bitcast.13), calls=%async_computation.2 | async-start | bytes 524288 | tf_op jit(solution)/shard_map/all_to_all | solution.py:293
  32.9 1.8 %dynamic-slice_dynamic-update-slice_fusion.4 = bf16[1024,1024]{1,0:T(8,128)(2,1)} fusion(bf16[1024,1024]{1,0:T(8,128)(2,1)} %dynamic-slice_dynamic-update-slice_fusion.5, bf16[1024,1024]{1,0:T(8,128)(2,1)} %param.15, s32[]{:T(128)S(6)} %select_n.31), kind=kLoop, calls=%fused_computation.8 | loop fusion | bytes 524292
  39.7 0.1 reshape.95
  42.5 0.9 shard_map.156.filter_spec
  43.4 1.3 %copy-done = f32[2,4,256,256]{3,2,1,0:T(8,128)} copy-done((f32[2,4,256,256]{3,2,1,0:T(8,128)}, f32[2,4,256,256]{3,2,1,0:T(8,128)S(1)}, u32[]{:S(2)}) %copy-start) | copy-done | bytes 2097176
  44.7 0.8 dynamic-slice_dynamic-update-slice_fusion.3
  45.5 0.8 dynamic-slice_dynamic-update-slice_fusion.2
  46.3 0.8 dynamic-slice_dynamic-update-slice_fusion.1
  47.1 0.8 dynamic-slice_dynamic-update-slice_fusion.entries
  47.9 0.3 reshape.94.w_cols
  48.2 0.1 broadcast_in_dim.22.taps
  48.4 8.7 %shard_map.157 = (bf16[16,192,128]{2,1,0:T(8,128)(2,1)S(1)}, bf16[16,192,128]{2,1,0:T(8,128)(2,1)S(1)}, bf16[16,64,128]{2,1,0:T(8,128)(2,1)S(1)}, bf16[16,64,128...) custom-call(bf16[16,8,128]{2,1,0:T(8,128)(2,1)S(1)} %slice.56.ids, ...), custom_call_target="tpu_custom_call" | custom-call | tf_op jit(solution)/shard_map/pallas_call | solution.py:332
  57.1 1.0 copy-done.8
  58.0 0.9 copy-done.11
  58.9 0.7 copy-done.15
  59.6 0.7 copy-done.17
  60.3 6.1 %all-to-all-start.1 = ((bf16[16,64,128]{2,1,0:T(8,128)(2,1)}), bf16[16,64,128]{2,1,0:T(8,128)(2,1)}, u32[]{:S(2)}, u32[]{:S(2)}) async-start(bf16[16,64,128]{2,1,0:T(8,128)(2,1)} %get-tuple-element.14), calls=%async_computation.1 | async-start | bytes 524288 | tf_op jit(solution)/shard_map/all_to_all | solution.py:293
  66.4 1.1 %copy-done.12 = bf16[16,192,128]{2,1,0:T(8,128)(2,1)S(1)} copy-done((bf16[16,192,128]{2,1,0:T(8,128)(2,1)S(1)}, bf16[16,192,128]{2,1,0:T(8,128)(2,1)}, u32[]{:S(2)}) %copy-start.12) | copy-done | bytes 786456
  67.5 0.9 copy-done.16
  68.5 0.9 copy-done.18
  69.4 8.2 %shard_map.158 = (bf16[1024,192]{1,0:T(8,128)(2,1)S(1)}, f32[3,192,1]{2,1,0:T(8,128)S(1)}, f32[2,4,256,256]{3,2,1,0:T(8,128)}) custom-call(bf16[16,8,128]{2,1,0:T(8,128)(2,1)S(1)} %slice.56.ids, bf16[1024,1024]{1,0:T(8,128)(2,1)} %dynamic-slice_dynamic-update-slice_fusion.entries, f32[3,192,128]{2,1,0:T(8,128)S(1)} %broadcast_in_dim.22.taps, ...), custom_call_target="tpu_custom_call" | custom-call | tf_op jit(solution)/shard_map/pallas_call | solution.py:346
  77.6 0.8 copy-done.14
  78.4 2.6 %reshape.98 = bf16[16,96,128]{2,1,0:T(8,128)(2,1)} reshape(bf16[1024,192]{1,0:T(8,128)(2,1)} %copy-done.14) | data formatting | bytes 786432 | tf_op jit(solution)/shard_map/reshape | solution.py:371
  81.0 0.2 reduce.1
  81.3 1.8 %pad_maximum_fusion = bf16[16,105,128]{2,1,0:T(8,128)(2,1)} fusion(bf16[16,9,128]{2,1,0:T(8,128)(2,1)S(1)} %broadcast_in_dim.24, bf16[16,96,128]{2,1,0:T(8,128)(2,1)} %reshape.98), kind=kLoop, calls=%fused_computation.1 | loop fusion | flops 860160 | bytes 860160 | tf_op jit(solution)/shard_map/concatenate | solution.py:372
  83.2 6.0 %all-to-all-start.3 = ((bf16[16,105,128]{2,1,0:T(8,128)(2,1)}), bf16[16,105,128]{2,1,0:T(8,128)(2,1)}, u32[]{:S(2)}, u32[]{:S(2)}) async-start(bf16[16,105,128]{2,1,0:T(8,128)(2,1)} %pad_maximum_fusion), calls=%async_computation.3 | async-start | bytes 917504 | tf_op jit(solution)/shard_map/all_to_all | solution.py:293
  89.2 1.2 %copy-done.9 = f32[4,256,256]{2,1,0:T(8,128)S(1)} copy-done((f32[4,256,256]{2,1,0:T(8,128)S(1)}, f32[4,256,256]{2,1,0:T(8,128)}, u32[]{:S(2)}) %copy-start.9) | copy-done | bytes 1048600
  90.4 1.2 %copy-done.10 = f32[4,256,256]{2,1,0:T(8,128)S(1)} copy-done((f32[4,256,256]{2,1,0:T(8,128)S(1)}, f32[4,256,256]{2,1,0:T(8,128)}, u32[]{:S(2)}) %copy-start.10) | copy-done | bytes 1048600
  91.6 1.9 %shard_map.159 = f32[2,64,2048]{2,1,0:T(8,128)} custom-call(f32[2,4,256,256]{3,2,1,0:T(8,128)S(1)} %copy-done.7, f32[4,256,256]{2,1,0:T(8,128)S(1)} %copy-done.9, f32[4,256,256]{2,1,0:T(8,128)S(1)} %copy-done.10, bf16[512,256]{1,0:T(8,128)(2,1)S(1)} %copy-done.2, bf16[256,512]{1,0:T(8,128)(2,1)S(1)} %copy-done.1, bf16[256,256]{1,0:T(8,128)(2,1)S(1)} %copy-done.6, ...), custom_call_target="tpu_custom_call" | custom-call | tf_op jit(solution)/shard_map/pallas_call | solution.py:360
  93.5 1.8 %copy.25 = bf16[1024,128]{0,1:T(8,128)(2,1)} copy(bf16[1024,128]{1,0:T(8,128)(2,1)} %bitcast.10) | data formatting | bytes 524288 | tf_op jit(solution)/shard_map/reshape | solution.py:345
  95.3 7.1 %all-to-all-done.3 = bf16[16,105,128]{2,1,0:T(8,128)(2,1)} async-done(((bf16[16,105,128]{2,1,0:T(8,128)(2,1)}), bf16[16,105,128]{2,1,0:T(8,128)(2,1)}, u32[]{:S(2)}, u32[]{:S(2)}) %all-to-all-start.3) | async-done | bytes 430112 | tf_op jit(solution)/shard_map/all_to_all | solution.py:293
  102.5 0.8 slice.59
  103.5 0.7 reshape.104
  104.2 1.1 slice_convert_fusion
  105.3 0.9 reshape.109
  106.2 2.1 %copy.27 = f32[64,3,16,64]{3,2,1,0:T(8,128)} copy(f32[64,3,16,64]{3,1,0,2:T(4,128)S(1)} %bitcast.28) | data formatting | bytes 1572864 | tf_op jit(solution)/shard_map/reshape | solution.py:374
  108.3 2.7 %reshape.106 = f32[64,3072]{1,0:T(8,128)} reshape(f32[64,3,16,64]{3,2,1,0:T(8,128)} %copy.27) | data formatting | bytes 1572864 | tf_op jit(solution)/shard_map/reshape | solution.py:374
  (51 shorter events, 0.7 us)
Async XLA Ops:
  2.9 9.6 %copy-start.22 = (s32[8]{0:T(128)S(1)}, s32[8]{0:T(128)}, u32[]{:S(2)}) copy-start(s32[8]{0:T(128)} %param.14) | copy-start | bytes 100
  2.9 15.4 %copy-start.20 = (bf16[128,1024]{1,0:T(8,128)(2,1)S(1)}, bf16[128,1024]{1,0:T(8,128)(2,1)}, u32[]{:S(2)}) copy-start(bf16[128,1024]{1,0:T(8,128)(2,1)} %param.19) | copy-start | bytes 786436
  4.8 34.9 %copy-start.21 = (f32[3,3072]{1,0:T(4,128)S(1)}, f32[3,3072]{1,0:T(4,128)}, u32[]{:S(2)}) copy-start(f32[3,3072]{1,0:T(4,128)} %param.17) | copy-start | bytes 110596
  4.8 37.6 %copy-start.1 = (bf16[256,512]{1,0:T(8,128)(2,1)S(1)}, bf16[256,512]{1,0:T(8,128)(2,1)}, u32[]{:S(2)}) copy-start(bf16[256,512]{1,0:T(8,128)(2,1)} %constant.26.clone.rest_1_) | copy-start | bytes 786436
  4.8 37.6 %copy-start.2 = (bf16[512,256]{1,0:T(8,128)(2,1)S(1)}, bf16[512,256]{1,0:T(8,128)(2,1)}, u32[]{:S(2)}) copy-start(bf16[512,256]{1,0:T(8,128)(2,1)} %constant.25.clone.rest_0_) | copy-start | bytes 786436
  4.8 37.6 %copy-start.3 = (f32[256,128]{1,0:T(8,128)S(1)}, f32[256,128]{1,0:T(8,128)}, u32[]{:S(2)}) copy-start(f32[256,128]{1,0:T(8,128)} %constant.30.clone.rest_5_) | copy-start | bytes 393220
  4.8 37.6 %copy-start.4 = (f32[256,128]{1,0:T(8,128)S(1)}, f32[256,128]{1,0:T(8,128)}, u32[]{:S(2)}) copy-start(f32[256,128]{1,0:T(8,128)} %constant.29.clone.rest_4_) | copy-start | bytes 393220
  4.8 37.6 %copy-start.5 = (bf16[256,256]{1,0:T(8,128)(2,1)S(1)}, bf16[256,256]{1,0:T(8,128)(2,1)}, u32[]{:S(2)}) copy-start(bf16[256,256]{1,0:T(8,128)(2,1)} %constant.28.clone.rest_3_) | copy-start | bytes 393220
  4.9 37.6 %copy-start.6 = (bf16[256,256]{1,0:T(8,128)(2,1)S(1)}, bf16[256,256]{1,0:T(8,128)(2,1)}, u32[]{:S(2)}) copy-start(bf16[256,256]{1,0:T(8,128)(2,1)} %constant.27.clone.rest_2_) | copy-start | bytes 393220
  4.9 37.6 %copy-start.13 = (bf16[2,64,2048]{2,1,0:T(8,128)(2,1)S(1)}, bf16[2,64,2048]{2,1,0:T(8,128)(2,1)}, u32[]{:S(2)}) copy-start(bf16[2,64,2048]{2,1,0:T(8,128)(2,1)} %filters.1) | copy-start | bytes 1572868
  4.9 22.0 %all-to-all-start = ((bf16[16,104,128]{2,1,0:T(8,128)(2,1)}), bf16[16,104,128]{2,1,0:T(8,128)(2,1)S(1)}, u32[]{:S(2)}, u32[]{:S(2)}) async-start(bf16[16,104,128]{2,1,0:T(8,128)(2,1)} %pad_maximum_fusion.1), calls=%async_computation | async-start | bytes 851968 | tf_op jit(solution)/shard_map/all_to_all | solution.py:293
  26.9 33.5 %all-to-all-start.2 = ((bf16[16,64,128]{2,1,0:T(8,128)(2,1)}), bf16[16,64,128]{2,1,0:T(8,128)(2,1)S(1)}, u32[]{:S(2)}, u32[]{:S(2)}) async-start(bf16[16,64,128]{2,1,0:T(8,128)(2,1)} %bitcast.13), calls=%async_computation.2 | async-start | bytes 524288 | tf_op jit(solution)/shard_map/all_to_all | solution.py:293
  42.5 2.2 %copy-start.19 = (bf16[1024,1024]{1,0:T(8,128)(2,1)S(1)}, bf16[1024,1024]{1,0:T(8,128)(2,1)}, u32[]{:S(2)}) copy-start(bf16[1024,1024]{1,0:T(8,128)(2,1)} %param.15) | copy-start | bytes 6291460
  43.4 1.3 %copy-start = (f32[2,4,256,256]{3,2,1,0:T(8,128)}, f32[2,4,256,256]{3,2,1,0:T(8,128)S(1)}, u32[]{:S(2)}) copy-start(f32[2,4,256,256]{3,2,1,0:T(8,128)S(1)} %shard_map.156.filter_spec) | copy-start | bytes 6291460
  57.1 1.0 copy-start.8
  58.0 0.9 copy-start.11
  58.9 0.7 copy-start.15
  59.6 0.7 copy-start.17
  60.3 22.8 %all-to-all-start.1 = ((bf16[16,64,128]{2,1,0:T(8,128)(2,1)}), bf16[16,64,128]{2,1,0:T(8,128)(2,1)}, u32[]{:S(2)}, u32[]{:S(2)}) async-start(bf16[16,64,128]{2,1,0:T(8,128)(2,1)} %get-tuple-element.14), calls=%async_computation.1 | async-start | bytes 524288 | tf_op jit(solution)/shard_map/all_to_all | solution.py:293
  66.4 1.1 %copy-start.12 = (bf16[16,192,128]{2,1,0:T(8,128)(2,1)S(1)}, bf16[16,192,128]{2,1,0:T(8,128)(2,1)}, u32[]{:S(2)}) copy-start(bf16[16,192,128]{2,1,0:T(8,128)(2,1)} %copy-done.11) | copy-start | bytes 2359300
  67.5 0.9 copy-start.16
  68.5 0.9 copy-start.18
  77.6 0.8 copy-start.14
  78.4 10.8 %copy-start.7 = (f32[2,4,256,256]{3,2,1,0:T(8,128)S(1)}, f32[2,4,256,256]{3,2,1,0:T(8,128)}, u32[]{:S(2)}) copy-start(f32[2,4,256,256]{3,2,1,0:T(8,128)} %get-tuple-element.21.grad_spec) | copy-start | bytes 6291460
  83.2 19.3 %all-to-all-start.3 = ((bf16[16,105,128]{2,1,0:T(8,128)(2,1)}), bf16[16,105,128]{2,1,0:T(8,128)(2,1)}, u32[]{:S(2)}, u32[]{:S(2)}) async-start(bf16[16,105,128]{2,1,0:T(8,128)(2,1)} %pad_maximum_fusion), calls=%async_computation.3 | async-start | bytes 917504 | tf_op jit(solution)/shard_map/all_to_all | solution.py:293
  89.2 1.2 %copy-start.9 = (f32[4,256,256]{2,1,0:T(8,128)S(1)}, f32[4,256,256]{2,1,0:T(8,128)}, u32[]{:S(2)}) copy-start(f32[4,256,256]{2,1,0:T(8,128)} %copy-done.8) | copy-start | bytes 3145732
  90.4 1.2 %copy-start.10 = (f32[4,256,256]{2,1,0:T(8,128)S(1)}, f32[4,256,256]{2,1,0:T(8,128)}, u32[]{:S(2)}) copy-start(f32[4,256,256]{2,1,0:T(8,128)} %get-tuple-element.23.mix_spec) | copy-start | bytes 3145732

commit v2 on v1

v2 whole, which is shorter than its diff:
```python
import functools


import jax
import jax.numpy as jnp
import ml_dtypes
import numpy as np
from jax import lax
from jax.experimental import pallas as pl
from jax.experimental.pallas import tpu as pltpu
from jax.sharding import PartitionSpec as P

F32 = jnp.float32
BF16 = jnp.bfloat16
LANES = 128
GROUP = 16


def widen(array):
    return array.astype(F32)


def rounded(array):
    return array.astype(BF16).astype(F32)


def transform_tables(blocks):
    total = 2 * blocks * LANES
    row = np.arange(blocks) + 0.5
    first = np.exp(-2j * np.pi * np.outer(row, np.arange(blocks)) / (2 * blocks))
    turn = np.exp(-2j * np.pi * np.outer(row, np.arange(LANES)) / total)
    second = np.exp(-2j * np.pi * np.outer(np.arange(LANES), np.arange(LANES)) / LANES)
    same = np.eye(GROUP)
    first_rows = np.concatenate([first.real, first.imag], axis=0)
    back_rows = np.concatenate([first.real.T, first.imag.T], axis=1) * (2.0 / total)
    forward = np.block([[second.real, second.imag], [-second.imag, second.real]])
    inverse = np.block([[second.real, -second.imag], [second.imag, second.real]])
    narrow = ml_dtypes.bfloat16
    return (
        np.kron(first_rows, same).astype(narrow),
        np.kron(back_rows, same).astype(narrow),
        forward.astype(narrow),
        inverse.astype(narrow),
        np.repeat(turn.real, GROUP, axis=0).astype(np.float32),
        np.repeat(turn.imag, GROUP, axis=0).astype(np.float32),
    )


def dot(left, right):
    return jnp.dot(left, right, preferred_element_type=F32)


def joined(parts, axis):
    return parts[0] if len(parts) == 1 else jnp.concatenate(parts, axis=axis)


def forward(series, tables):
    first, _, second, _, turn_re, turn_im = tables
    rows = turn_re.shape[0]
    part = dot(first[...], joined(series, 1))
    spectra = []
    for place in range(len(series)):
        lanes = slice(place * LANES, (place + 1) * LANES)
        part_re = part[:rows, lanes]
        part_im = part[rows:, lanes]
        turned = jnp.concatenate(
            [
                part_re * turn_re[...] - part_im * turn_im[...],
                part_re * turn_im[...] + part_im * turn_re[...],
            ],
            axis=1,
        )
        spectra.append(dot(turned.astype(BF16), second[...]))
    return spectra


def inverse(spectra, tables):
    _, last, _, second, turn_re, turn_im = tables
    turned = []
    for spectrum in spectra:
        back = dot(spectrum.astype(BF16), second[...])
        back_re = back[:, :LANES]
        back_im = back[:, LANES:]
        turned.append(
            jnp.concatenate(
                [
                    back_re * turn_re[...] + back_im * turn_im[...],
                    back_im * turn_re[...] - back_re * turn_im[...],
                ],
                axis=0,
            ).astype(BF16)
        )
    signal = dot(last[...], joined(turned, 1))
    return [signal[:, place * LANES : (place + 1) * LANES] for place in range(len(spectra))]


def product(left, right, conjugate):
    left_re, left_im = left[:, :LANES], left[:, LANES:]
    right_re, right_im = right[:, :LANES], right[:, LANES:]
    if conjugate:
        return jnp.concatenate(
            [
                left_re * right_re + left_im * right_im,
                left_im * right_re - left_re * right_im,
            ],
            axis=1,
        )
    return jnp.concatenate(
        [
            left_re * right_re - left_im * right_im,
            left_re * right_im + left_im * right_re,
        ],
        axis=1,
    )


def batches(chans):
    groups = chans // GROUP
    size = 2 if groups % 2 == 0 else 1
    return [range(start, start + size) for start in range(0, groups, size)]


def channel_rows(group, offset=0):
    return slice(offset + group * GROUP, offset + (group + 1) * GROUP)


def flat(block):
    return block.reshape(block.shape[0] * block.shape[1], block.shape[2])


def one_hot(ids, codes):
    fields, lanes = ids.shape
    code = lax.broadcasted_iota(jnp.int32, (codes, lanes), 0).astype(F32)
    return jnp.concatenate(
        [
            jnp.where(code == ids[field : field + 1], 1.0, 0.0).astype(BF16)
            for field in range(fields)
        ],
        axis=0,
    )


def prepare_kernel(offsets, filters, table, *rest):
    tables = rest[:6]
    spectra, entries = rest[6:]
    chans, steps = filters.shape[1:]
    blocks = steps // LANES
    fields = offsets.shape[0]
    codes = entries.shape[0] // fields
    window = codes + GROUP
    for field in range(fields):
        start = jnp.minimum(offsets[field] // GROUP * GROUP, table.shape[0] - window)
        row = lax.broadcasted_iota(jnp.int32, (codes, window), 0) + (offsets[field] - start)
        place = lax.broadcasted_iota(jnp.int32, (codes, window), 1)
        picked = jnp.where(row == place, 1.0, 0.0).astype(BF16)
        entries[field * codes : (field + 1) * codes, :] = dot(
            picked, table[pl.ds(pl.multiple_of(start, GROUP), window), :]
        ).astype(BF16)
    for which in range(2):
        for batch in batches(chans):
            series = [
                jnp.concatenate(
                    [
                        filters[which, channel_rows(group), t * LANES : (t + 1) * LANES]
                        for t in range(blocks)
                    ],
                    axis=0,
                )
                for group in batch
            ]
            for group, spectrum in zip(batch, forward(series, tables)):
                spectra[which, group] = spectrum


def halves(array):
    lane = lax.broadcasted_iota(jnp.int32, array.shape, 1)
    return pltpu.roll(array, LANES // 2, 1), lane < LANES // 2


def packed_parts(rows):
    half = rows // 2
    marks = [0, rows, rows + half, 2 * rows + half, 2 * rows + half + 16]
    return [slice(low, high) for low, high in zip(marks[:-1], marks[1:])]


def pack_kernel(token_ids, w_in, cotangent, packed):
    peers = packed.shape[0]
    rows, wide = w_in.shape
    half = rows // 2
    part_two, part_one, part_time, part_ids = packed_parts(rows)
    fields = token_ids.shape[1]
    ids = jnp.concatenate(
        [widen(token_ids[...]), jnp.zeros((token_ids.shape[0], LANES - fields), F32)], axis=1
    )
    ids = ids.T[:16].astype(BF16)
    for pair in range(peers // 2):
        tiles = []
        for column in range(3):
            start = column * (wide // 3) + pair * LANES
            tile = widen(w_in[:, start : start + LANES])
            turned, first = halves(tile)
            tiles.append((tile, turned))
        first_half = first[:half]
        (zero, zero_turned), (one, one_turned), (two, two_turned) = tiles
        even, odd = 2 * pair, 2 * pair + 1
        packed[even, part_two, :] = jnp.where(first, zero, one_turned).astype(BF16)
        packed[odd, part_two, :] = jnp.where(first, zero_turned, one).astype(BF16)
        packed[even, part_one, :] = jnp.where(first_half, two[:half], two_turned[half:]).astype(
            BF16
        )
        packed[odd, part_one, :] = jnp.where(first_half, two_turned[:half], two[half:]).astype(
            BF16
        )
        turned = widen(cotangent[:, pair * LANES : (pair + 1) * LANES]).T.astype(BF16)
        packed[even, part_time, :] = turned[:rows]
        packed[odd, part_time, :] = turned[rows:]
        packed[even, part_ids, :] = ids
        packed[odd, part_ids, :] = ids


def unpack_kernel(packed, mixer_out, weight_grads, tap_grads):
    peers = packed.shape[0]
    rows, wide = weight_grads.shape
    half = rows // 2
    part_two, part_one, part_time, part_taps = packed_parts(rows)
    for pair in range(peers // 2):
        even, odd = 2 * pair, 2 * pair + 1
        starts = [column * (wide // 3) + pair * LANES for column in range(3)]
        lanes = [slice(start, start + LANES) for start in starts]

        def merged(low, high):
            low_turned, first = halves(low)
            high_turned, _ = halves(high)
            return jnp.where(first, low, high_turned), jnp.where(first, low_turned, high)

        zero, one = merged(widen(packed[even, part_two, :]), widen(packed[odd, part_two, :]))
        weight_grads[:, lanes[0]] = zero
        weight_grads[:, lanes[1]] = one
        upper, lower = merged(widen(packed[even, part_one, :]), widen(packed[odd, part_one, :]))
        weight_grads[:half, lanes[2]] = upper
        weight_grads[half:, lanes[2]] = lower
        both = widen(jnp.concatenate([packed[even, part_time, :], packed[odd, part_time, :]], 0))
        mixer_out[:, pair * LANES : (pair + 1) * LANES] = both.T.astype(BF16)
        low = widen(packed[even, part_taps, :])
        high = widen(packed[odd, part_taps, :])
        low = low[:8] + low[8:]
        high = high[:8] + high[8:]
        zero, one = merged(low, high)
        tap_grads[:, lanes[0]] = zero[:3]
        tap_grads[:, lanes[1]] = one[:3]
        tap_grads[:, lanes[2]] = zero[3:6]


def mixer_kernel(packed_form, *refs):
    if packed_form:
        arrived, refs = refs[0], refs[1:]
        chans = refs[0].shape[0] // arrived.shape[0]
        part_two, part_one, part_time, part_small = packed_parts(chans)
        width = refs[0].shape[1]
        fields = refs[0].shape[0] // LANES
        two = widen(flat(arrived[:, part_two, :]))
        one = widen(arrived[:, part_one, :])
        one_turned = pltpu.roll(flat(one), LANES // 2, 1).reshape(one.shape)
        one = flat(jnp.concatenate([one, one_turned], axis=1))
        w_cols = jnp.concatenate([two, one], axis=1).astype(BF16)
        cotangent = arrived.at[:, part_time, :]

        def ids_of(block):
            return widen(arrived[block, part_small, :])[:fields]

    else:
        w_cols, ids, cotangent = refs[0][...], refs[1], refs[2]
        refs = refs[3:]
        chans = cotangent.shape[1]

        def ids_of(block):
            return widen(ids[block])

    entries, taps, filter_spec = refs[:3]
    tables, refs = refs[3:9], refs[9:]
    if packed_form:
        sent, lagged_spec = refs[:2]
        refs = refs[2:]
        mixer_out = sent.at[:, part_time, :]
    else:
        mixer_out, weight_part, tap_terms, lagged_spec = refs[:4]
        refs = refs[4:]
    hot, proj, mixed, grad_mixed, grad_proj = refs
    blocks = mixed.shape[0]
    codes = LANES

    coded = dot(entries[...], w_cols).T[: 3 * chans].astype(BF16)
    lane = lax.broadcasted_iota(jnp.int32, (3 * chans, LANES), 1)
    last1 = jnp.zeros((3 * chans, LANES), F32)
    last2 = last1
    for pair in range(blocks // 2):
        lanes = slice(2 * pair * LANES, (2 * pair + 2) * LANES)
        hot[:, lanes] = jnp.concatenate(
            [one_hot(ids_of(2 * pair + side), codes) for side in range(2)], axis=1
        )
        both = dot(coded, hot[:, lanes]).astype(BF16)
        for side in range(2):
            block = 2 * pair + side
            now = both[:, side * LANES : (side + 1) * LANES]
            proj[block] = now
            now = widen(now)
            turn1 = pltpu.roll(now, 1, 1)
            turn2 = pltpu.roll(now, 2, 1)
            late1 = jnp.where(lane < 1, last1, turn1)
            late2 = jnp.where(lane < 2, last2, turn2)
            last1, last2 = turn1, turn2
            mixed[block] = (taps[0] * now + taps[1] * late1 + taps[2] * late2).astype(BF16)

    def column(ref, group, place=0):
        return flat(ref[:, channel_rows(group, place * chans), :])

    def blocked(value):
        return value.reshape(blocks, GROUP, LANES)

    for batch in batches(chans):
        value_spec = forward([column(mixed, group) for group in batch], tables)
        turned = [
            product(spectrum, filter_spec[0, group], False)
            for group, spectrum in zip(batch, value_spec)
        ]
        first_conv = [rounded(signal) for signal in inverse(turned, tables)]
        series = [
            (widen(column(mixed, group, 1)) * conv).astype(BF16)
            for group, conv in zip(batch, first_conv)
        ]
        mix_spec = forward(series, tables)
        turned = [
            product(spectrum, filter_spec[1, group], False)
            for group, spectrum in zip(batch, mix_spec)
        ]
        series = []
        for group, signal in zip(batch, inverse(turned, tables)):
            second_conv = rounded(signal)
            gate = widen(column(mixed, group, 2))
            upstream = widen(column(cotangent, group))
            mixer_out[:, channel_rows(group), :] = blocked((gate * second_conv).astype(BF16))
            grad_mixed[:, channel_rows(group, 2 * chans), :] = blocked(
                (upstream * second_conv).astype(BF16)
            )
            series.append((upstream * gate).astype(BF16))
        grad_spec = forward(series, tables)
        turned = []
        for place, group in enumerate(batch):
            lagged_spec[1, group] = product(grad_spec[place], mix_spec[place], True).astype(BF16)
            turned.append(product(grad_spec[place], filter_spec[1, group], True))
        series = []
        for place, signal in enumerate(inverse(turned, tables)):
            grad_mix = rounded(signal)
            group = batch[place]
            grad_mixed[:, channel_rows(group, chans), :] = blocked(
                (grad_mix * first_conv[place]).astype(BF16)
            )
            series.append((grad_mix * widen(column(mixed, group, 1))).astype(BF16))
        grad_spec = forward(series, tables)
        turned = []
        for place, group in enumerate(batch):
            lagged_spec[0, group] = product(grad_spec[place], value_spec[place], True).astype(BF16)
            turned.append(product(grad_spec[place], filter_spec[0, group], True))
        for group, signal in zip(batch, inverse(turned, tables)):
            grad_mixed[:, channel_rows(group), :] = blocked(signal.astype(BF16))

    next1 = jnp.zeros((3 * chans, LANES), F32)
    next2 = next1
    sums = [next1] * 3
    for block in reversed(range(blocks)):
        now = widen(grad_mixed[block])
        turn1 = pltpu.roll(now, LANES - 1, 1)
        turn2 = pltpu.roll(now, LANES - 2, 1)
        soon1 = jnp.where(lane >= LANES - 1, next1, turn1)
        soon2 = jnp.where(lane >= LANES - 2, next2, turn2)
        next1, next2 = turn1, turn2
        grad_proj[:, block * LANES : (block + 1) * LANES] = (
            taps[0] * now + taps[1] * soon1 + taps[2] * soon2
        ).astype(BF16)
        held = widen(proj[block])
        sums = [total + held * moved for total, moved in zip(sums, (now, soon1, soon2))]
    coded = lax.dot_general(
        grad_proj[...], hot[...], (((1,), (1,)), ((), ())), preferred_element_type=F32
    )
    weights = dot(coded.astype(BF16), entries[...])
    if not packed_form:
        weight_part[...] = weights.T.astype(BF16)
        for tap in range(3):
            tap_terms[tap] = jnp.sum(sums[tap], axis=1, keepdims=True)
        return
    for tap in range(3):
        sums[tap] = jnp.sum(sums[tap].T, axis=0, keepdims=True)
    space = jnp.zeros((1, LANES), F32)
    total = jnp.concatenate(
        [sums[tap][:, :LANES] for tap in range(3)]
        + [
            jnp.concatenate([sums[tap][:, LANES:], space[:, : LANES - chans]], axis=1)
            for tap in range(3)
        ]
        + [space] * 2,
        axis=0,
    )
    high = rounded(total)
    small = jnp.concatenate([high, total - high], axis=0).astype(BF16)
    two = weights[: 2 * chans].T
    one = jnp.concatenate([weights[2 * chans :], jnp.zeros((LANES - chans, width), F32)], axis=0).T
    one = one.reshape(blocks, chans, LANES)
    half = chans // 2
    turned = pltpu.roll(flat(one[:, half:]), LANES // 2, 1)
    one = flat(one[:, :half])
    one = jnp.where(lax.broadcasted_iota(jnp.int32, one.shape, 1) < LANES // 2, one, turned)
    sent[:, part_two, :] = two.astype(BF16).reshape(blocks, chans, LANES)
    sent[:, part_one, :] = one.astype(BF16).reshape(blocks, half, LANES)
    for block in range(blocks):
        sent[block, part_small, :] = small


def lagged_kernel(lagged_spec, *rest):
    tables, filter_grads = rest[:6], rest[6]
    chans, steps = filter_grads.shape[1:]
    blocks = steps // LANES
    for which in range(2):
        for batch in batches(chans):
            turned = [lagged_spec[which, group] for group in batch]
            for group, signal in zip(batch, inverse(turned, tables)):
                for t in range(blocks):
                    filter_grads[which, channel_rows(group), t * LANES : (t + 1) * LANES] = signal[
                        t * GROUP : (t + 1) * GROUP
                    ]


def shape(dims, kind):
    return jax.ShapeDtypeStruct(dims, kind)


def exchange(blocks):
    return lax.all_to_all(blocks, "tm", split_axis=0, concat_axis=0, tiled=True)


def call(kernel, name, megabytes, **settings):
    return pl.pallas_call(
        kernel,
        name=name,
        compiler_params=pltpu.CompilerParams(vmem_limit_bytes=megabytes * 1024 * 1024),
        **settings,
    )


def send_inputs(token_ids, w_in, cotangent, peers):
    tok_rows, width = cotangent.shape
    rows, fields, chans = w_in.shape[0], token_ids.shape[1], width // peers
    w_send = w_in.reshape(rows, 3, peers, chans).transpose(2, 0, 1, 3)
    w_send = w_send.reshape(peers, rows * 3 * chans // LANES, LANES)
    ids_send = jnp.broadcast_to(token_ids.T.astype(BF16)[None], (peers, fields, tok_rows))
    cot_send = cotangent.T.reshape(peers, chans, tok_rows)
    arrived = exchange(jnp.concatenate([w_send, ids_send, cot_send], axis=1))
    count = w_send.shape[1]
    w_cols = arrived[:, :count].reshape(width, 3 * chans)
    return w_cols, arrived[:, count : count + fields], arrived[:, count + fields :]


def send_results(mixer_out, weight_part, tap_terms, peers, rows):
    _, chans, tok_rows = mixer_out.shape
    width = peers * chans
    count = 9 * chans
    tap_terms = tap_terms.reshape(1, count)
    tap_high = tap_terms.astype(BF16)
    tap_low = (tap_terms - widen(tap_high)).astype(BF16)
    tap_send = jnp.concatenate([tap_high, tap_low], axis=1)
    tap_send = jnp.pad(tap_send, ((0, 0), (0, -2 * count % LANES))).reshape(1, -1, LANES)
    tap_send = jnp.broadcast_to(tap_send, (peers,) + tap_send.shape[1:])
    weight_send = weight_part.reshape(peers, rows * 3 * chans // LANES, LANES)
    arrived = exchange(jnp.concatenate([mixer_out, weight_send, tap_send], axis=1))
    mixer_out = arrived[:, :chans].reshape(width, tok_rows).T
    place = chans + weight_send.shape[1]
    weight_grads = arrived[:, chans:place].reshape(peers, rows, 3, chans)
    weight_grads = widen(weight_grads).transpose(1, 2, 0, 3).reshape(rows, 3 * width)
    taps_moved = arrived[:, place:].reshape(peers, -1)
    tap_grads = widen(taps_moved[:, :count]) + widen(taps_moved[:, count : 2 * count])
    tap_grads = tap_grads.reshape(peers, 3, 3, chans).transpose(1, 2, 0, 3)
    return mixer_out, weight_grads, tap_grads.reshape(3, 3 * width)


def local(token_ids, field_offsets, embed_table, w_in, short_taps, filters, cotangent):
    tok_rows, width = cotangent.shape
    peers = lax.axis_size("tm")
    fields = token_ids.shape[1]
    rows = w_in.shape[0]
    chans = width // peers
    steps = tok_rows * peers
    groups = chans // GROUP
    tables = transform_tables(peers)
    packed_form = 2 * chans == LANES and rows == chans and fields <= 8
    spec = (2, groups, peers * GROUP, 2 * LANES)
    moved = (peers, chans, LANES)
    wide = (peers, 3 * chans, LANES)
    packed = shape((peers, packed_parts(rows)[-1].stop, LANES), BF16)

    if packed_form:
        sent = call(pack_kernel, "pack", 16, out_shape=packed)(token_ids, w_in, cotangent)
        arrived = (exchange(sent),)
    else:
        arrived = send_inputs(token_ids, w_in, cotangent, peers)

    whole = pl.BlockSpec(memory_space=pltpu.VMEM)
    filter_spec, entries = call(
        prepare_kernel,
        "prepare",
        32,
        in_specs=[pl.BlockSpec(memory_space=pltpu.SMEM)] + [whole] * 8,
        out_shape=(shape(spec, F32), shape(embed_table.shape, BF16)),
        cost_estimate=pl.CostEstimate(
            flops=10**10, bytes_accessed=3 * 10**7, transcendentals=0
        ),
    )(field_offsets, filters, embed_table, *tables)
    taps = short_taps.reshape(3, 3, peers, chans)
    taps = lax.dynamic_index_in_dim(taps, lax.axis_index("tm"), axis=2, keepdims=False)
    taps = jnp.broadcast_to(taps.reshape(3, 3 * chans, 1), (3, 3 * chans, LANES))

    if packed_form:
        out_shape = (packed, shape(spec, BF16))
    else:
        out_shape = (
            shape(moved, BF16),
            shape((width, 3 * chans), BF16),
            shape((3, 3 * chans, 1), F32),
            shape(spec, BF16),
        )
    hot_bytes = 2 * embed_table.shape[0] * steps
    results = call(
        functools.partial(mixer_kernel, packed_form),
        "mixer",
        20 + 2 * hot_bytes // 2**20,
        out_shape=out_shape,
        scratch_shapes=[
            pltpu.VMEM((embed_table.shape[0], steps), BF16),
            pltpu.VMEM(wide, BF16),
            pltpu.VMEM(wide, BF16),
            pltpu.VMEM(wide, BF16),
            pltpu.VMEM((3 * chans, steps), BF16),
        ],
    )(*arrived, entries, taps, filter_spec, *tables)
    filter_grads = call(
        lagged_kernel,
        "lagged",
        24,
        out_shape=shape((2, chans, steps), F32),
        cost_estimate=pl.CostEstimate(
            flops=10**10, bytes_accessed=3 * 10**7, transcendentals=0
        ),
    )(results[-1], *tables)
    if packed_form:
        mixer_out, weight_grads, tap_grads = call(
            unpack_kernel,
            "unpack",
            16,
            out_shape=(
                shape((tok_rows, width), BF16),
                shape((rows, 3 * width), F32),
                shape((3, 3 * width), F32),
            ),
        )(exchange(results[0]))
    else:
        mixer_out, weight_grads, tap_grads = send_results(*results[:3], peers, rows)
    return (mixer_out, weight_grads, tap_grads, filter_grads)


def solution(mesh):
    return jax.shard_map(
        local,
        mesh=mesh,
        in_specs=(
            P(("groups", "tm"), None),
            P("groups"),
            P(),
            P("tm", None),
            P(),
            P(None, "tm", None),
            P(("groups", "tm"), None),
        ),
        out_specs=(
            P(("groups", "tm"), None),
            P(("groups", "tm"), None),
            P("groups", None),
            P("groups", "tm", None),
        ),
        check_vma=False,
    )
```

time: 112 us -> 71.5 us (0.64)
  local copies, waits for them, and re-layouts: 37.7 us -> 19 us
  between operations: 16.2 us -> 0.75 us
  waiting for transfers between devices: 7.14 us -> 20.5 us
  starting transfers between devices: 25.6 us -> 12.5 us
  other arithmetic: 4.71 us -> 0 us
  Pallas kernels: 19.7 us -> 18 us
    reshape x12 -> x0, local copies, waits for them, and re-layouts: 13.9 us -> none  [the longest x3 5.68 us: local(): widen(weight_grads).transpose(1, 2, 0, 3).reshape(rows, 3 * width)]
    all_to_all x4 -> x2, waiting for transfers between devices: 7.14 us -> 20.5 us  [exchange(): return lax.all_to_all(blocks, 'tm', split_axis=0, concat_axis=0, tiled=True)]
    all_to_all x4 -> x2, starting transfers between devices: 25.6 us -> 12.5 us  [exchange(): return lax.all_to_all(blocks, 'tm', split_axis=0, concat_axis=0, tiled=True)]
    concatenate x3 -> x0, other arithmetic: 2.7 us -> none  [the longest x1 1.81 us: local(): arrived = exchange(jnp.concatenate([weight_send, tap_send], axis=1))]
    pallas_call x4 -> x5, Pallas kernels: 19.7 us -> 18 us  [the longest x1 11.7 us: local(): call(functools.partial(mixer_kernel, packed_form), 'mixer', 20 + 2 * hot_...]
    unnamed x54 -> x45, local copies, waits for them, and re-layouts: 20.2 us -> 18.6 us
    slice x4 -> x0, local copies, waits for them, and re-layouts: 1.55 us -> none  [the longest x1 0.85 us: local(): taps_moved = arrived[:, weight_send.shape[1]:].reshape(peers, -1)]
  transfers between devices with their start and end apart: 4 -> 2, of which waited for: 1 -> 2; matrix products, arithmetic and copies ran while one was open for 17% -> 0% of each run, Pallas kernels for 18% -> 6%
where the time goes in v2:
time: 71.5 us; the launch traced here: 70.7 us
  waiting for transfers between devices  20.5 us (29%)
  local copies, waits for them, and re-layouts  19 us (27%)
  Pallas kernels  18 us (25%)
  starting transfers between devices  12.5 us (17%)
  between operations  0.75 us (1%)
    all_to_all x2, waiting for transfers between devices, exchange(): return lax.all_to_all(blocks, 'tm', split_axis=0, concat_axis=0, tiled=True)  20.5 us
    unnamed x45, local copies, waits for them, and re-layouts  18.6 us
    all_to_all x2, starting transfers between devices, exchange(): return lax.all_to_all(blocks, 'tm', split_axis=0, concat_axis=0, tiled=True)  12.5 us
    pallas_call x1, Pallas kernels, local(): call(functools.partial(mixer_kernel, packed_form), 'mixer', 20 + 2 * hot_...  11.7 us
    pallas_call x1, Pallas kernels, local(): call(prepare_kernel, 'prepare', 32, in_specs=[pl.BlockSpec(memory_space=p...  1.98 us
    pallas_call x1, Pallas kernels, local(): call(lagged_kernel, 'lagged', 24, out_shape=shape((2, chans, steps), F32)...  1.92 us
  transfers between devices with their start and end apart: 2, of which 2 were waited for; matrix products, arithmetic and copies ran while one was open for 0% of the time, Pallas kernels for 6%

profile of v2, /device:TPU:0, one launch (start us, length us, event | category | flops | bytes accessed | tf_op | source)
XLA Modules:
  0.0 70.7 jit_solution(17154544396428312112)
XLA Ops:
  0.6 0.0 copy-start.21
  0.6 0.0 copy-start.20
  0.7 0.8 %copy.17.token_ids = s32[128,8]{1,0:T(8,128)S(1)} copy(s32[128,8]{0,1:T(8,128)} %param.13) | data formatting | bytes 8192 | tf_op args[0]
  1.5 0.0 copy-start.2
  1.5 1.0 %copy-done.2 = bf16[64,3072]{1,0:T(8,128)(2,1)S(1)} copy-done((bf16[64,3072]{1,0:T(8,128)(2,1)S(1)}, bf16[64,3072]{1,0:T(8,128)(2,1)}, u32[]{:S(2)}) %copy-start.2) | copy-done | bytes 393240
  2.5 0.0 copy-start.5
  2.5 0.9 %copy-done.5 = bf16[128,1024]{1,0:T(8,128)(2,1)S(1)} copy-done((bf16[128,1024]{1,0:T(8,128)(2,1)S(1)}, bf16[128,1024]{1,0:T(8,128)(2,1)}, u32[]{:S(2)}) %copy-start.5) | copy-done | bytes 262168
  3.4 0.0 copy-start.3
  3.4 0.0 copy-start.4
  3.4 0.0 copy-start.6
  3.4 1.1 %pack.1 = bf16[16,176,128]{2,1,0:T(8,128)(2,1)} custom-call(s32[128,8]{1,0:T(8,128)S(1)} %copy.17.token_ids, bf16[64,3072]{1,0:T(8,128)(2,1)S(1)} %copy-done.2, bf16[128,1024]{1,0:T(8,128)(2,1)S(1)} %copy-done.5), custom_call_target="tpu_custom_call" | custom-call | tf_op jit(solution)/shard_map/pack/pallas_call | solution.py:500
  4.5 7.4 %all-to-all-start = ((bf16[16,176,128]{2,1,0:T(8,128)(2,1)}), bf16[16,176,128]{2,1,0:T(8,128)(2,1)S(1)}, u32[]{:S(2)}, u32[]{:S(2)}) async-start(bf16[16,176,128]{2,1,0:T(8,128)(2,1)} %pack.1), calls=%async_computation | async-start | bytes 1441792 | tf_op jit(solution)/shard_map/all_to_all | solution.py:437
  11.9 0.0 copy-done.21
  12.0 0.1 reshape.14
  12.1 0.1 broadcast_in_dim.7
  12.2 0.0 copy-done.20
  12.2 0.0 copy-done.3
  12.2 0.0 copy-done.4
  12.2 0.0 copy-done.6
  12.2 0.0 copy-start.7
  12.2 0.9 %copy-done.7 = f32[256,128]{1,0:T(8,128)S(1)} copy-done((f32[256,128]{1,0:T(8,128)S(1)}, f32[256,128]{1,0:T(8,128)}, u32[]{:S(2)}) %copy-start.7) | copy-done | bytes 131096
  13.1 0.0 copy-start.10
  13.1 0.9 %copy-done.10 = bf16[256,256]{1,0:T(8,128)(2,1)S(1)} copy-done((bf16[256,256]{1,0:T(8,128)(2,1)S(1)}, bf16[256,256]{1,0:T(8,128)(2,1)}, u32[]{:S(2)}) %copy-start.10) | copy-done | bytes 131096
  14.0 0.0 copy-start.13
  14.0 0.9 %copy-done.13 = bf16[256,256]{1,0:T(8,128)(2,1)S(1)} copy-done((bf16[256,256]{1,0:T(8,128)(2,1)S(1)}, bf16[256,256]{1,0:T(8,128)(2,1)}, u32[]{:S(2)}) %copy-start.13) | copy-done | bytes 131096
  14.9 1.6 %copy-done.16 = bf16[1024,1024]{1,0:T(8,128)(2,1)S(1)} copy-done((bf16[1024,1024]{1,0:T(8,128)(2,1)S(1)}, bf16[1024,1024]{1,0:T(8,128)(2,1)}, u32[]{:S(2)}) %copy-start.16) | copy-done | bytes 2097176
  16.5 1.0 %copy-done.19 = bf16[2,64,2048]{2,1,0:T(8,128)(2,1)S(1)} copy-done((bf16[2,64,2048]{2,1,0:T(8,128)(2,1)S(1)}, bf16[2,64,2048]{2,1,0:T(8,128)(2,1)}, u32[]{:S(2)}) %copy-start.19) | copy-done | bytes 524312
  17.5 2.0 %prepare.1 = (f32[2,4,256,256]{3,2,1,0:T(8,128)S(1)}, bf16[1024,1024]{1,0:T(8,128)(2,1)S(1)}) custom-call(s32[8]{0:T(128)S(1)} %copy-done.20, bf16[2,64,2048]{2,1,0:T(8,128)(2,1)S(1)} %copy-done.19, bf16[1024,1024]{1,0:T(8,128)(2,1)S(1)} %copy-done.16, bf16[512,256]{1,0:T(8,128)(2,1)S(1)} %copy-done.4, bf16[256,512]{1,0:T(8,128)(2,1)S(1)} %copy-done.3, ...), custom_call_target="tpu_custom_call" | custom-call | flops 10000000000 | bytes 30000000 | tf_op jit(solution)/shard_map/prepare/pallas_call | solution.py:506
  19.5 0.0 copy-start
  19.5 1.3 %copy-done = bf16[1024,1024]{1,0:T(8,128)(2,1)} copy-done((bf16[1024,1024]{1,0:T(8,128)(2,1)}, bf16[1024,1024]{1,0:T(8,128)(2,1)S(1)}, u32[]{:S(2)}) %copy-start) | copy-done | bytes 2097176
  20.9 8.7 %all-to-all-done.refs_0_ = bf16[16,176,128]{2,1,0:T(8,128)(2,1)S(1)} async-done(((bf16[16,176,128]{2,1,0:T(8,128)(2,1)}), bf16[16,176,128]{2,1,0:T(8,128)(2,1)S(1)}, u32[]{:S(2)}, u32[]{:S(2)}) %all-to-all-start) | async-done | bytes 720928 | tf_op jit(solution)/shard_map/all_to_all | solution.py:437
  29.6 0.1 broadcast_in_dim.8.refs_2_
  29.7 0.0 copy-start.1
  29.7 1.6 %copy-done.1 = bf16[1024,1024]{1,0:T(8,128)(2,1)S(1)} copy-done((bf16[1024,1024]{1,0:T(8,128)(2,1)S(1)}, bf16[1024,1024]{1,0:T(8,128)(2,1)}, u32[]{:S(2)}) %copy-start.1) | copy-done | bytes 2097176
  31.3 0.9 %copy-done.8 = f32[256,128]{1,0:T(8,128)S(1)} copy-done((f32[256,128]{1,0:T(8,128)S(1)}, f32[256,128]{1,0:T(8,128)}, u32[]{:S(2)}) %copy-start.8) | copy-done | bytes 131096
  32.2 0.9 %copy-done.11 = bf16[256,256]{1,0:T(8,128)(2,1)S(1)} copy-done((bf16[256,256]{1,0:T(8,128)(2,1)S(1)}, bf16[256,256]{1,0:T(8,128)(2,1)}, u32[]{:S(2)}) %copy-start.11) | copy-done | bytes 131096
  33.1 0.9 %copy-done.14 = bf16[256,256]{1,0:T(8,128)(2,1)S(1)} copy-done((bf16[256,256]{1,0:T(8,128)(2,1)S(1)}, bf16[256,256]{1,0:T(8,128)(2,1)}, u32[]{:S(2)}) %copy-start.14) | copy-done | bytes 131096
  34.0 11.7 %mixer.1 = (bf16[16,176,128]{2,1,0:T(8,128)(2,1)}, bf16[2,4,256,256]{3,2,1,0:T(8,128)(2,1)S(1)}) custom-call(bf16[16,176,128]{2,1,0:T(8,128)(2,1)S(1)} %all-to-all-done.refs_0_, bf16[1024,1024]{1,0:T(8,128)(2,1)S(1)} %copy-done.1, f32[3,192,128]{2,1,0:T(8,128)S(1)} %broadcast_in_dim.8.refs_2_, f32[2,4,256,256]{3,2,1,0:T(8,128)S(1)} %get-tuple-element.12.refs_3_, ...), custom_call_target="tpu_custom_call" | custom-call | tf_op jit(solution)/shard_map/mixer/pallas_call | solution.py:530
  45.7 1.0 %copy-done.17 = bf16[2,4,256,256]{3,2,1,0:T(8,128)(2,1)} copy-done((bf16[2,4,256,256]{3,2,1,0:T(8,128)(2,1)}, bf16[2,4,256,256]{3,2,1,0:T(8,128)(2,1)S(1)}, u32[]{:S(2)}) %copy-start.17) | copy-done | bytes 1048600
  46.7 5.1 %all-to-all-start.1 = ((bf16[16,176,128]{2,1,0:T(8,128)(2,1)}), bf16[16,176,128]{2,1,0:T(8,128)(2,1)S(1)}, u32[]{:S(2)}, u32[]{:S(2)}) async-start(bf16[16,176,128]{2,1,0:T(8,128)(2,1)} %get-tuple-element.13), calls=%async_computation.1 | async-start | bytes 1441792 | tf_op jit(solution)/shard_map/all_to_all | solution.py:437
  51.8 0.0 copy-start.9
  51.9 0.9 %copy-done.9 = f32[256,128]{1,0:T(8,128)S(1)} copy-done((f32[256,128]{1,0:T(8,128)S(1)}, f32[256,128]{1,0:T(8,128)}, u32[]{:S(2)}) %copy-start.9) | copy-done | bytes 131096
  52.7 0.9 %copy-done.12 = bf16[256,256]{1,0:T(8,128)(2,1)S(1)} copy-done((bf16[256,256]{1,0:T(8,128)(2,1)S(1)}, bf16[256,256]{1,0:T(8,128)(2,1)}, u32[]{:S(2)}) %copy-start.12) | copy-done | bytes 131096
  53.7 0.9 %copy-done.15 = bf16[256,256]{1,0:T(8,128)(2,1)S(1)} copy-done((bf16[256,256]{1,0:T(8,128)(2,1)S(1)}, bf16[256,256]{1,0:T(8,128)(2,1)}, u32[]{:S(2)}) %copy-start.15) | copy-done | bytes 131096
  54.6 1.2 %copy-done.18 = bf16[2,4,256,256]{3,2,1,0:T(8,128)(2,1)S(1)} copy-done((bf16[2,4,256,256]{3,2,1,0:T(8,128)(2,1)S(1)}, bf16[2,4,256,256]{3,2,1,0:T(8,128)(2,1)}, u32[]{:S(2)}) %copy-start.18) | copy-done | bytes 1048600
  55.8 1.9 %lagged.1 = f32[2,64,2048]{2,1,0:T(8,128)} custom-call(bf16[2,4,256,256]{3,2,1,0:T(8,128)(2,1)S(1)} %copy-done.18, bf16[512,256]{1,0:T(8,128)(2,1)S(1)} %copy-done.4, bf16[256,512]{1,0:T(8,128)(2,1)S(1)} %copy-done.3, bf16[256,256]{1,0:T(8,128)(2,1)S(1)} %copy-done.15, bf16[256,256]{1,0:T(8,128)(2,1)S(1)} %copy-done.12, f32[256,128]{1,0:T(8,128)S(1)} %copy-done.9, ...), custom_call_target="tpu_custom_call" | custom-call | flops 10000000000 | bytes 30000000 | tf_op jit(solution)/shard_map/lagged/pallas_call | solution.py:543
  57.7 11.8 %all-to-all-done.1.packed = bf16[16,176,128]{2,1,0:T(8,128)(2,1)S(1)} async-done(((bf16[16,176,128]{2,1,0:T(8,128)(2,1)}), bf16[16,176,128]{2,1,0:T(8,128)(2,1)S(1)}, u32[]{:S(2)}, u32[]{:S(2)}) %all-to-all-start.1) | async-done | bytes 720928 | tf_op jit(solution)/shard_map/all_to_all | solution.py:437
  69.5 1.2 %unpack.1 = (bf16[128,1024]{1,0:T(8,128)(2,1)}, f32[64,3072]{1,0:T(8,128)}, f32[3,3072]{1,0:T(4,128)}) custom-call(bf16[16,176,128]{2,1,0:T(8,128)(2,1)S(1)} %all-to-all-done.1.packed), custom_call_target="tpu_custom_call" | custom-call | tf_op jit(solution)/shard_map/unpack/pallas_call | solution.py:553
  (10 shorter events, 0.0 us)
Async XLA Ops:
  0.6 11.3 %copy-start.21 = (f32[3,3072]{1,0:T(4,128)S(1)}, f32[3,3072]{1,0:T(4,128)}, u32[]{:S(2)}) copy-start(f32[3,3072]{1,0:T(4,128)} %param.17) | copy-start | bytes 110596
  0.6 11.5 %copy-start.20 = (s32[8]{0:T(128)S(1)}, s32[8]{0:T(128)}, u32[]{:S(2)}) copy-start(s32[8]{0:T(128)} %offsets.1) | copy-start | bytes 100
  1.5 1.0 %copy-start.2 = (bf16[64,3072]{1,0:T(8,128)(2,1)S(1)}, bf16[64,3072]{1,0:T(8,128)(2,1)}, u32[]{:S(2)}) copy-start(bf16[64,3072]{1,0:T(8,128)(2,1)} %w_in.1) | copy-start | bytes 1179652
  2.5 0.9 %copy-start.5 = (bf16[128,1024]{1,0:T(8,128)(2,1)S(1)}, bf16[128,1024]{1,0:T(8,128)(2,1)}, u32[]{:S(2)}) copy-start(bf16[128,1024]{1,0:T(8,128)(2,1)} %cotangent.1) | copy-start | bytes 786436
  3.4 8.8 %copy-start.3 = (bf16[256,512]{1,0:T(8,128)(2,1)S(1)}, bf16[256,512]{1,0:T(8,128)(2,1)}, u32[]{:S(2)}) copy-start(bf16[256,512]{1,0:T(8,128)(2,1)} %constant.23.clone.rest_1_.refs_5_) | copy-start | bytes 786436
  3.4 8.8 %copy-start.4 = (bf16[512,256]{1,0:T(8,128)(2,1)S(1)}, bf16[512,256]{1,0:T(8,128)(2,1)}, u32[]{:S(2)}) copy-start(bf16[512,256]{1,0:T(8,128)(2,1)} %constant.22.clone.rest_0_.refs_4_) | copy-start | bytes 786436
  3.4 8.8 %copy-start.6 = (f32[256,128]{1,0:T(8,128)S(1)}, f32[256,128]{1,0:T(8,128)}, u32[]{:S(2)}) copy-start(f32[256,128]{1,0:T(8,128)} %constant.27.clone.rest_5_.refs_9_) | copy-start | bytes 393220
  4.5 25.0 %all-to-all-start = ((bf16[16,176,128]{2,1,0:T(8,128)(2,1)}), bf16[16,176,128]{2,1,0:T(8,128)(2,1)S(1)}, u32[]{:S(2)}, u32[]{:S(2)}) async-start(bf16[16,176,128]{2,1,0:T(8,128)(2,1)} %pack.1), calls=%async_computation | async-start | bytes 1441792 | tf_op jit(solution)/shard_map/all_to_all | solution.py:437
  12.2 0.9 %copy-start.7 = (f32[256,128]{1,0:T(8,128)S(1)}, f32[256,128]{1,0:T(8,128)}, u32[]{:S(2)}) copy-start(f32[256,128]{1,0:T(8,128)} %constant.26.clone.rest_4_.refs_8_) | copy-start | bytes 393220
  13.1 0.9 %copy-start.10 = (bf16[256,256]{1,0:T(8,128)(2,1)S(1)}, bf16[256,256]{1,0:T(8,128)(2,1)}, u32[]{:S(2)}) copy-start(bf16[256,256]{1,0:T(8,128)(2,1)} %constant.25.clone.rest_3_.refs_7_) | copy-start | bytes 393220
  14.0 0.9 %copy-start.13 = (bf16[256,256]{1,0:T(8,128)(2,1)S(1)}, bf16[256,256]{1,0:T(8,128)(2,1)}, u32[]{:S(2)}) copy-start(bf16[256,256]{1,0:T(8,128)(2,1)} %constant.24.clone.rest_2_.refs_6_) | copy-start | bytes 393220
  14.9 1.6 %copy-start.16 = (bf16[1024,1024]{1,0:T(8,128)(2,1)S(1)}, bf16[1024,1024]{1,0:T(8,128)(2,1)}, u32[]{:S(2)}) copy-start(bf16[1024,1024]{1,0:T(8,128)(2,1)} %table.1) | copy-start | bytes 6291460
  16.5 1.0 %copy-start.19 = (bf16[2,64,2048]{2,1,0:T(8,128)(2,1)S(1)}, bf16[2,64,2048]{2,1,0:T(8,128)(2,1)}, u32[]{:S(2)}) copy-start(bf16[2,64,2048]{2,1,0:T(8,128)(2,1)} %filters.1) | copy-start | bytes 1572868
  19.5 1.3 %copy-start = (bf16[1024,1024]{1,0:T(8,128)(2,1)}, bf16[1024,1024]{1,0:T(8,128)(2,1)S(1)}, u32[]{:S(2)}) copy-start(bf16[1024,1024]{1,0:T(8,128)(2,1)S(1)} %get-tuple-element.11.refs_1_) | copy-start | bytes 6291460
  29.7 1.6 %copy-start.1 = (bf16[1024,1024]{1,0:T(8,128)(2,1)S(1)}, bf16[1024,1024]{1,0:T(8,128)(2,1)}, u32[]{:S(2)}) copy-start(bf16[1024,1024]{1,0:T(8,128)(2,1)} %copy-done) | copy-start | bytes 6291460
  31.3 0.9 %copy-start.8 = (f32[256,128]{1,0:T(8,128)S(1)}, f32[256,128]{1,0:T(8,128)}, u32[]{:S(2)}) copy-start(f32[256,128]{1,0:T(8,128)} %constant.26.clone.rest_4_.refs_8_) | copy-start | bytes 393220
  32.2 0.9 %copy-start.11 = (bf16[256,256]{1,0:T(8,128)(2,1)S(1)}, bf16[256,256]{1,0:T(8,128)(2,1)}, u32[]{:S(2)}) copy-start(bf16[256,256]{1,0:T(8,128)(2,1)} %constant.25.clone.rest_3_.refs_7_) | copy-start | bytes 393220
  33.1 0.9 %copy-start.14 = (bf16[256,256]{1,0:T(8,128)(2,1)S(1)}, bf16[256,256]{1,0:T(8,128)(2,1)}, u32[]{:S(2)}) copy-start(bf16[256,256]{1,0:T(8,128)(2,1)} %constant.24.clone.rest_2_.refs_6_) | copy-start | bytes 393220
  45.7 1.0 %copy-start.17 = (bf16[2,4,256,256]{3,2,1,0:T(8,128)(2,1)}, bf16[2,4,256,256]{3,2,1,0:T(8,128)(2,1)S(1)}, u32[]{:S(2)}) copy-start(bf16[2,4,256,256]{3,2,1,0:T(8,128)(2,1)S(1)} %get-tuple-element.17.lagged_spec) | copy-start | bytes 3145732
  46.7 22.8 %all-to-all-start.1 = ((bf16[16,176,128]{2,1,0:T(8,128)(2,1)}), bf16[16,176,128]{2,1,0:T(8,128)(2,1)S(1)}, u32[]{:S(2)}, u32[]{:S(2)}) async-start(bf16[16,176,128]{2,1,0:T(8,128)(2,1)} %get-tuple-element.13), calls=%async_computation.1 | async-start | bytes 1441792 | tf_op jit(solution)/shard_map/all_to_all | solution.py:437
  51.8 0.9 %copy-start.9 = (f32[256,128]{1,0:T(8,128)S(1)}, f32[256,128]{1,0:T(8,128)}, u32[]{:S(2)}) copy-start(f32[256,128]{1,0:T(8,128)} %constant.26.clone.rest_4_.refs_8_) | copy-start | bytes 393220
  52.7 0.9 %copy-start.12 = (bf16[256,256]{1,0:T(8,128)(2,1)S(1)}, bf16[256,256]{1,0:T(8,128)(2,1)}, u32[]{:S(2)}) copy-start(bf16[256,256]{1,0:T(8,128)(2,1)} %constant.25.clone.rest_3_.refs_7_) | copy-start | bytes 393220
  53.7 0.9 %copy-start.15 = (bf16[256,256]{1,0:T(8,128)(2,1)S(1)}, bf16[256,256]{1,0:T(8,128)(2,1)}, u32[]{:S(2)}) copy-start(bf16[256,256]{1,0:T(8,128)(2,1)} %constant.24.clone.rest_2_.refs_6_) | copy-start | bytes 393220
  54.6 1.2 %copy-start.18 = (bf16[2,4,256,256]{3,2,1,0:T(8,128)(2,1)S(1)}, bf16[2,4,256,256]{3,2,1,0:T(8,128)(2,1)}, u32[]{:S(2)}) copy-start(bf16[2,4,256,256]{3,2,1,0:T(8,128)(2,1)} %copy-done.17) | copy-start | bytes 3145732

commit v3 on v2

--- a/solution.py
+++ b/solution.py
@@ -183,16 +183,23 @@
     return [slice(low, high) for low, high in zip(marks[:-1], marks[1:])]
 
 
-def pack_kernel(token_ids, w_in, cotangent, packed):
+def pack_kernel(token_ids, w_in_far, cotangent_far, packed_far, w_in, cotangent, packed, sems):
     peers = packed.shape[0]
     rows, wide = w_in.shape
     half = rows // 2
     part_two, part_one, part_time, part_ids = packed_parts(rows)
-    fields = token_ids.shape[1]
-    ids = jnp.concatenate(
-        [widen(token_ids[...]), jnp.zeros((token_ids.shape[0], LANES - fields), F32)], axis=1
-    )
-    ids = ids.T[:16].astype(BF16)
+    arrivals = [
+        pltpu.make_async_copy(far, near, sems.at[place])
+        for place, (far, near) in enumerate(((w_in_far, w_in), (cotangent_far, cotangent)))
+    ]
+    for copy in arrivals:
+        copy.start()
+    fields, steps = token_ids.shape
+    ids = jnp.concatenate([widen(token_ids[...]), jnp.zeros((16 - fields, steps), F32)], axis=0)
+    ids = ids.astype(BF16)
+    for copy in arrivals:
+        copy.wait()
+    departures = []
     for pair in range(peers // 2):
         tiles = []
         for column in range(3):
@@ -216,6 +223,13 @@
         packed[odd, part_time, :] = turned[rows:]
         packed[even, part_ids, :] = ids
         packed[odd, part_ids, :] = ids
+        both = pl.ds(even, 2)
+        departures.append(
+            pltpu.make_async_copy(packed.at[both], packed_far.at[both], sems.at[2 + pair])
+        )
+        departures[-1].start()
+    for copy in departures:
+        copy.wait()
 
 
 def unpack_kernel(packed, mixer_out, weight_grads, tap_grads):
@@ -276,28 +290,45 @@
         def ids_of(block):
             return widen(ids[block])
 
-    entries, taps, filter_spec = refs[:3]
-    tables, refs = refs[3:9], refs[9:]
+    far, refs = refs[:9], refs[9:]
+    lagged_far, refs = refs[0], refs[1:]
     if packed_form:
-        sent, lagged_spec = refs[:2]
-        refs = refs[2:]
+        sent_far, refs = refs[0], refs[1:]
+    else:
+        (mixer_out, weight_part, tap_terms), refs = refs[:3], refs[3:]
+    near, refs = refs[:9], refs[9:]
+    sems, lagged_spec, hot, proj, mixed, grad_mixed, grad_proj = refs[:7]
+    if packed_form:
+        sent = refs[7]
         mixer_out = sent.at[:, part_time, :]
-    else:
-        mixer_out, weight_part, tap_terms, lagged_spec = refs[:4]
-        refs = refs[4:]
-    hot, proj, mixed, grad_mixed, grad_proj = refs
+    entries, taps, filter_spec = near[:3]
+    tables = near[3:]
     blocks = mixed.shape[0]
     codes = LANES
-
+    arrivals = [
+        pltpu.make_async_copy(source, target, sems.at[place])
+        for place, (source, target) in enumerate(zip(far, near))
+    ]
+    for copy in arrivals:
+        copy.start()
+    departures = []
+
+    def depart(source, target):
+        departures.append(
+            pltpu.make_async_copy(source, target, sems.at[len(arrivals) + len(departures)])
+        )
+        departures[-1].start()
+
+    for block in range(blocks):
+        hot[:, block * LANES : (block + 1) * LANES] = one_hot(ids_of(block), codes)
+    arrivals[0].wait()
     coded = dot(entries[...], w_cols).T[: 3 * chans].astype(BF16)
+    arrivals[1].wait()
     lane = lax.broadcasted_iota(jnp.int32, (3 * chans, LANES), 1)
     last1 = jnp.zeros((3 * chans, LANES), F32)
     last2 = last1
     for pair in range(blocks // 2):
         lanes = slice(2 * pair * LANES, (2 * pair + 2) * LANES)
-        hot[:, lanes] = jnp.concatenate(
-            [one_hot(ids_of(2 * pair + side), codes) for side in range(2)], axis=1
-        )
         both = dot(coded, hot[:, lanes]).astype(BF16)
         for side in range(2):
             block = 2 * pair + side
@@ -317,6 +348,8 @@
     def blocked(value):
         return value.reshape(blocks, GROUP, LANES)
 
+    for copy in arrivals[2:]:
+        copy.wait()
     for batch in batches(chans):
         value_spec = forward([column(mixed, group) for group in batch], tables)
         turned = [
@@ -343,6 +376,9 @@
                 (upstream * second_conv).astype(BF16)
             )
             series.append((upstream * gate).astype(BF16))
+        if packed_form:
+            rows = pl.ds(part_time.start + batch[0] * GROUP, len(batch) * GROUP)
+            depart(sent.at[:, rows, :], sent_far.at[:, rows, :])
         grad_spec = forward(series, tables)
         turned = []
         for place, group in enumerate(batch):
@@ -361,6 +397,8 @@
         for place, group in enumerate(batch):
             lagged_spec[0, group] = product(grad_spec[place], value_spec[place], True).astype(BF16)
             turned.append(product(grad_spec[place], filter_spec[0, group], True))
+        some = pl.ds(batch[0], len(batch))
+        depart(lagged_spec.at[:, some], lagged_far.at[:, some])
         for group, signal in zip(batch, inverse(turned, tables)):
             grad_mixed[:, channel_rows(group), :] = blocked(signal.astype(BF16))
 
@@ -387,6 +425,8 @@
         weight_part[...] = weights.T.astype(BF16)
         for tap in range(3):
             tap_terms[tap] = jnp.sum(sums[tap], axis=1, keepdims=True)
+        for copy in departures:
+            copy.wait()
         return
     for tap in range(3):
         sums[tap] = jnp.sum(sums[tap].T, axis=0, keepdims=True)
@@ -402,17 +442,22 @@
     )
     high = rounded(total)
     small = jnp.concatenate([high, total - high], axis=0).astype(BF16)
+    for block in range(blocks):
+        sent[block, part_small, :] = small
+    depart(sent.at[:, part_small, :], sent_far.at[:, part_small, :])
     two = weights[: 2 * chans].T
+    sent[:, part_two, :] = two.astype(BF16).reshape(blocks, chans, LANES)
+    depart(sent.at[:, part_two, :], sent_far.at[:, part_two, :])
     one = jnp.concatenate([weights[2 * chans :], jnp.zeros((LANES - chans, width), F32)], axis=0).T
     one = one.reshape(blocks, chans, LANES)
     half = chans // 2
     turned = pltpu.roll(flat(one[:, half:]), LANES // 2, 1)
     one = flat(one[:, :half])
     one = jnp.where(lax.broadcasted_iota(jnp.int32, one.shape, 1) < LANES // 2, one, turned)
-    sent[:, part_two, :] = two.astype(BF16).reshape(blocks, chans, LANES)
     sent[:, part_one, :] = one.astype(BF16).reshape(blocks, half, LANES)
-    for block in range(blocks):
-        sent[block, part_small, :] = small
+    depart(sent.at[:, part_one, :], sent_far.at[:, part_one, :])
+    for copy in departures:
+        copy.wait()
 
 
 def lagged_kernel(lagged_spec, *rest):
@@ -496,18 +541,33 @@
     wide = (peers, 3 * chans, LANES)
     packed = shape((peers, packed_parts(rows)[-1].stop, LANES), BF16)
 
+    near = pl.BlockSpec(memory_space=pltpu.VMEM)
+    far = pl.BlockSpec(memory_space=pltpu.HBM)
+
     if packed_form:
-        sent = call(pack_kernel, "pack", 16, out_shape=packed)(token_ids, w_in, cotangent)
+        sent = call(
+            pack_kernel,
+            "pack",
+            16,
+            in_specs=[near, far, far],
+            out_specs=far,
+            out_shape=packed,
+            scratch_shapes=[
+                pltpu.VMEM(w_in.shape, BF16),
+                pltpu.VMEM(cotangent.shape, BF16),
+                pltpu.VMEM(packed.shape, BF16),
+                pltpu.SemaphoreType.DMA((2 + peers // 2,)),
+            ],
+        )(token_ids.T, w_in, cotangent)
         arrived = (exchange(sent),)
     else:
         arrived = send_inputs(token_ids, w_in, cotangent, peers)
 
-    whole = pl.BlockSpec(memory_space=pltpu.VMEM)
     filter_spec, entries = call(
         prepare_kernel,
         "prepare",
         32,
-        in_specs=[pl.BlockSpec(memory_space=pltpu.SMEM)] + [whole] * 8,
+        in_specs=[pl.BlockSpec(memory_space=pltpu.SMEM)] + [near] * 8,
         out_shape=(shape(spec, F32), shape(embed_table.shape, BF16)),
         cost_estimate=pl.CostEstimate(
             flops=10**10, bytes_accessed=3 * 10**7, transcendentals=0
@@ -518,28 +578,39 @@
     taps = jnp.broadcast_to(taps.reshape(3, 3 * chans, 1), (3, 3 * chans, LANES))
 
     if packed_form:
-        out_shape = (packed, shape(spec, BF16))
+        out_shape = (shape(spec, BF16), packed)
+        out_specs = (far, far)
+        scratch_shapes = [pltpu.VMEM(packed.shape, BF16)]
     else:
         out_shape = (
+            shape(spec, BF16),
             shape(moved, BF16),
             shape((width, 3 * chans), BF16),
             shape((3, 3 * chans, 1), F32),
-            shape(spec, BF16),
-        )
+        )
+        out_specs = (far, near, near, near)
+        scratch_shapes = []
+    operands = (entries, taps, filter_spec) + tables
     hot_bytes = 2 * embed_table.shape[0] * steps
     results = call(
         functools.partial(mixer_kernel, packed_form),
         "mixer",
         20 + 2 * hot_bytes // 2**20,
+        in_specs=[near] * len(arrived) + [far] * len(operands),
         out_shape=out_shape,
-        scratch_shapes=[
+        out_specs=out_specs,
+        scratch_shapes=[pltpu.VMEM(operand.shape, operand.dtype) for operand in operands]
+        + [
+            pltpu.SemaphoreType.DMA((len(operands) + 2 * groups + 3,)),
+            pltpu.VMEM(spec, BF16),
             pltpu.VMEM((embed_table.shape[0], steps), BF16),
             pltpu.VMEM(wide, BF16),
             pltpu.VMEM(wide, BF16),
             pltpu.VMEM(wide, BF16),
             pltpu.VMEM((3 * chans, steps), BF16),
-        ],
-    )(*arrived, entries, taps, filter_spec, *tables)
+        ]
+        + scratch_shapes,
+    )(*arrived, *operands)
     filter_grads = call(
         lagged_kernel,
         "lagged",
@@ -548,7 +619,7 @@
         cost_estimate=pl.CostEstimate(
             flops=10**10, bytes_accessed=3 * 10**7, transcendentals=0
         ),
-    )(results[-1], *tables)
+    )(results[0], *tables)
     if packed_form:
         mixer_out, weight_grads, tap_grads = call(
             unpack_kernel,
@@ -559,9 +630,9 @@
                 shape((rows, 3 * width), F32),
                 shape((3, 3 * width), F32),
             ),
-        )(exchange(results[0]))
+        )(exchange(results[1]))
     else:
-        mixer_out, weight_grads, tap_grads = send_results(*results[:3], peers, rows)
+        mixer_out, weight_grads, tap_grads = send_results(*results[1:], peers, rows)
     return (mixer_out, weight_grads, tap_grads, filter_grads)
 
 

time: 71.5 us -> 74.4 us (1.041)
  Pallas kernels: 18 us -> 21 us
    pallas_call x1, Pallas kernels: 11.7 us -> 14.5 us  [local(): call(functools.partial(mixer_kernel, packed_form), 'mixer', 20 + 2 * hot_...]
    unnamed x45 -> x46, local copies, waits for them, and re-layouts: 18.6 us -> 18.5 us
  transfers between devices with their start and end apart: 2 -> 2, of which waited for: 2 -> 2; matrix products, arithmetic and copies ran while one was open for 0% -> 0% of each run, Pallas kernels for 6% -> 5%
where the time goes in v3:
time: 74.4 us; the launch traced here: 73.7 us
  Pallas kernels  21 us (28%)
  waiting for transfers between devices  20.5 us (28%)
  local copies, waits for them, and re-layouts  18.9 us (25%)
  starting transfers between devices  12.5 us (17%)
  between operations  0.78 us (1%)
    all_to_all x2, waiting for transfers between devices, exchange(): return lax.all_to_all(blocks, 'tm', split_axis=0, concat_axis=0, tiled=True)  20.5 us
    unnamed x46, local copies, waits for them, and re-layouts  18.5 us
    pallas_call x1, Pallas kernels, local(): call(functools.partial(mixer_kernel, packed_form), 'mixer', 20 + 2 * hot_...  14.5 us
    all_to_all x2, starting transfers between devices, exchange(): return lax.all_to_all(blocks, 'tm', split_axis=0, concat_axis=0, tiled=True)  12.5 us
    pallas_call x1, Pallas kernels, local(): call(prepare_kernel, 'prepare', 32, in_specs=[pl.BlockSpec(memory_space=p...  1.98 us
    pallas_call x1, Pallas kernels, local(): call(lagged_kernel, 'lagged', 24, out_shape=shape((2, chans, steps), F32)...  1.92 us
  transfers between devices with their start and end apart: 2, of which 2 were waited for; matrix products, arithmetic and copies ran while one was open for 0% of the time, Pallas kernels for 5%

profile of v3, /device:TPU:0, one launch (start us, length us, event | category | flops | bytes accessed | tf_op | source)
XLA Modules:
  0.0 73.7 jit_solution(11206078767933077114)
XLA Ops:
  0.6 0.0 copy-start.21
  0.6 0.0 copy-start.2
  0.7 1.0 %copy-done.2 = bf16[64,3072]{1,0:T(8,128)(2,1)S(1)} copy-done((bf16[64,3072]{1,0:T(8,128)(2,1)S(1)}, bf16[64,3072]{1,0:T(8,128)(2,1)}, u32[]{:S(2)}) %copy-start.2) | copy-done | bytes 393240
  1.6 0.0 copy-start.5
  1.6 0.9 %copy-done.5 = bf16[128,1024]{1,0:T(8,128)(2,1)S(1)} copy-done((bf16[128,1024]{1,0:T(8,128)(2,1)S(1)}, bf16[128,1024]{1,0:T(8,128)(2,1)}, u32[]{:S(2)}) %copy-start.5) | copy-done | bytes 262168
  2.6 0.0 copy-start.16
  2.6 0.7 copy-done.16
  3.3 0.0 copy-start.22
  3.3 0.0 copy-start.3
  3.3 0.0 copy-start.4
  3.3 0.0 copy-start.6
  3.3 1.3 %pack.1 = bf16[16,176,128]{2,1,0:T(8,128)(2,1)} custom-call(s32[8,128]{1,0:T(8,128)S(1)} %bitcast.1, bf16[64,3072]{1,0:T(8,128)(2,1)S(1)} %copy-done.2, bf16[128,1024]{1,0:T(8,128)(2,1)S(1)} %copy-done.5), custom_call_target="tpu_custom_call" | custom-call | tf_op jit(solution)/shard_map/pack/pallas_call | solution.py:548
  4.6 7.4 %all-to-all-start = ((bf16[16,176,128]{2,1,0:T(8,128)(2,1)}), bf16[16,176,128]{2,1,0:T(8,128)(2,1)S(1)}, u32[]{:S(2)}, u32[]{:S(2)}) async-start(bf16[16,176,128]{2,1,0:T(8,128)(2,1)} %pack.1), calls=%async_computation | async-start | bytes 1441792 | tf_op jit(solution)/shard_map/all_to_all | solution.py:482
  12.0 0.0 copy-done.22
  12.0 0.1 reshape.14
  12.2 0.1 broadcast_in_dim.7
  12.3 0.0 copy-done.21
  12.3 0.0 copy-done.3
  12.3 0.0 copy-done.4
  12.3 0.0 copy-done.6
  12.3 0.0 copy-start.7
  12.3 0.9 %copy-done.7 = f32[256,128]{1,0:T(8,128)S(1)} copy-done((f32[256,128]{1,0:T(8,128)S(1)}, f32[256,128]{1,0:T(8,128)}, u32[]{:S(2)}) %copy-start.7) | copy-done | bytes 131096
  13.2 0.9 %copy-done.10 = bf16[256,256]{1,0:T(8,128)(2,1)S(1)} copy-done((bf16[256,256]{1,0:T(8,128)(2,1)S(1)}, bf16[256,256]{1,0:T(8,128)(2,1)}, u32[]{:S(2)}) %copy-start.10) | copy-done | bytes 131096
  14.1 0.9 %copy-done.13 = bf16[256,256]{1,0:T(8,128)(2,1)S(1)} copy-done((bf16[256,256]{1,0:T(8,128)(2,1)S(1)}, bf16[256,256]{1,0:T(8,128)(2,1)}, u32[]{:S(2)}) %copy-start.13) | copy-done | bytes 131096
  15.0 1.6 %copy-done.17 = bf16[1024,1024]{1,0:T(8,128)(2,1)S(1)} copy-done((bf16[1024,1024]{1,0:T(8,128)(2,1)S(1)}, bf16[1024,1024]{1,0:T(8,128)(2,1)}, u32[]{:S(2)}) %copy-start.17) | copy-done | bytes 2097176
  16.6 1.0 %copy-done.20 = bf16[2,64,2048]{2,1,0:T(8,128)(2,1)S(1)} copy-done((bf16[2,64,2048]{2,1,0:T(8,128)(2,1)S(1)}, bf16[2,64,2048]{2,1,0:T(8,128)(2,1)}, u32[]{:S(2)}) %copy-start.20) | copy-done | bytes 524312
  17.6 2.0 %prepare.1 = (f32[2,4,256,256]{3,2,1,0:T(8,128)S(1)}, bf16[1024,1024]{1,0:T(8,128)(2,1)S(1)}) custom-call(s32[8]{0:T(128)S(1)} %copy-done.21, bf16[2,64,2048]{2,1,0:T(8,128)(2,1)S(1)} %copy-done.20, bf16[1024,1024]{1,0:T(8,128)(2,1)S(1)} %copy-done.17, bf16[512,256]{1,0:T(8,128)(2,1)S(1)} %copy-done.4, bf16[256,512]{1,0:T(8,128)(2,1)S(1)} %copy-done.3, ...), custom_call_target="tpu_custom_call" | custom-call | flops 10000000000 | bytes 30000000 | tf_op jit(solution)/shard_map/prepare/pallas_call | solution.py:566
  19.6 0.0 copy-start
  19.6 1.3 %copy-done = bf16[1024,1024]{1,0:T(8,128)(2,1)} copy-done((bf16[1024,1024]{1,0:T(8,128)(2,1)}, bf16[1024,1024]{1,0:T(8,128)(2,1)S(1)}, u32[]{:S(2)}) %copy-start) | copy-done | bytes 2097176
  20.9 8.7 %all-to-all-done.refs_0_ = bf16[16,176,128]{2,1,0:T(8,128)(2,1)S(1)} async-done(((bf16[16,176,128]{2,1,0:T(8,128)(2,1)}), bf16[16,176,128]{2,1,0:T(8,128)(2,1)S(1)}, u32[]{:S(2)}, u32[]{:S(2)}) %all-to-all-start) | async-done | bytes 720928 | tf_op jit(solution)/shard_map/all_to_all | solution.py:482
  29.7 0.1 broadcast_in_dim.8.refs_2_
  29.8 0.0 copy-start.1
  29.8 1.6 %copy-done.1 = bf16[1024,1024]{1,0:T(8,128)(2,1)S(1)} copy-done((bf16[1024,1024]{1,0:T(8,128)(2,1)S(1)}, bf16[1024,1024]{1,0:T(8,128)(2,1)}, u32[]{:S(2)}) %copy-start.1) | copy-done | bytes 2097176
  31.4 0.9 %copy-done.8 = f32[256,128]{1,0:T(8,128)S(1)} copy-done((f32[256,128]{1,0:T(8,128)S(1)}, f32[256,128]{1,0:T(8,128)}, u32[]{:S(2)}) %copy-start.8) | copy-done | bytes 131096
  32.3 0.9 %copy-done.11 = bf16[256,256]{1,0:T(8,128)(2,1)S(1)} copy-done((bf16[256,256]{1,0:T(8,128)(2,1)S(1)}, bf16[256,256]{1,0:T(8,128)(2,1)}, u32[]{:S(2)}) %copy-start.11) | copy-done | bytes 131096
  33.2 0.9 %copy-done.14 = bf16[256,256]{1,0:T(8,128)(2,1)S(1)} copy-done((bf16[256,256]{1,0:T(8,128)(2,1)S(1)}, bf16[256,256]{1,0:T(8,128)(2,1)}, u32[]{:S(2)}) %copy-start.14) | copy-done | bytes 131096
  34.1 14.5 %mixer.1 = (bf16[2,4,256,256]{3,2,1,0:T(8,128)(2,1)S(1)}, bf16[16,176,128]{2,1,0:T(8,128)(2,1)}) custom-call(bf16[16,176,128]{2,1,0:T(8,128)(2,1)S(1)} %all-to-all-done.refs_0_, bf16[1024,1024]{1,0:T(8,128)(2,1)S(1)} %copy-done.1, f32[3,192,128]{2,1,0:T(8,128)S(1)} %broadcast_in_dim.8.refs_2_, f32[2,4,256,256]{3,2,1,0:T(8,128)S(1)} %get-tuple-element.12.refs_3_, ...), custom_call_target="tpu_custom_call" | custom-call | tf_op jit(solution)/shard_map/mixer/pallas_call | solution.py:595
  48.7 0.0 copy-start.18
  48.7 1.0 %copy-done.18 = bf16[2,4,256,256]{3,2,1,0:T(8,128)(2,1)} copy-done((bf16[2,4,256,256]{3,2,1,0:T(8,128)(2,1)}, bf16[2,4,256,256]{3,2,1,0:T(8,128)(2,1)S(1)}, u32[]{:S(2)}) %copy-start.18) | copy-done | bytes 1048600
  49.7 5.1 %all-to-all-start.1 = ((bf16[16,176,128]{2,1,0:T(8,128)(2,1)}), bf16[16,176,128]{2,1,0:T(8,128)(2,1)S(1)}, u32[]{:S(2)}, u32[]{:S(2)}) async-start(bf16[16,176,128]{2,1,0:T(8,128)(2,1)} %get-tuple-element.13), calls=%async_computation.1 | async-start | bytes 1441792 | tf_op jit(solution)/shard_map/all_to_all | solution.py:482
  54.8 0.0 copy-start.9
  54.8 0.9 %copy-done.9 = f32[256,128]{1,0:T(8,128)S(1)} copy-done((f32[256,128]{1,0:T(8,128)S(1)}, f32[256,128]{1,0:T(8,128)}, u32[]{:S(2)}) %copy-start.9) | copy-done | bytes 131096
  55.7 0.9 %copy-done.12 = bf16[256,256]{1,0:T(8,128)(2,1)S(1)} copy-done((bf16[256,256]{1,0:T(8,128)(2,1)S(1)}, bf16[256,256]{1,0:T(8,128)(2,1)}, u32[]{:S(2)}) %copy-start.12) | copy-done | bytes 131096
  56.6 0.9 %copy-done.15 = bf16[256,256]{1,0:T(8,128)(2,1)S(1)} copy-done((bf16[256,256]{1,0:T(8,128)(2,1)S(1)}, bf16[256,256]{1,0:T(8,128)(2,1)}, u32[]{:S(2)}) %copy-start.15) | copy-done | bytes 131096
  57.5 1.2 %copy-done.19 = bf16[2,4,256,256]{3,2,1,0:T(8,128)(2,1)S(1)} copy-done((bf16[2,4,256,256]{3,2,1,0:T(8,128)(2,1)S(1)}, bf16[2,4,256,256]{3,2,1,0:T(8,128)(2,1)}, u32[]{:S(2)}) %copy-start.19) | copy-done | bytes 1048600
  58.7 1.9 %lagged.1 = f32[2,64,2048]{2,1,0:T(8,128)} custom-call(bf16[2,4,256,256]{3,2,1,0:T(8,128)(2,1)S(1)} %copy-done.19, bf16[512,256]{1,0:T(8,128)(2,1)S(1)} %copy-done.4, bf16[256,512]{1,0:T(8,128)(2,1)S(1)} %copy-done.3, bf16[256,256]{1,0:T(8,128)(2,1)S(1)} %copy-done.15, bf16[256,256]{1,0:T(8,128)(2,1)S(1)} %copy-done.12, f32[256,128]{1,0:T(8,128)S(1)} %copy-done.9, ...), custom_call_target="tpu_custom_call" | custom-call | flops 10000000000 | bytes 30000000 | tf_op jit(solution)/shard_map/lagged/pallas_call | solution.py:614
  60.7 11.8 %all-to-all-done.1.packed = bf16[16,176,128]{2,1,0:T(8,128)(2,1)S(1)} async-done(((bf16[16,176,128]{2,1,0:T(8,128)(2,1)}), bf16[16,176,128]{2,1,0:T(8,128)(2,1)S(1)}, u32[]{:S(2)}, u32[]{:S(2)}) %all-to-all-start.1) | async-done | bytes 720928 | tf_op jit(solution)/shard_map/all_to_all | solution.py:482
  72.5 1.2 %unpack.1 = (bf16[128,1024]{1,0:T(8,128)(2,1)}, f32[64,3072]{1,0:T(8,128)}, f32[3,3072]{1,0:T(4,128)}) custom-call(bf16[16,176,128]{2,1,0:T(8,128)(2,1)S(1)} %all-to-all-done.1.packed), custom_call_target="tpu_custom_call" | custom-call | tf_op jit(solution)/shard_map/unpack/pallas_call | solution.py:624
  (11 shorter events, 0.0 us)
Async XLA Ops:
  0.6 11.6 %copy-start.21 = (s32[8]{0:T(128)S(1)}, s32[8]{0:T(128)}, u32[]{:S(2)}) copy-start(s32[8]{0:T(128)} %offsets.1) | copy-start | bytes 100
  0.6 1.0 %copy-start.2 = (bf16[64,3072]{1,0:T(8,128)(2,1)S(1)}, bf16[64,3072]{1,0:T(8,128)(2,1)}, u32[]{:S(2)}) copy-start(bf16[64,3072]{1,0:T(8,128)(2,1)} %w_in_far.1) | copy-start | bytes 1179652
  1.6 0.9 %copy-start.5 = (bf16[128,1024]{1,0:T(8,128)(2,1)S(1)}, bf16[128,1024]{1,0:T(8,128)(2,1)}, u32[]{:S(2)}) copy-start(bf16[128,1024]{1,0:T(8,128)(2,1)} %cotangent_far.1) | copy-start | bytes 786436
  2.6 0.7 copy-start.16
  3.3 8.8 %copy-start.22 = (f32[3,3072]{1,0:T(4,128)S(1)}, f32[3,3072]{1,0:T(4,128)}, u32[]{:S(2)}) copy-start(f32[3,3072]{1,0:T(4,128)} %param.17) | copy-start | bytes 110596
  3.3 9.0 %copy-start.3 = (bf16[256,512]{1,0:T(8,128)(2,1)S(1)}, bf16[256,512]{1,0:T(8,128)(2,1)}, u32[]{:S(2)}) copy-start(bf16[256,512]{1,0:T(8,128)(2,1)} %constant.23.clone.rest_1_.refs_5_) | copy-start | bytes 786436
  3.3 9.0 %copy-start.4 = (bf16[512,256]{1,0:T(8,128)(2,1)S(1)}, bf16[512,256]{1,0:T(8,128)(2,1)}, u32[]{:S(2)}) copy-start(bf16[512,256]{1,0:T(8,128)(2,1)} %constant.22.clone.rest_0_.refs_4_) | copy-start | bytes 786436
  3.3 9.0 %copy-start.6 = (f32[256,128]{1,0:T(8,128)S(1)}, f32[256,128]{1,0:T(8,128)}, u32[]{:S(2)}) copy-start(f32[256,128]{1,0:T(8,128)} %constant.27.clone.rest_5_.refs_9_) | copy-start | bytes 393220
  4.6 25.1 %all-to-all-start = ((bf16[16,176,128]{2,1,0:T(8,128)(2,1)}), bf16[16,176,128]{2,1,0:T(8,128)(2,1)S(1)}, u32[]{:S(2)}, u32[]{:S(2)}) async-start(bf16[16,176,128]{2,1,0:T(8,128)(2,1)} %pack.1), calls=%async_computation | async-start | bytes 1441792 | tf_op jit(solution)/shard_map/all_to_all | solution.py:482
  12.3 0.9 %copy-start.7 = (f32[256,128]{1,0:T(8,128)S(1)}, f32[256,128]{1,0:T(8,128)}, u32[]{:S(2)}) copy-start(f32[256,128]{1,0:T(8,128)} %constant.26.clone.rest_4_.refs_8_) | copy-start | bytes 393220
  13.2 0.9 %copy-start.10 = (bf16[256,256]{1,0:T(8,128)(2,1)S(1)}, bf16[256,256]{1,0:T(8,128)(2,1)}, u32[]{:S(2)}) copy-start(bf16[256,256]{1,0:T(8,128)(2,1)} %constant.25.clone.rest_3_.refs_7_) | copy-start | bytes 393220
  14.1 0.9 %copy-start.13 = (bf16[256,256]{1,0:T(8,128)(2,1)S(1)}, bf16[256,256]{1,0:T(8,128)(2,1)}, u32[]{:S(2)}) copy-start(bf16[256,256]{1,0:T(8,128)(2,1)} %constant.24.clone.rest_2_.refs_6_) | copy-start | bytes 393220
  15.0 1.6 %copy-start.17 = (bf16[1024,1024]{1,0:T(8,128)(2,1)S(1)}, bf16[1024,1024]{1,0:T(8,128)(2,1)}, u32[]{:S(2)}) copy-start(bf16[1024,1024]{1,0:T(8,128)(2,1)} %table.1) | copy-start | bytes 6291460
  16.6 1.0 %copy-start.20 = (bf16[2,64,2048]{2,1,0:T(8,128)(2,1)S(1)}, bf16[2,64,2048]{2,1,0:T(8,128)(2,1)}, u32[]{:S(2)}) copy-start(bf16[2,64,2048]{2,1,0:T(8,128)(2,1)} %filters.1) | copy-start | bytes 1572868
  19.6 1.3 %copy-start = (bf16[1024,1024]{1,0:T(8,128)(2,1)}, bf16[1024,1024]{1,0:T(8,128)(2,1)S(1)}, u32[]{:S(2)}) copy-start(bf16[1024,1024]{1,0:T(8,128)(2,1)S(1)} %get-tuple-element.11.refs_1_) | copy-start | bytes 6291460
  29.8 1.6 %copy-start.1 = (bf16[1024,1024]{1,0:T(8,128)(2,1)S(1)}, bf16[1024,1024]{1,0:T(8,128)(2,1)}, u32[]{:S(2)}) copy-start(bf16[1024,1024]{1,0:T(8,128)(2,1)} %copy-done) | copy-start | bytes 6291460
  31.4 0.9 %copy-start.8 = (f32[256,128]{1,0:T(8,128)S(1)}, f32[256,128]{1,0:T(8,128)}, u32[]{:S(2)}) copy-start(f32[256,128]{1,0:T(8,128)} %constant.26.clone.rest_4_.refs_8_) | copy-start | bytes 393220
  32.3 0.9 %copy-start.11 = (bf16[256,256]{1,0:T(8,128)(2,1)S(1)}, bf16[256,256]{1,0:T(8,128)(2,1)}, u32[]{:S(2)}) copy-start(bf16[256,256]{1,0:T(8,128)(2,1)} %constant.25.clone.rest_3_.refs_7_) | copy-start | bytes 393220
  33.2 0.9 %copy-start.14 = (bf16[256,256]{1,0:T(8,128)(2,1)S(1)}, bf16[256,256]{1,0:T(8,128)(2,1)}, u32[]{:S(2)}) copy-start(bf16[256,256]{1,0:T(8,128)(2,1)} %constant.24.clone.rest_2_.refs_6_) | copy-start | bytes 393220
  48.7 1.0 %copy-start.18 = (bf16[2,4,256,256]{3,2,1,0:T(8,128)(2,1)}, bf16[2,4,256,256]{3,2,1,0:T(8,128)(2,1)S(1)}, u32[]{:S(2)}) copy-start(bf16[2,4,256,256]{3,2,1,0:T(8,128)(2,1)S(1)} %get-tuple-element.17.lagged_spec) | copy-start | bytes 3145732
  49.7 22.8 %all-to-all-start.1 = ((bf16[16,176,128]{2,1,0:T(8,128)(2,1)}), bf16[16,176,128]{2,1,0:T(8,128)(2,1)S(1)}, u32[]{:S(2)}, u32[]{:S(2)}) async-start(bf16[16,176,128]{2,1,0:T(8,128)(2,1)} %get-tuple-element.13), calls=%async_computation.1 | async-start | bytes 1441792 | tf_op jit(solution)/shard_map/all_to_all | solution.py:482
  54.8 0.9 %copy-start.9 = (f32[256,128]{1,0:T(8,128)S(1)}, f32[256,128]{1,0:T(8,128)}, u32[]{:S(2)}) copy-start(f32[256,128]{1,0:T(8,128)} %constant.26.clone.rest_4_.refs_8_) | copy-start | bytes 393220
  55.7 0.9 %copy-start.12 = (bf16[256,256]{1,0:T(8,128)(2,1)S(1)}, bf16[256,256]{1,0:T(8,128)(2,1)}, u32[]{:S(2)}) copy-start(bf16[256,256]{1,0:T(8,128)(2,1)} %constant.25.clone.rest_3_.refs_7_) | copy-start | bytes 393220
  56.6 0.9 %copy-start.15 = (bf16[256,256]{1,0:T(8,128)(2,1)S(1)}, bf16[256,256]{1,0:T(8,128)(2,1)}, u32[]{:S(2)}) copy-start(bf16[256,256]{1,0:T(8,128)(2,1)} %constant.24.clone.rest_2_.refs_6_) | copy-start | bytes 393220
  57.5 1.2 %copy-start.19 = (bf16[2,4,256,256]{3,2,1,0:T(8,128)(2,1)S(1)}, bf16[2,4,256,256]{3,2,1,0:T(8,128)(2,1)}, u32[]{:S(2)}) copy-start(bf16[2,4,256,256]{3,2,1,0:T(8,128)(2,1)} %copy-done.18) | copy-start | bytes 3145732

commit v4 on v3

--- a/solution.py
+++ b/solution.py
@@ -1,4 +1,5 @@
 import functools
+import math
 
 
 import jax
@@ -14,6 +15,8 @@
 BF16 = jnp.bfloat16
 LANES = 128
 GROUP = 16
+PACK_MB = 62
+MIX_MB = 61.5
 
 
 def widen(array):
@@ -116,7 +119,7 @@
 
 def batches(chans):
     groups = chans // GROUP
-    size = 2 if groups % 2 == 0 else 1
+    size = math.gcd(groups, 4)
     return [range(start, start + size) for start in range(0, groups, size)]
 
 
@@ -130,19 +133,18 @@
 
 def one_hot(ids, codes):
     fields, lanes = ids.shape
-    code = lax.broadcasted_iota(jnp.int32, (codes, lanes), 0).astype(F32)
+    code = lax.broadcasted_iota(jnp.int32, (codes, lanes), 0).astype(F32).astype(BF16)
+    one, zero = jnp.ones((codes, lanes), BF16), jnp.zeros((codes, lanes), BF16)
     return jnp.concatenate(
-        [
-            jnp.where(code == ids[field : field + 1], 1.0, 0.0).astype(BF16)
-            for field in range(fields)
-        ],
+        [jnp.where(code == ids[field : field + 1], one, zero) for field in range(fields)],
         axis=0,
     )
 
 
-def prepare_kernel(offsets, filters, table, *rest):
+def prepare_kernel(offsets, filters, table, short_taps, *rest):
     tables = rest[:6]
-    spectra, entries = rest[6:]
+    spectra, entries, taps = rest[6:]
+    taps[...] = jnp.broadcast_to(short_taps[...], taps.shape)
     chans, steps = filters.shape[1:]
     blocks = steps // LANES
     fields = offsets.shape[0]
@@ -179,7 +181,7 @@
 
 def packed_parts(rows):
     half = rows // 2
-    marks = [0, rows, rows + half, 2 * rows + half, 2 * rows + half + 16]
+    marks = [0, rows, rows + half, 2 * rows + half, 2 * rows + half + 8]
     return [slice(low, high) for low, high in zip(marks[:-1], marks[1:])]
 
 
@@ -194,9 +196,7 @@
     ]
     for copy in arrivals:
         copy.start()
-    fields, steps = token_ids.shape
-    ids = jnp.concatenate([widen(token_ids[...]), jnp.zeros((16 - fields, steps), F32)], axis=0)
-    ids = ids.astype(BF16)
+    ids = widen(token_ids[...]).astype(BF16)
     for copy in arrivals:
         copy.wait()
     departures = []
@@ -257,8 +257,6 @@
         mixer_out[:, pair * LANES : (pair + 1) * LANES] = both.T.astype(BF16)
         low = widen(packed[even, part_taps, :])
         high = widen(packed[odd, part_taps, :])
-        low = low[:8] + low[8:]
-        high = high[:8] + high[8:]
         zero, one = merged(low, high)
         tap_grads[:, lanes[0]] = zero[:3]
         tap_grads[:, lanes[1]] = one[:3]
@@ -271,7 +269,6 @@
         chans = refs[0].shape[0] // arrived.shape[0]
         part_two, part_one, part_time, part_small = packed_parts(chans)
         width = refs[0].shape[1]
-        fields = refs[0].shape[0] // LANES
         two = widen(flat(arrived[:, part_two, :]))
         one = widen(arrived[:, part_one, :])
         one_turned = pltpu.roll(flat(one), LANES // 2, 1).reshape(one.shape)
@@ -280,7 +277,7 @@
         cotangent = arrived.at[:, part_time, :]
 
         def ids_of(block):
-            return widen(arrived[block, part_small, :])[:fields]
+            return arrived[block, part_small, :]
 
     else:
         w_cols, ids, cotangent = refs[0][...], refs[1], refs[2]
@@ -288,7 +285,7 @@
         chans = cotangent.shape[1]
 
         def ids_of(block):
-            return widen(ids[block])
+            return ids[block]
 
     far, refs = refs[:9], refs[9:]
     lagged_far, refs = refs[0], refs[1:]
@@ -376,9 +373,6 @@
                 (upstream * second_conv).astype(BF16)
             )
             series.append((upstream * gate).astype(BF16))
-        if packed_form:
-            rows = pl.ds(part_time.start + batch[0] * GROUP, len(batch) * GROUP)
-            depart(sent.at[:, rows, :], sent_far.at[:, rows, :])
         grad_spec = forward(series, tables)
         turned = []
         for place, group in enumerate(batch):
@@ -440,14 +434,10 @@
         + [space] * 2,
         axis=0,
     )
-    high = rounded(total)
-    small = jnp.concatenate([high, total - high], axis=0).astype(BF16)
     for block in range(blocks):
-        sent[block, part_small, :] = small
-    depart(sent.at[:, part_small, :], sent_far.at[:, part_small, :])
+        sent[block, part_small, :] = total.astype(BF16)
     two = weights[: 2 * chans].T
     sent[:, part_two, :] = two.astype(BF16).reshape(blocks, chans, LANES)
-    depart(sent.at[:, part_two, :], sent_far.at[:, part_two, :])
     one = jnp.concatenate([weights[2 * chans :], jnp.zeros((LANES - chans, width), F32)], axis=0).T
     one = one.reshape(blocks, chans, LANES)
     half = chans // 2
@@ -455,7 +445,7 @@
     one = flat(one[:, :half])
     one = jnp.where(lax.broadcasted_iota(jnp.int32, one.shape, 1) < LANES // 2, one, turned)
     sent[:, part_one, :] = one.astype(BF16).reshape(blocks, half, LANES)
-    depart(sent.at[:, part_one, :], sent_far.at[:, part_one, :])
+    depart(sent, sent_far)
     for copy in departures:
         copy.wait()
 
@@ -486,7 +476,7 @@
     return pl.pallas_call(
         kernel,
         name=name,
-        compiler_params=pltpu.CompilerParams(vmem_limit_bytes=megabytes * 1024 * 1024),
+        compiler_params=pltpu.CompilerParams(vmem_limit_bytes=int(megabytes * 1024 * 1024)),
         **settings,
     )
 
@@ -535,7 +525,7 @@
     steps = tok_rows * peers
     groups = chans // GROUP
     tables = transform_tables(peers)
-    packed_form = 2 * chans == LANES and rows == chans and fields <= 8
+    packed_form = 2 * chans == LANES and rows == chans and fields == 8
     spec = (2, groups, peers * GROUP, 2 * LANES)
     moved = (peers, chans, LANES)
     wide = (peers, 3 * chans, LANES)
@@ -548,7 +538,7 @@
         sent = call(
             pack_kernel,
             "pack",
-            16,
+            PACK_MB,
             in_specs=[near, far, far],
             out_specs=far,
             out_shape=packed,
@@ -563,20 +553,22 @@
     else:
         arrived = send_inputs(token_ids, w_in, cotangent, peers)
 
-    filter_spec, entries = call(
+    taps = short_taps.reshape(3, 3, peers, chans)
+    taps = lax.dynamic_index_in_dim(taps, lax.axis_index("tm"), axis=2, keepdims=False)
+    filter_spec, entries, taps = call(
         prepare_kernel,
         "prepare",
         32,
-        in_specs=[pl.BlockSpec(memory_space=pltpu.SMEM)] + [near] * 8,
-        out_shape=(shape(spec, F32), shape(embed_table.shape, BF16)),
+        in_specs=[pl.BlockSpec(memory_space=pltpu.SMEM)] + [near] * 9,
+        out_shape=(
+            shape(spec, F32),
+            shape(embed_table.shape, BF16),
+            shape((3, 3 * chans, LANES), F32),
+        ),
         cost_estimate=pl.CostEstimate(
             flops=10**10, bytes_accessed=3 * 10**7, transcendentals=0
         ),
-    )(field_offsets, filters, embed_table, *tables)
-    taps = short_taps.reshape(3, 3, peers, chans)
-    taps = lax.dynamic_index_in_dim(taps, lax.axis_index("tm"), axis=2, keepdims=False)
-    taps = jnp.broadcast_to(taps.reshape(3, 3 * chans, 1), (3, 3 * chans, LANES))
-
+    )(field_offsets, filters, embed_table, taps.reshape(3, 3 * chans, 1), *tables)
     if packed_form:
         out_shape = (shape(spec, BF16), packed)
         out_specs = (far, far)
@@ -591,17 +583,16 @@
         out_specs = (far, near, near, near)
         scratch_shapes = []
     operands = (entries, taps, filter_spec) + tables
-    hot_bytes = 2 * embed_table.shape[0] * steps
     results = call(
         functools.partial(mixer_kernel, packed_form),
         "mixer",
-        20 + 2 * hot_bytes // 2**20,
+        MIX_MB,
         in_specs=[near] * len(arrived) + [far] * len(operands),
         out_shape=out_shape,
         out_specs=out_specs,
         scratch_shapes=[pltpu.VMEM(operand.shape, operand.dtype) for operand in operands]
         + [
-            pltpu.SemaphoreType.DMA((len(operands) + 2 * groups + 3,)),
+            pltpu.SemaphoreType.DMA((len(operands) + groups + 1,)),
             pltpu.VMEM(spec, BF16),
             pltpu.VMEM((embed_table.shape[0], steps), BF16),
             pltpu.VMEM(wide, BF16),

time: 74.4 us -> 65.7 us (0.88)
  local copies, waits for them, and re-layouts: 18.9 us -> 7.47 us
  waiting for transfers between devices: 20.5 us -> 23.6 us
    unnamed x46 -> x42, local copies, waits for them, and re-layouts: 18.5 us -> 7.07 us
    all_to_all x2, waiting for transfers between devices: 20.5 us -> 23.6 us  [exchange(): return lax.all_to_all(blocks, 'tm', split_axis=0, concat_axis=0, tiled=True)]
  transfers between devices with their start and end apart: 2 -> 2, of which waited for: 2 -> 2; matrix products, arithmetic and copies ran while one was open for 0% -> 1% of each run, Pallas kernels for 5% -> 6%
where the time goes in v4:
time: 65.7 us; the launch traced here: 65.3 us
  waiting for transfers between devices  23.6 us (36%)
  Pallas kernels  21 us (32%)
  starting transfers between devices  12.4 us (19%)
  local copies, waits for them, and re-layouts  7.47 us (11%)
  between operations  0.92 us (1%)
    all_to_all x2, waiting for transfers between devices, exchange(): return lax.all_to_all(blocks, 'tm', split_axis=0, concat_axis=0, tiled=True)  23.6 us
    pallas_call x1, Pallas kernels, local(): call(functools.partial(mixer_kernel, packed_form), 'mixer', MIX_MB, in_sp...  12.8 us
    all_to_all x2, starting transfers between devices, exchange(): return lax.all_to_all(blocks, 'tm', split_axis=0, concat_axis=0, tiled=True)  12.4 us
    unnamed x42, local copies, waits for them, and re-layouts  7.07 us
    pallas_call x1, Pallas kernels, local(): call(pack_kernel, 'pack', PACK_MB, in_specs=[near, far, far], out_specs=f...  2.97 us
    pallas_call x1, Pallas kernels, local(): call(prepare_kernel, 'prepare', 32, in_specs=[pl.BlockSpec(memory_space=p...  2.04 us
    pallas_call x1, Pallas kernels, local(): call(lagged_kernel, 'lagged', 24, out_shape=shape((2, chans, steps), F32)...  1.92 us
  transfers between devices with their start and end apart: 2, of which 2 were waited for; matrix products, arithmetic and copies ran while one was open for 1% of the time, Pallas kernels for 6%

profile of v4, /device:TPU:0, one launch (start us, length us, event | category | flops | bytes accessed | tf_op | source)
XLA Modules:
  0.0 65.3 jit_solution(8915238343203059765)
XLA Ops:
  0.6 0.0 copy-start.7
  0.6 0.0 copy-start.9
  0.7 0.0 copy-start.11
  0.7 0.0 copy-start.13
  0.7 0.0 copy-start.3
  0.7 0.0 copy-start.5
  0.7 0.0 copy-start.20
  0.7 0.0 copy-start.17
  0.7 0.0 copy-start.18
  0.7 3.0 %pack.1 = bf16[16,168,128]{2,1,0:T(8,128)(2,1)} custom-call(s32[8,128]{1,0:T(8,128)} %bitcast.1, bf16[64,3072]{1,0:T(8,128)(2,1)} %w_in_far.1, bf16[128,1024]{1,0:T(8,128)(2,1)} %cotangent_far.1), custom_call_target="tpu_custom_call" | custom-call | tf_op jit(solution)/shard_map/pack/pallas_call | solution.py:538
  3.7 7.4 %all-to-all-start = ((bf16[16,168,128]{2,1,0:T(8,128)(2,1)}), bf16[16,168,128]{2,1,0:T(8,128)(2,1)S(1)}, u32[]{:S(2)}, u32[]{:S(2)}) async-start(bf16[16,168,128]{2,1,0:T(8,128)(2,1)} %pack.1), calls=%async_computation | async-start | bytes 1376256 | tf_op jit(solution)/shard_map/all_to_all | solution.py:472
  11.1 0.0 copy-done.20
  11.1 0.1 reshape.15
  11.3 0.3 reshape.19.short_taps
  11.5 0.0 copy-done.7
  11.6 0.0 copy-done.9
  11.6 0.0 copy-done.11
  11.6 0.0 copy-done.13
  11.6 0.0 copy-done.3
  11.6 0.0 copy-done.5
  11.6 0.0 copy-done.17
  11.6 0.0 copy-done.18
  11.6 0.0 copy-start.15
  11.6 1.6 %copy-done.15 = bf16[1024,1024]{1,0:T(8,128)(2,1)S(1)} copy-done((bf16[1024,1024]{1,0:T(8,128)(2,1)S(1)}, bf16[1024,1024]{1,0:T(8,128)(2,1)}, u32[]{:S(2)}) %copy-start.15) | copy-done | bytes 2097176
  13.2 2.0 %prepare.1 = (f32[2,4,256,256]{3,2,1,0:T(8,128)S(1)}, bf16[1024,1024]{1,0:T(8,128)(2,1)S(1)}, f32[3,192,128]{2,1,0:T(8,128)S(1)}) custom-call(s32[8]{0:T(128)S(1)} %copy-done.18, bf16[2,64,2048]{2,1,0:T(8,128)(2,1)S(1)} %copy-done.17, bf16[1024,1024]{1,0:T(8,128)(2,1)S(1)} %copy-done.15, f32[3,192,1]{2,1,0:T(8,128)S(1)} %reshape.19.short_taps, ...), custom_call_target="tpu_custom_call" | custom-call | flops 10000000000 | bytes 30000000 | tf_op jit(solution)/shard_map/prepare/pallas_call | solution.py:558
  15.3 0.0 copy-start
  15.3 1.3 %copy-done = f32[2,4,256,256]{3,2,1,0:T(8,128)} copy-done((f32[2,4,256,256]{3,2,1,0:T(8,128)}, f32[2,4,256,256]{3,2,1,0:T(8,128)S(1)}, u32[]{:S(2)}) %copy-start) | copy-done | bytes 2097176
  16.6 0.0 copy-start.1
  16.6 1.3 %copy-done.1 = bf16[1024,1024]{1,0:T(8,128)(2,1)} copy-done((bf16[1024,1024]{1,0:T(8,128)(2,1)}, bf16[1024,1024]{1,0:T(8,128)(2,1)S(1)}, u32[]{:S(2)}) %copy-start.1) | copy-done | bytes 2097176
  17.9 0.0 copy-start.2
  17.9 0.7 %copy-done.2 = f32[3,192,128]{2,1,0:T(8,128)} copy-done((f32[3,192,128]{2,1,0:T(8,128)}, f32[3,192,128]{2,1,0:T(8,128)S(1)}, u32[]{:S(2)}) %copy-start.2) | copy-done | bytes 294936
  18.6 9.6 %all-to-all-done.refs_0_ = bf16[16,168,128]{2,1,0:T(8,128)(2,1)S(1)} async-done(((bf16[16,168,128]{2,1,0:T(8,128)(2,1)}), bf16[16,168,128]{2,1,0:T(8,128)(2,1)S(1)}, u32[]{:S(2)}, u32[]{:S(2)}) %all-to-all-start) | async-done | bytes 688160 | tf_op jit(solution)/shard_map/all_to_all | solution.py:472
  28.3 0.8 %copy-done.19 = bf16[16,168,128]{2,1,0:T(8,128)(2,1)} copy-done((bf16[16,168,128]{2,1,0:T(8,128)(2,1)}, bf16[16,168,128]{2,1,0:T(8,128)(2,1)S(1)}, u32[]{:S(2)}) %copy-start.19) | copy-done | bytes 688152
  29.1 0.0 copy-start.12
  29.1 0.0 copy-start.14
  29.1 12.8 %mixer.1 = (bf16[2,4,256,256]{3,2,1,0:T(8,128)(2,1)}, bf16[16,168,128]{2,1,0:T(8,128)(2,1)}) custom-call(bf16[16,168,128]{2,1,0:T(8,128)(2,1)} %copy-done.19, bf16[1024,1024]{1,0:T(8,128)(2,1)} %copy-done.1, f32[3,192,128]{2,1,0:T(8,128)} %copy-done.2, f32[2,4,256,256]{3,2,1,0:T(8,128)} %copy-done, bf16[512,256]{1,0:T(8,128)(2,1)} %constant.22.clone.rest_0_.refs_4_, ...), custom_call_target="tpu_custom_call" | custom-call | tf_op jit(solution)/shard_map/mixer/pallas_call | solution.py:586
  42.0 5.0 %all-to-all-start.1 = ((bf16[16,168,128]{2,1,0:T(8,128)(2,1)}), bf16[16,168,128]{2,1,0:T(8,128)(2,1)S(1)}, u32[]{:S(2)}, u32[]{:S(2)}) async-start(bf16[16,168,128]{2,1,0:T(8,128)(2,1)} %get-tuple-element.15), calls=%async_computation.1 | async-start | bytes 1376256 | tf_op jit(solution)/shard_map/all_to_all | solution.py:472
  46.9 0.0 copy-done.4
  46.9 0.0 copy-done.6
  46.9 0.0 copy-done.8
  47.0 0.0 copy-done.10
  47.0 0.0 copy-done.12
  47.0 0.0 copy-done.14
  47.0 0.0 copy-start.16
  47.0 1.2 %copy-done.16 = bf16[2,4,256,256]{3,2,1,0:T(8,128)(2,1)S(1)} copy-done((bf16[2,4,256,256]{3,2,1,0:T(8,128)(2,1)S(1)}, bf16[2,4,256,256]{3,2,1,0:T(8,128)(2,1)}, u32[]{:S(2)}) %copy-start.16) | copy-done | bytes 1048600
  48.2 1.9 %lagged.1 = f32[2,64,2048]{2,1,0:T(8,128)} custom-call(bf16[2,4,256,256]{3,2,1,0:T(8,128)(2,1)S(1)} %copy-done.16, bf16[512,256]{1,0:T(8,128)(2,1)S(1)} %copy-done.6, bf16[256,512]{1,0:T(8,128)(2,1)S(1)} %copy-done.4, bf16[256,256]{1,0:T(8,128)(2,1)S(1)} %copy-done.14, bf16[256,256]{1,0:T(8,128)(2,1)S(1)} %copy-done.12, f32[256,128]{1,0:T(8,128)S(1)} %copy-done.10, ...), custom_call_target="tpu_custom_call" | custom-call | flops 10000000000 | bytes 30000000 | tf_op jit(solution)/shard_map/lagged/pallas_call | solution.py:605
  50.1 13.9 %all-to-all-done.1.packed = bf16[16,168,128]{2,1,0:T(8,128)(2,1)S(1)} async-done(((bf16[16,168,128]{2,1,0:T(8,128)(2,1)}), bf16[16,168,128]{2,1,0:T(8,128)(2,1)S(1)}, u32[]{:S(2)}, u32[]{:S(2)}) %all-to-all-start.1) | async-done | bytes 688160 | tf_op jit(solution)/shard_map/all_to_all | solution.py:472
  64.1 1.2 %unpack.1 = (bf16[128,1024]{1,0:T(8,128)(2,1)}, f32[64,3072]{1,0:T(8,128)}, f32[3,3072]{1,0:T(4,128)}) custom-call(bf16[16,168,128]{2,1,0:T(8,128)(2,1)S(1)} %all-to-all-done.1.packed), custom_call_target="tpu_custom_call" | custom-call | tf_op jit(solution)/shard_map/unpack/pallas_call | solution.py:615
  (6 shorter events, 0.0 us)
Async XLA Ops:
  0.6 10.9 %copy-start.7 = (f32[256,128]{1,0:T(8,128)S(1)}, f32[256,128]{1,0:T(8,128)}, u32[]{:S(2)}) copy-start(f32[256,128]{1,0:T(8,128)} %constant.27.clone.rest_5_.refs_9_) | copy-start | bytes 393220
  0.6 10.9 %copy-start.9 = (f32[256,128]{1,0:T(8,128)S(1)}, f32[256,128]{1,0:T(8,128)}, u32[]{:S(2)}) copy-start(f32[256,128]{1,0:T(8,128)} %constant.26.clone.rest_4_.refs_8_) | copy-start | bytes 393220
  0.7 10.9 %copy-start.11 = (bf16[256,256]{1,0:T(8,128)(2,1)S(1)}, bf16[256,256]{1,0:T(8,128)(2,1)}, u32[]{:S(2)}) copy-start(bf16[256,256]{1,0:T(8,128)(2,1)} %constant.25.clone.rest_3_.refs_7_) | copy-start | bytes 393220
  0.7 10.9 %copy-start.13 = (bf16[256,256]{1,0:T(8,128)(2,1)S(1)}, bf16[256,256]{1,0:T(8,128)(2,1)}, u32[]{:S(2)}) copy-start(bf16[256,256]{1,0:T(8,128)(2,1)} %constant.24.clone.rest_2_.refs_6_) | copy-start | bytes 393220
  0.7 10.9 %copy-start.3 = (bf16[256,512]{1,0:T(8,128)(2,1)S(1)}, bf16[256,512]{1,0:T(8,128)(2,1)}, u32[]{:S(2)}) copy-start(bf16[256,512]{1,0:T(8,128)(2,1)} %constant.23.clone.rest_1_.refs_5_) | copy-start | bytes 786436
  0.7 10.9 %copy-start.5 = (bf16[512,256]{1,0:T(8,128)(2,1)S(1)}, bf16[512,256]{1,0:T(8,128)(2,1)}, u32[]{:S(2)}) copy-start(bf16[512,256]{1,0:T(8,128)(2,1)} %constant.22.clone.rest_0_.refs_4_) | copy-start | bytes 786436
  0.7 10.4 %copy-start.20 = (f32[3,3072]{1,0:T(4,128)S(1)}, f32[3,3072]{1,0:T(4,128)}, u32[]{:S(2)}) copy-start(f32[3,3072]{1,0:T(4,128)} %param.17) | copy-start | bytes 110596
  0.7 10.9 %copy-start.17 = (bf16[2,64,2048]{2,1,0:T(8,128)(2,1)S(1)}, bf16[2,64,2048]{2,1,0:T(8,128)(2,1)}, u32[]{:S(2)}) copy-start(bf16[2,64,2048]{2,1,0:T(8,128)(2,1)} %filters.1) | copy-start | bytes 1572868
  0.7 10.9 %copy-start.18 = (s32[8]{0:T(128)S(1)}, s32[8]{0:T(128)}, u32[]{:S(2)}) copy-start(s32[8]{0:T(128)} %offsets.1) | copy-start | bytes 100
  3.7 24.5 %all-to-all-start = ((bf16[16,168,128]{2,1,0:T(8,128)(2,1)}), bf16[16,168,128]{2,1,0:T(8,128)(2,1)S(1)}, u32[]{:S(2)}, u32[]{:S(2)}) async-start(bf16[16,168,128]{2,1,0:T(8,128)(2,1)} %pack.1), calls=%async_computation | async-start | bytes 1376256 | tf_op jit(solution)/shard_map/all_to_all | solution.py:472
  11.6 1.6 %copy-start.15 = (bf16[1024,1024]{1,0:T(8,128)(2,1)S(1)}, bf16[1024,1024]{1,0:T(8,128)(2,1)}, u32[]{:S(2)}) copy-start(bf16[1024,1024]{1,0:T(8,128)(2,1)} %table.1) | copy-start | bytes 6291460
  15.3 1.3 %copy-start = (f32[2,4,256,256]{3,2,1,0:T(8,128)}, f32[2,4,256,256]{3,2,1,0:T(8,128)S(1)}, u32[]{:S(2)}) copy-start(f32[2,4,256,256]{3,2,1,0:T(8,128)S(1)} %get-tuple-element.14.refs_3_) | copy-start | bytes 6291460
  16.6 1.3 %copy-start.1 = (bf16[1024,1024]{1,0:T(8,128)(2,1)}, bf16[1024,1024]{1,0:T(8,128)(2,1)S(1)}, u32[]{:S(2)}) copy-start(bf16[1024,1024]{1,0:T(8,128)(2,1)S(1)} %get-tuple-element.12.refs_1_) | copy-start | bytes 6291460
  17.9 0.7 %copy-start.2 = (f32[3,192,128]{2,1,0:T(8,128)}, f32[3,192,128]{2,1,0:T(8,128)S(1)}, u32[]{:S(2)}) copy-start(f32[3,192,128]{2,1,0:T(8,128)S(1)} %get-tuple-element.13.refs_2_) | copy-start | bytes 884740
  28.3 0.8 %copy-start.19 = (bf16[16,168,128]{2,1,0:T(8,128)(2,1)}, bf16[16,168,128]{2,1,0:T(8,128)(2,1)S(1)}, u32[]{:S(2)}) copy-start(bf16[16,168,128]{2,1,0:T(8,128)(2,1)S(1)} %all-to-all-done.refs_0_) | copy-start | bytes 2064388
  29.1 17.8 %copy-start.4 = (bf16[256,512]{1,0:T(8,128)(2,1)S(1)}, bf16[256,512]{1,0:T(8,128)(2,1)}, u32[]{:S(2)}) copy-start(bf16[256,512]{1,0:T(8,128)(2,1)} %constant.23.clone.rest_1_.refs_5_) | copy-start | bytes 786436
  29.1 17.8 %copy-start.6 = (bf16[512,256]{1,0:T(8,128)(2,1)S(1)}, bf16[512,256]{1,0:T(8,128)(2,1)}, u32[]{:S(2)}) copy-start(bf16[512,256]{1,0:T(8,128)(2,1)} %constant.22.clone.rest_0_.refs_4_) | copy-start | bytes 786436
  29.1 17.8 %copy-start.8 = (f32[256,128]{1,0:T(8,128)S(1)}, f32[256,128]{1,0:T(8,128)}, u32[]{:S(2)}) copy-start(f32[256,128]{1,0:T(8,128)} %constant.27.clone.rest_5_.refs_9_) | copy-start | bytes 393220
  29.1 17.9 %copy-start.10 = (f32[256,128]{1,0:T(8,128)S(1)}, f32[256,128]{1,0:T(8,128)}, u32[]{:S(2)}) copy-start(f32[256,128]{1,0:T(8,128)} %constant.26.clone.rest_4_.refs_8_) | copy-start | bytes 393220
  29.1 17.9 %copy-start.12 = (bf16[256,256]{1,0:T(8,128)(2,1)S(1)}, bf16[256,256]{1,0:T(8,128)(2,1)}, u32[]{:S(2)}) copy-start(bf16[256,256]{1,0:T(8,128)(2,1)} %constant.25.clone.rest_3_.refs_7_) | copy-start | bytes 393220
  29.1 17.9 %copy-start.14 = (bf16[256,256]{1,0:T(8,128)(2,1)S(1)}, bf16[256,256]{1,0:T(8,128)(2,1)}, u32[]{:S(2)}) copy-start(bf16[256,256]{1,0:T(8,128)(2,1)} %constant.24.clone.rest_2_.refs_6_) | copy-start | bytes 393220
  42.0 22.1 %all-to-all-start.1 = ((bf16[16,168,128]{2,1,0:T(8,128)(2,1)}), bf16[16,168,128]{2,1,0:T(8,128)(2,1)S(1)}, u32[]{:S(2)}, u32[]{:S(2)}) async-start(bf16[16,168,128]{2,1,0:T(8,128)(2,1)} %get-tuple-element.15), calls=%async_computation.1 | async-start | bytes 1376256 | tf_op jit(solution)/shard_map/all_to_all | solution.py:472
  47.0 1.2 %copy-start.16 = (bf16[2,4,256,256]{3,2,1,0:T(8,128)(2,1)S(1)}, bf16[2,4,256,256]{3,2,1,0:T(8,128)(2,1)}, u32[]{:S(2)}) copy-start(bf16[2,4,256,256]{3,2,1,0:T(8,128)(2,1)} %get-tuple-element.19.lagged_spec) | copy-start | bytes 3145732

commit v5 on v4

--- a/solution.py
+++ b/solution.py
@@ -15,6 +15,7 @@
 BF16 = jnp.bfloat16
 LANES = 128
 GROUP = 16
+QUARTERS = 2
 PACK_MB = 62
 MIX_MB = 61.5
 
@@ -265,15 +266,11 @@
 
 def mixer_kernel(packed_form, *refs):
     if packed_form:
-        arrived, refs = refs[0], refs[1:]
+        arrived_far, refs = refs[0], refs[1:]
+        arrived, refs = refs[-1], refs[:-1]
         chans = refs[0].shape[0] // arrived.shape[0]
         part_two, part_one, part_time, part_small = packed_parts(chans)
         width = refs[0].shape[1]
-        two = widen(flat(arrived[:, part_two, :]))
-        one = widen(arrived[:, part_one, :])
-        one_turned = pltpu.roll(flat(one), LANES // 2, 1).reshape(one.shape)
-        one = flat(jnp.concatenate([one, one_turned], axis=1))
-        w_cols = jnp.concatenate([two, one], axis=1).astype(BF16)
         cotangent = arrived.at[:, part_time, :]
 
         def ids_of(block):
@@ -304,23 +301,46 @@
     codes = LANES
     arrivals = [
         pltpu.make_async_copy(source, target, sems.at[place])
-        for place, (source, target) in enumerate(zip(far, near))
+        for place, (source, target) in enumerate(zip(far[1:], near[1:]))
     ]
+    quarter = entries.shape[0] // QUARTERS
+    quarters = [slice(part * quarter, (part + 1) * quarter) for part in range(QUARTERS)]
+    entry_arrivals = [
+        pltpu.make_async_copy(far[0].at[rows], entries.at[rows], sems.at[len(arrivals) + part])
+        for part, rows in enumerate(quarters)
+    ]
+    taken = len(arrivals) + QUARTERS
+    if packed_form:
+        first = pltpu.make_async_copy(arrived_far, arrived, sems.at[taken])
+        first.start()
+    for copy in entry_arrivals:
+        copy.start()
+    if packed_form:
+        first.wait()
     for copy in arrivals:
         copy.start()
     departures = []
 
     def depart(source, target):
         departures.append(
-            pltpu.make_async_copy(source, target, sems.at[len(arrivals) + len(departures)])
+            pltpu.make_async_copy(source, target, sems.at[taken + 1 + len(departures)])
         )
         departures[-1].start()
 
     for block in range(blocks):
         hot[:, block * LANES : (block + 1) * LANES] = one_hot(ids_of(block), codes)
+    if packed_form:
+        two = widen(flat(arrived[:, part_two, :]))
+        one = widen(arrived[:, part_one, :])
+        one_turned = pltpu.roll(flat(one), LANES // 2, 1).reshape(one.shape)
+        one = flat(jnp.concatenate([one, one_turned], axis=1))
+        w_cols = jnp.concatenate([two, one], axis=1).astype(BF16)
+    coded = []
+    for copy, rows in zip(entry_arrivals, quarters):
+        copy.wait()
+        coded.append(dot(entries[rows], w_cols).T[: 3 * chans].astype(BF16))
+    coded = jnp.concatenate(coded, axis=1)
     arrivals[0].wait()
-    coded = dot(entries[...], w_cols).T[: 3 * chans].astype(BF16)
-    arrivals[1].wait()
     lane = lax.broadcasted_iota(jnp.int32, (3 * chans, LANES), 1)
     last1 = jnp.zeros((3 * chans, LANES), F32)
     last2 = last1
@@ -345,7 +365,7 @@
     def blocked(value):
         return value.reshape(blocks, GROUP, LANES)
 
-    for copy in arrivals[2:]:
+    for copy in arrivals[1:]:
         copy.wait()
     for batch in batches(chans):
         value_spec = forward([column(mixed, group) for group in batch], tables)
@@ -414,8 +434,9 @@
     coded = lax.dot_general(
         grad_proj[...], hot[...], (((1,), (1,)), ((), ())), preferred_element_type=F32
     )
-    weights = dot(coded.astype(BF16), entries[...])
+    coded = coded.astype(BF16)
     if not packed_form:
+        weights = dot(coded, entries[...])
         weight_part[...] = weights.T.astype(BF16)
         for tap in range(3):
             tap_terms[tap] = jnp.sum(sums[tap], axis=1, keepdims=True)
@@ -436,16 +457,21 @@
     )
     for block in range(blocks):
         sent[block, part_small, :] = total.astype(BF16)
-    two = weights[: 2 * chans].T
-    sent[:, part_two, :] = two.astype(BF16).reshape(blocks, chans, LANES)
-    one = jnp.concatenate([weights[2 * chans :], jnp.zeros((LANES - chans, width), F32)], axis=0).T
-    one = one.reshape(blocks, chans, LANES)
     half = chans // 2
-    turned = pltpu.roll(flat(one[:, half:]), LANES // 2, 1)
-    one = flat(one[:, :half])
-    one = jnp.where(lax.broadcasted_iota(jnp.int32, one.shape, 1) < LANES // 2, one, turned)
-    sent[:, part_one, :] = one.astype(BF16).reshape(blocks, half, LANES)
-    depart(sent, sent_far)
+    for columns in quarters:
+        weights = dot(coded, entries[:, columns])
+        some = slice(columns.start // chans, columns.stop // chans)
+        two = weights[: 2 * chans].T
+        sent[some, part_two, :] = two.astype(BF16).reshape(-1, chans, LANES)
+        space = jnp.zeros((LANES - chans, weights.shape[1]), F32)
+        one = jnp.concatenate([weights[2 * chans :], space], axis=0).T
+        one = one.reshape(-1, chans, LANES)
+        turned = pltpu.roll(flat(one[:, half:]), LANES // 2, 1)
+        one = flat(one[:, :half])
+        lane = lax.broadcasted_iota(jnp.int32, one.shape, 1)
+        one = jnp.where(lane < LANES // 2, one, turned)
+        sent[some, part_one, :] = one.astype(BF16).reshape(-1, half, LANES)
+        depart(sent.at[some], sent_far.at[some])
     for copy in departures:
         copy.wait()
 
@@ -572,7 +598,7 @@
     if packed_form:
         out_shape = (shape(spec, BF16), packed)
         out_specs = (far, far)
-        scratch_shapes = [pltpu.VMEM(packed.shape, BF16)]
+        scratch_shapes = [pltpu.VMEM(packed.shape, BF16)] * 2
     else:
         out_shape = (
             shape(spec, BF16),
@@ -587,12 +613,12 @@
         functools.partial(mixer_kernel, packed_form),
         "mixer",
         MIX_MB,
-        in_specs=[near] * len(arrived) + [far] * len(operands),
+        in_specs=[far if packed_form else near] * len(arrived) + [far] * len(operands),
         out_shape=out_shape,
         out_specs=out_specs,
         scratch_shapes=[pltpu.VMEM(operand.shape, operand.dtype) for operand in operands]
         + [
-            pltpu.SemaphoreType.DMA((len(operands) + groups + 1,)),
+            pltpu.SemaphoreType.DMA((len(operands) + groups + 2 * QUARTERS,)),
             pltpu.VMEM(spec, BF16),
             pltpu.VMEM((embed_table.shape[0], steps), BF16),
             pltpu.VMEM(wide, BF16),

time: 65.7 us -> 65 us (0.989)
  Pallas kernels: 21 us -> 20.3 us
    pallas_call x1, Pallas kernels: 12.8 us -> 12.1 us  [local(): call(functools.partial(mixer_kernel, packed_form), 'mixer', MIX_MB, in_sp...]
where the time goes in v5:
time: 65 us; the launch traced here: 64.6 us
  waiting for transfers between devices  23.6 us (36%)
  Pallas kernels  20.3 us (31%)
  starting transfers between devices  12.4 us (19%)
  local copies, waits for them, and re-layouts  7.47 us (11%)
  between operations  0.92 us (1%)
    all_to_all x2, waiting for transfers between devices, exchange(): return lax.all_to_all(blocks, 'tm', split_axis=0, concat_axis=0, tiled=True)  23.6 us
    all_to_all x2, starting transfers between devices, exchange(): return lax.all_to_all(blocks, 'tm', split_axis=0, concat_axis=0, tiled=True)  12.4 us
    pallas_call x1, Pallas kernels, local(): call(functools.partial(mixer_kernel, packed_form), 'mixer', MIX_MB, in_sp...  12.1 us
    unnamed x42, local copies, waits for them, and re-layouts  7.07 us
    pallas_call x1, Pallas kernels, local(): call(pack_kernel, 'pack', PACK_MB, in_specs=[near, far, far], out_specs=f...  2.97 us
    pallas_call x1, Pallas kernels, local(): call(prepare_kernel, 'prepare', 32, in_specs=[pl.BlockSpec(memory_space=p...  2.04 us
    pallas_call x1, Pallas kernels, local(): call(lagged_kernel, 'lagged', 24, out_shape=shape((2, chans, steps), F32)...  1.92 us
  transfers between devices with their start and end apart: 2, of which 2 were waited for; matrix products, arithmetic and copies ran while one was open for 1% of the time, Pallas kernels for 6%

profile of v5, /device:TPU:0, one launch (start us, length us, event | category | flops | bytes accessed | tf_op | source)
XLA Modules:
  0.0 64.6 jit_solution(3517850630940811856)
XLA Ops:
  0.6 0.0 copy-start.7
  0.6 0.0 copy-start.9
  0.7 0.0 copy-start.11
  0.7 0.0 copy-start.13
  0.7 0.0 copy-start.3
  0.7 0.0 copy-start.5
  0.7 0.0 copy-start.20
  0.7 0.0 copy-start.17
  0.7 0.0 copy-start.18
  0.7 3.0 %pack.1 = bf16[16,168,128]{2,1,0:T(8,128)(2,1)} custom-call(s32[8,128]{1,0:T(8,128)} %bitcast.1, bf16[64,3072]{1,0:T(8,128)(2,1)} %w_in_far.1, bf16[128,1024]{1,0:T(8,128)(2,1)} %cotangent_far.1), custom_call_target="tpu_custom_call" | custom-call | tf_op jit(solution)/shard_map/pack/pallas_call | solution.py:564
  3.7 7.4 %all-to-all-start = ((bf16[16,168,128]{2,1,0:T(8,128)(2,1)}), bf16[16,168,128]{2,1,0:T(8,128)(2,1)S(1)}, u32[]{:S(2)}, u32[]{:S(2)}) async-start(bf16[16,168,128]{2,1,0:T(8,128)(2,1)} %pack.1), calls=%async_computation | async-start | bytes 1376256 | tf_op jit(solution)/shard_map/all_to_all | solution.py:498
  11.1 0.0 copy-done.20
  11.1 0.1 reshape.15
  11.3 0.3 reshape.19.short_taps
  11.5 0.0 copy-done.7
  11.6 0.0 copy-done.9
  11.6 0.0 copy-done.11
  11.6 0.0 copy-done.13
  11.6 0.0 copy-done.3
  11.6 0.0 copy-done.5
  11.6 0.0 copy-done.17
  11.6 0.0 copy-done.18
  11.6 0.0 copy-start.15
  11.6 1.6 %copy-done.15 = bf16[1024,1024]{1,0:T(8,128)(2,1)S(1)} copy-done((bf16[1024,1024]{1,0:T(8,128)(2,1)S(1)}, bf16[1024,1024]{1,0:T(8,128)(2,1)}, u32[]{:S(2)}) %copy-start.15) | copy-done | bytes 2097176
  13.2 2.0 %prepare.1 = (f32[2,4,256,256]{3,2,1,0:T(8,128)S(1)}, bf16[1024,1024]{1,0:T(8,128)(2,1)S(1)}, f32[3,192,128]{2,1,0:T(8,128)S(1)}) custom-call(s32[8]{0:T(128)S(1)} %copy-done.18, bf16[2,64,2048]{2,1,0:T(8,128)(2,1)S(1)} %copy-done.17, bf16[1024,1024]{1,0:T(8,128)(2,1)S(1)} %copy-done.15, f32[3,192,1]{2,1,0:T(8,128)S(1)} %reshape.19.short_taps, ...), custom_call_target="tpu_custom_call" | custom-call | flops 10000000000 | bytes 30000000 | tf_op jit(solution)/shard_map/prepare/pallas_call | solution.py:584
  15.3 0.0 copy-start
  15.3 1.3 %copy-done = f32[2,4,256,256]{3,2,1,0:T(8,128)} copy-done((f32[2,4,256,256]{3,2,1,0:T(8,128)}, f32[2,4,256,256]{3,2,1,0:T(8,128)S(1)}, u32[]{:S(2)}) %copy-start) | copy-done | bytes 2097176
  16.6 0.0 copy-start.1
  16.6 1.3 %copy-done.1 = bf16[1024,1024]{1,0:T(8,128)(2,1)} copy-done((bf16[1024,1024]{1,0:T(8,128)(2,1)}, bf16[1024,1024]{1,0:T(8,128)(2,1)S(1)}, u32[]{:S(2)}) %copy-start.1) | copy-done | bytes 2097176
  17.9 0.0 copy-start.2
  17.9 0.7 %copy-done.2 = f32[3,192,128]{2,1,0:T(8,128)} copy-done((f32[3,192,128]{2,1,0:T(8,128)}, f32[3,192,128]{2,1,0:T(8,128)S(1)}, u32[]{:S(2)}) %copy-start.2) | copy-done | bytes 294936
  18.6 9.6 %all-to-all-done.refs_0_ = bf16[16,168,128]{2,1,0:T(8,128)(2,1)S(1)} async-done(((bf16[16,168,128]{2,1,0:T(8,128)(2,1)}), bf16[16,168,128]{2,1,0:T(8,128)(2,1)S(1)}, u32[]{:S(2)}, u32[]{:S(2)}) %all-to-all-start) | async-done | bytes 688160 | tf_op jit(solution)/shard_map/all_to_all | solution.py:498
  28.3 0.8 %copy-done.19 = bf16[16,168,128]{2,1,0:T(8,128)(2,1)} copy-done((bf16[16,168,128]{2,1,0:T(8,128)(2,1)}, bf16[16,168,128]{2,1,0:T(8,128)(2,1)S(1)}, u32[]{:S(2)}) %copy-start.19) | copy-done | bytes 688152
  29.1 0.0 copy-start.12
  29.1 0.0 copy-start.14
  29.1 12.1 %mixer.1 = (bf16[2,4,256,256]{3,2,1,0:T(8,128)(2,1)}, bf16[16,168,128]{2,1,0:T(8,128)(2,1)}) custom-call(bf16[16,168,128]{2,1,0:T(8,128)(2,1)} %copy-done.19, bf16[1024,1024]{1,0:T(8,128)(2,1)} %copy-done.1, f32[3,192,128]{2,1,0:T(8,128)} %copy-done.2, f32[2,4,256,256]{3,2,1,0:T(8,128)} %copy-done, bf16[512,256]{1,0:T(8,128)(2,1)} %constant.22.clone.rest_0_.refs_4_, ...), custom_call_target="tpu_custom_call" | custom-call | tf_op jit(solution)/shard_map/mixer/pallas_call | solution.py:612
  41.3 5.0 %all-to-all-start.1 = ((bf16[16,168,128]{2,1,0:T(8,128)(2,1)}), bf16[16,168,128]{2,1,0:T(8,128)(2,1)S(1)}, u32[]{:S(2)}, u32[]{:S(2)}) async-start(bf16[16,168,128]{2,1,0:T(8,128)(2,1)} %get-tuple-element.15), calls=%async_computation.1 | async-start | bytes 1376256 | tf_op jit(solution)/shard_map/all_to_all | solution.py:498
  46.3 0.0 copy-done.4
  46.3 0.0 copy-done.6
  46.3 0.0 copy-done.8
  46.3 0.0 copy-done.10
  46.3 0.0 copy-done.12
  46.3 0.0 copy-done.14
  46.3 0.0 copy-start.16
  46.3 1.2 %copy-done.16 = bf16[2,4,256,256]{3,2,1,0:T(8,128)(2,1)S(1)} copy-done((bf16[2,4,256,256]{3,2,1,0:T(8,128)(2,1)S(1)}, bf16[2,4,256,256]{3,2,1,0:T(8,128)(2,1)}, u32[]{:S(2)}) %copy-start.16) | copy-done | bytes 1048600
  47.5 1.9 %lagged.1 = f32[2,64,2048]{2,1,0:T(8,128)} custom-call(bf16[2,4,256,256]{3,2,1,0:T(8,128)(2,1)S(1)} %copy-done.16, bf16[512,256]{1,0:T(8,128)(2,1)S(1)} %copy-done.6, bf16[256,512]{1,0:T(8,128)(2,1)S(1)} %copy-done.4, bf16[256,256]{1,0:T(8,128)(2,1)S(1)} %copy-done.14, bf16[256,256]{1,0:T(8,128)(2,1)S(1)} %copy-done.12, f32[256,128]{1,0:T(8,128)S(1)} %copy-done.10, ...), custom_call_target="tpu_custom_call" | custom-call | flops 10000000000 | bytes 30000000 | tf_op jit(solution)/shard_map/lagged/pallas_call | solution.py:631
  49.5 13.9 %all-to-all-done.1.packed = bf16[16,168,128]{2,1,0:T(8,128)(2,1)S(1)} async-done(((bf16[16,168,128]{2,1,0:T(8,128)(2,1)}), bf16[16,168,128]{2,1,0:T(8,128)(2,1)S(1)}, u32[]{:S(2)}, u32[]{:S(2)}) %all-to-all-start.1) | async-done | bytes 688160 | tf_op jit(solution)/shard_map/all_to_all | solution.py:498
  63.4 1.2 %unpack.1 = (bf16[128,1024]{1,0:T(8,128)(2,1)}, f32[64,3072]{1,0:T(8,128)}, f32[3,3072]{1,0:T(4,128)}) custom-call(bf16[16,168,128]{2,1,0:T(8,128)(2,1)S(1)} %all-to-all-done.1.packed), custom_call_target="tpu_custom_call" | custom-call | tf_op jit(solution)/shard_map/unpack/pallas_call | solution.py:641
  (6 shorter events, 0.0 us)
Async XLA Ops:
  0.6 10.9 %copy-start.7 = (f32[256,128]{1,0:T(8,128)S(1)}, f32[256,128]{1,0:T(8,128)}, u32[]{:S(2)}) copy-start(f32[256,128]{1,0:T(8,128)} %constant.27.clone.rest_5_.refs_9_) | copy-start | bytes 393220
  0.6 10.9 %copy-start.9 = (f32[256,128]{1,0:T(8,128)S(1)}, f32[256,128]{1,0:T(8,128)}, u32[]{:S(2)}) copy-start(f32[256,128]{1,0:T(8,128)} %constant.26.clone.rest_4_.refs_8_) | copy-start | bytes 393220
  0.7 10.9 %copy-start.11 = (bf16[256,256]{1,0:T(8,128)(2,1)S(1)}, bf16[256,256]{1,0:T(8,128)(2,1)}, u32[]{:S(2)}) copy-start(bf16[256,256]{1,0:T(8,128)(2,1)} %constant.25.clone.rest_3_.refs_7_) | copy-start | bytes 393220
  0.7 10.9 %copy-start.13 = (bf16[256,256]{1,0:T(8,128)(2,1)S(1)}, bf16[256,256]{1,0:T(8,128)(2,1)}, u32[]{:S(2)}) copy-start(bf16[256,256]{1,0:T(8,128)(2,1)} %constant.24.clone.rest_2_.refs_6_) | copy-start | bytes 393220
  0.7 10.9 %copy-start.3 = (bf16[256,512]{1,0:T(8,128)(2,1)S(1)}, bf16[256,512]{1,0:T(8,128)(2,1)}, u32[]{:S(2)}) copy-start(bf16[256,512]{1,0:T(8,128)(2,1)} %constant.23.clone.rest_1_.refs_5_) | copy-start | bytes 786436
  0.7 10.9 %copy-start.5 = (bf16[512,256]{1,0:T(8,128)(2,1)S(1)}, bf16[512,256]{1,0:T(8,128)(2,1)}, u32[]{:S(2)}) copy-start(bf16[512,256]{1,0:T(8,128)(2,1)} %constant.22.clone.rest_0_.refs_4_) | copy-start | bytes 786436
  0.7 10.4 %copy-start.20 = (f32[3,3072]{1,0:T(4,128)S(1)}, f32[3,3072]{1,0:T(4,128)}, u32[]{:S(2)}) copy-start(f32[3,3072]{1,0:T(4,128)} %param.17) | copy-start | bytes 110596
  0.7 10.9 %copy-start.17 = (bf16[2,64,2048]{2,1,0:T(8,128)(2,1)S(1)}, bf16[2,64,2048]{2,1,0:T(8,128)(2,1)}, u32[]{:S(2)}) copy-start(bf16[2,64,2048]{2,1,0:T(8,128)(2,1)} %filters.1) | copy-start | bytes 1572868
  0.7 10.9 %copy-start.18 = (s32[8]{0:T(128)S(1)}, s32[8]{0:T(128)}, u32[]{:S(2)}) copy-start(s32[8]{0:T(128)} %offsets.1) | copy-start | bytes 100
  3.7 24.5 %all-to-all-start = ((bf16[16,168,128]{2,1,0:T(8,128)(2,1)}), bf16[16,168,128]{2,1,0:T(8,128)(2,1)S(1)}, u32[]{:S(2)}, u32[]{:S(2)}) async-start(bf16[16,168,128]{2,1,0:T(8,128)(2,1)} %pack.1), calls=%async_computation | async-start | bytes 1376256 | tf_op jit(solution)/shard_map/all_to_all | solution.py:498
  11.6 1.6 %copy-start.15 = (bf16[1024,1024]{1,0:T(8,128)(2,1)S(1)}, bf16[1024,1024]{1,0:T(8,128)(2,1)}, u32[]{:S(2)}) copy-start(bf16[1024,1024]{1,0:T(8,128)(2,1)} %table.1) | copy-start | bytes 6291460
  15.3 1.3 %copy-start = (f32[2,4,256,256]{3,2,1,0:T(8,128)}, f32[2,4,256,256]{3,2,1,0:T(8,128)S(1)}, u32[]{:S(2)}) copy-start(f32[2,4,256,256]{3,2,1,0:T(8,128)S(1)} %get-tuple-element.14.refs_3_) | copy-start | bytes 6291460
  16.6 1.3 %copy-start.1 = (bf16[1024,1024]{1,0:T(8,128)(2,1)}, bf16[1024,1024]{1,0:T(8,128)(2,1)S(1)}, u32[]{:S(2)}) copy-start(bf16[1024,1024]{1,0:T(8,128)(2,1)S(1)} %get-tuple-element.12.refs_1_) | copy-start | bytes 6291460
  17.9 0.7 %copy-start.2 = (f32[3,192,128]{2,1,0:T(8,128)}, f32[3,192,128]{2,1,0:T(8,128)S(1)}, u32[]{:S(2)}) copy-start(f32[3,192,128]{2,1,0:T(8,128)S(1)} %get-tuple-element.13.refs_2_) | copy-start | bytes 884740
  28.3 0.8 %copy-start.19 = (bf16[16,168,128]{2,1,0:T(8,128)(2,1)}, bf16[16,168,128]{2,1,0:T(8,128)(2,1)S(1)}, u32[]{:S(2)}) copy-start(bf16[16,168,128]{2,1,0:T(8,128)(2,1)S(1)} %all-to-all-done.refs_0_) | copy-start | bytes 2064388
  29.1 17.2 %copy-start.4 = (bf16[256,512]{1,0:T(8,128)(2,1)S(1)}, bf16[256,512]{1,0:T(8,128)(2,1)}, u32[]{:S(2)}) copy-start(bf16[256,512]{1,0:T(8,128)(2,1)} %constant.23.clone.rest_1_.refs_5_) | copy-start | bytes 786436
  29.1 17.2 %copy-start.6 = (bf16[512,256]{1,0:T(8,128)(2,1)S(1)}, bf16[512,256]{1,0:T(8,128)(2,1)}, u32[]{:S(2)}) copy-start(bf16[512,256]{1,0:T(8,128)(2,1)} %constant.22.clone.rest_0_.refs_4_) | copy-start | bytes 786436
  29.1 17.2 %copy-start.8 = (f32[256,128]{1,0:T(8,128)S(1)}, f32[256,128]{1,0:T(8,128)}, u32[]{:S(2)}) copy-start(f32[256,128]{1,0:T(8,128)} %constant.27.clone.rest_5_.refs_9_) | copy-start | bytes 393220
  29.1 17.2 %copy-start.10 = (f32[256,128]{1,0:T(8,128)S(1)}, f32[256,128]{1,0:T(8,128)}, u32[]{:S(2)}) copy-start(f32[256,128]{1,0:T(8,128)} %constant.26.clone.rest_4_.refs_8_) | copy-start | bytes 393220
  29.1 17.2 %copy-start.12 = (bf16[256,256]{1,0:T(8,128)(2,1)S(1)}, bf16[256,256]{1,0:T(8,128)(2,1)}, u32[]{:S(2)}) copy-start(bf16[256,256]{1,0:T(8,128)(2,1)} %constant.25.clone.rest_3_.refs_7_) | copy-start | bytes 393220
  29.1 17.2 %copy-start.14 = (bf16[256,256]{1,0:T(8,128)(2,1)S(1)}, bf16[256,256]{1,0:T(8,128)(2,1)}, u32[]{:S(2)}) copy-start(bf16[256,256]{1,0:T(8,128)(2,1)} %constant.24.clone.rest_2_.refs_6_) | copy-start | bytes 393220
  41.3 22.1 %all-to-all-start.1 = ((bf16[16,168,128]{2,1,0:T(8,128)(2,1)}), bf16[16,168,128]{2,1,0:T(8,128)(2,1)S(1)}, u32[]{:S(2)}, u32[]{:S(2)}) async-start(bf16[16,168,128]{2,1,0:T(8,128)(2,1)} %get-tuple-element.15), calls=%async_computation.1 | async-start | bytes 1376256 | tf_op jit(solution)/shard_map/all_to_all | solution.py:498
  46.3 1.2 %copy-start.16 = (bf16[2,4,256,256]{3,2,1,0:T(8,128)(2,1)S(1)}, bf16[2,4,256,256]{3,2,1,0:T(8,128)(2,1)}, u32[]{:S(2)}) copy-start(bf16[2,4,256,256]{3,2,1,0:T(8,128)(2,1)} %get-tuple-element.19.lagged_spec) | copy-start | bytes 3145732

commit v6 on v5

--- a/solution.py
+++ b/solution.py
@@ -142,10 +142,28 @@
     )
 
 
+def narrow_places(tables):
+    places, low = [], 0
+    for which in range(4):
+        rows, columns = tables[which].shape
+        for start in range(0, columns, 2 * LANES):
+            places.append((low, low + rows, which, slice(start, start + 2 * LANES)))
+            low += rows
+    return places
+
+
 def prepare_kernel(offsets, filters, table, short_taps, *rest):
     tables = rest[:6]
-    spectra, entries, taps = rest[6:]
-    taps[...] = jnp.broadcast_to(short_taps[...], taps.shape)
+    spectra, entries, narrow, wide = rest[6:]
+    for low, high, which, lanes in narrow_places(tables):
+        narrow[low:high] = tables[which][:, lanes]
+    count = short_taps.shape[1]
+    rows = tables[4].shape[0]
+    for tap in range(3):
+        wide[tap * count : (tap + 1) * count] = jnp.broadcast_to(short_taps[tap], (count, LANES))
+    for part in range(2):
+        start = 3 * count + part * rows
+        wide[start : start + rows] = tables[4 + part][...]
     chans, steps = filters.shape[1:]
     blocks = steps // LANES
     fields = offsets.shape[0]
@@ -284,7 +302,7 @@
         def ids_of(block):
             return ids[block]
 
-    far, refs = refs[:9], refs[9:]
+    (entries_far, filter_far, narrow_far, wide_far), refs = refs[:4], refs[4:]
     lagged_far, refs = refs[0], refs[1:]
     if packed_form:
         sent_far, refs = refs[0], refs[1:]
@@ -299,14 +317,23 @@
     tables = near[3:]
     blocks = mixed.shape[0]
     codes = LANES
+    count = taps.shape[1]
+    rows = tables[4].shape[0]
+    parts = [(wide_far.at[pl.ds(tap * count, count)], taps.at[tap]) for tap in range(3)]
+    parts.append((filter_far, filter_spec))
+    for low, high, which, lanes in narrow_places(tables):
+        lanes = pl.ds(lanes.start, 2 * LANES)
+        parts.append((narrow_far.at[pl.ds(low, high - low)], tables[which].at[:, lanes]))
+    for part in range(2):
+        parts.append((wide_far.at[pl.ds(3 * count + part * rows, rows)], tables[4 + part]))
     arrivals = [
         pltpu.make_async_copy(source, target, sems.at[place])
-        for place, (source, target) in enumerate(zip(far[1:], near[1:]))
+        for place, (source, target) in enumerate(parts)
     ]
     quarter = entries.shape[0] // QUARTERS
     quarters = [slice(part * quarter, (part + 1) * quarter) for part in range(QUARTERS)]
     entry_arrivals = [
-        pltpu.make_async_copy(far[0].at[rows], entries.at[rows], sems.at[len(arrivals) + part])
+        pltpu.make_async_copy(entries_far.at[rows], entries.at[rows], sems.at[len(arrivals) + part])
         for part, rows in enumerate(quarters)
     ]
     taken = len(arrivals) + QUARTERS
@@ -340,7 +367,8 @@
         copy.wait()
         coded.append(dot(entries[rows], w_cols).T[: 3 * chans].astype(BF16))
     coded = jnp.concatenate(coded, axis=1)
-    arrivals[0].wait()
+    for copy in arrivals[:3]:
+        copy.wait()
     lane = lax.broadcasted_iota(jnp.int32, (3 * chans, LANES), 1)
     last1 = jnp.zeros((3 * chans, LANES), F32)
     last2 = last1
@@ -365,7 +393,7 @@
     def blocked(value):
         return value.reshape(blocks, GROUP, LANES)
 
-    for copy in arrivals[1:]:
+    for copy in arrivals[3:]:
         copy.wait()
     for batch in batches(chans):
         value_spec = forward([column(mixed, group) for group in batch], tables)
@@ -581,7 +609,7 @@
 
     taps = short_taps.reshape(3, 3, peers, chans)
     taps = lax.dynamic_index_in_dim(taps, lax.axis_index("tm"), axis=2, keepdims=False)
-    filter_spec, entries, taps = call(
+    filter_spec, entries, narrow, wide_tables = call(
         prepare_kernel,
         "prepare",
         32,
@@ -589,7 +617,8 @@
         out_shape=(
             shape(spec, F32),
             shape(embed_table.shape, BF16),
-            shape((3, 3 * chans, LANES), F32),
+            shape((narrow_places(tables)[-1][1], 2 * LANES), BF16),
+            shape((9 * chans + 2 * peers * GROUP, LANES), F32),
         ),
         cost_estimate=pl.CostEstimate(
             flops=10**10, bytes_accessed=3 * 10**7, transcendentals=0
@@ -608,7 +637,8 @@
         )
         out_specs = (far, near, near, near)
         scratch_shapes = []
-    operands = (entries, taps, filter_spec) + tables
+    operands = (entries, filter_spec, narrow, wide_tables)
+    places = (entries, shape((3, 3 * chans, LANES), F32), filter_spec) + tables
     results = call(
         functools.partial(mixer_kernel, packed_form),
         "mixer",
@@ -616,9 +646,9 @@
         in_specs=[far if packed_form else near] * len(arrived) + [far] * len(operands),
         out_shape=out_shape,
         out_specs=out_specs,
-        scratch_shapes=[pltpu.VMEM(operand.shape, operand.dtype) for operand in operands]
+        scratch_shapes=[pltpu.VMEM(place.shape, place.dtype) for place in places]
         + [
-            pltpu.SemaphoreType.DMA((len(operands) + groups + 2 * QUARTERS,)),
+            pltpu.SemaphoreType.DMA((len(narrow_places(tables)) + 8 + groups + 2 * QUARTERS,)),
             pltpu.VMEM(spec, BF16),
             pltpu.VMEM((embed_table.shape[0], steps), BF16),
             pltpu.VMEM(wide, BF16),

time: 65 us -> 64.3 us (0.989)
  waiting for transfers between devices: 23.6 us -> 22.6 us
    all_to_all x2, waiting for transfers between devices: 23.6 us -> 22.6 us  [exchange(): return lax.all_to_all(blocks, 'tm', split_axis=0, concat_axis=0, tiled=True)]
    unnamed x42 -> x30, local copies, waits for them, and re-layouts: 7.07 us -> 7.18 us
where the time goes in v6:
time: 64.3 us; the launch traced here: 63.8 us
  waiting for transfers between devices  22.6 us (35%)
  Pallas kernels  20.3 us (32%)
  starting transfers between devices  12.4 us (19%)
  local copies, waits for them, and re-layouts  7.58 us (12%)
  between operations  0.85 us (1%)
    all_to_all x2, waiting for transfers between devices, exchange(): return lax.all_to_all(blocks, 'tm', split_axis=0, concat_axis=0, tiled=True)  22.6 us
    all_to_all x2, starting transfers between devices, exchange(): return lax.all_to_all(blocks, 'tm', split_axis=0, concat_axis=0, tiled=True)  12.4 us
    pallas_call x1, Pallas kernels, local(): call(functools.partial(mixer_kernel, packed_form), 'mixer', MIX_MB, in_sp...  12.1 us
    unnamed x30, local copies, waits for them, and re-layouts  7.18 us
    pallas_call x1, Pallas kernels, local(): call(pack_kernel, 'pack', PACK_MB, in_specs=[near, far, far], out_specs=f...  2.97 us
    pallas_call x1, Pallas kernels, local(): call(prepare_kernel, 'prepare', 32, in_specs=[pl.BlockSpec(memory_space=p...  2.09 us
    pallas_call x1, Pallas kernels, local(): call(lagged_kernel, 'lagged', 24, out_shape=shape((2, chans, steps), F32)...  1.92 us
  transfers between devices with their start and end apart: 2, of which 2 were waited for; matrix products, arithmetic and copies ran while one was open for 1% of the time, Pallas kernels for 6%

profile of v6, /device:TPU:0, one launch (start us, length us, event | category | flops | bytes accessed | tf_op | source)
XLA Modules:
  0.0 63.8 jit_solution(7060700597276052655)
XLA Ops:
  0.6 0.0 copy-start.10
  0.6 0.0 copy-start.11
  0.7 0.0 copy-start.12
  0.7 0.0 copy-start.13
  0.7 0.0 copy-start.8
  0.7 0.0 copy-start.9
  0.7 0.0 copy-start.14
  0.7 0.0 copy-start.6
  0.7 0.0 copy-start.7
  0.7 3.0 %pack.1 = bf16[16,168,128]{2,1,0:T(8,128)(2,1)} custom-call(s32[8,128]{1,0:T(8,128)} %bitcast.1, bf16[64,3072]{1,0:T(8,128)(2,1)} %w_in_far.1, bf16[128,1024]{1,0:T(8,128)(2,1)} %cotangent_far.1), custom_call_target="tpu_custom_call" | custom-call | tf_op jit(solution)/shard_map/pack/pallas_call | solution.py:592
  3.7 7.4 %all-to-all-start = ((bf16[16,168,128]{2,1,0:T(8,128)(2,1)}), bf16[16,168,128]{2,1,0:T(8,128)(2,1)}, u32[]{:S(2)}, u32[]{:S(2)}) async-start(bf16[16,168,128]{2,1,0:T(8,128)(2,1)} %pack.1), calls=%async_computation | async-start | bytes 1376256 | tf_op jit(solution)/shard_map/all_to_all | solution.py:526
  11.2 0.0 copy-done.14
  11.2 0.1 reshape.15
  11.3 0.3 reshape.19.short_taps
  11.6 0.0 copy-done.10
  11.6 0.0 copy-done.11
  11.6 0.0 copy-done.12
  11.6 0.0 copy-done.13
  11.6 0.0 copy-done.8
  11.6 0.0 copy-done.9
  11.6 0.0 copy-done.6
  11.7 0.0 copy-done.7
  11.7 0.0 copy-start.4
  11.7 1.6 %copy-done.4 = bf16[1024,1024]{1,0:T(8,128)(2,1)S(1)} copy-done((bf16[1024,1024]{1,0:T(8,128)(2,1)S(1)}, bf16[1024,1024]{1,0:T(8,128)(2,1)}, u32[]{:S(2)}) %copy-start.4) | copy-done | bytes 2097176
  13.3 2.1 %prepare.1 = (f32[2,4,256,256]{3,2,1,0:T(8,128)S(1)}, bf16[1024,1024]{1,0:T(8,128)(2,1)S(1)}, bf16[1536,256]{1,0:T(8,128)(2,1)S(1)}, f32[1088,128]{1,0:T(8,128)S(1)}) custom-call(s32[8]{0:T(128)S(1)} %copy-done.7, bf16[2,64,2048]{2,1,0:T(8,128)(2,1)S(1)} %copy-done.6, bf16[1024,1024]{1,0:T(8,128)(2,1)S(1)} %copy-done.4, ...), custom_call_target="tpu_custom_call" | custom-call | flops 10000000000 | bytes 30000000 | tf_op jit(solution)/shard_map/prepare/pallas_call | solution.py:612
  15.4 0.0 copy-start
  15.4 1.3 %copy-done = f32[2,4,256,256]{3,2,1,0:T(8,128)} copy-done((f32[2,4,256,256]{3,2,1,0:T(8,128)}, f32[2,4,256,256]{3,2,1,0:T(8,128)S(1)}, u32[]{:S(2)}) %copy-start) | copy-done | bytes 2097176
  16.7 0.0 copy-start.1
  16.7 1.3 %copy-done.1 = bf16[1024,1024]{1,0:T(8,128)(2,1)} copy-done((bf16[1024,1024]{1,0:T(8,128)(2,1)}, bf16[1024,1024]{1,0:T(8,128)(2,1)S(1)}, u32[]{:S(2)}) %copy-start.1) | copy-done | bytes 2097176
  18.0 0.0 copy-start.2
  18.0 0.9 %copy-done.2 = bf16[1536,256]{1,0:T(8,128)(2,1)} copy-done((bf16[1536,256]{1,0:T(8,128)(2,1)}, bf16[1536,256]{1,0:T(8,128)(2,1)S(1)}, u32[]{:S(2)}) %copy-start.2) | copy-done | bytes 786456
  18.9 0.0 copy-start.3
  18.9 0.8 %copy-done.3 = f32[1088,128]{1,0:T(8,128)} copy-done((f32[1088,128]{1,0:T(8,128)}, f32[1088,128]{1,0:T(8,128)S(1)}, u32[]{:S(2)}) %copy-start.3) | copy-done | bytes 557080
  19.7 8.7 %all-to-all-done.refs_0_ = bf16[16,168,128]{2,1,0:T(8,128)(2,1)} async-done(((bf16[16,168,128]{2,1,0:T(8,128)(2,1)}), bf16[16,168,128]{2,1,0:T(8,128)(2,1)}, u32[]{:S(2)}, u32[]{:S(2)}) %all-to-all-start) | async-done | bytes 688160 | tf_op jit(solution)/shard_map/all_to_all | solution.py:526
  28.4 12.1 %mixer.1 = (bf16[2,4,256,256]{3,2,1,0:T(8,128)(2,1)}, bf16[16,168,128]{2,1,0:T(8,128)(2,1)}) custom-call(bf16[16,168,128]{2,1,0:T(8,128)(2,1)} %all-to-all-done.refs_0_, bf16[1024,1024]{1,0:T(8,128)(2,1)} %copy-done.1, f32[2,4,256,256]{3,2,1,0:T(8,128)} %copy-done, bf16[1536,256]{1,0:T(8,128)(2,1)} %copy-done.2, f32[1088,128]{1,0:T(8,128)} %copy-done.3), custom_call_target="tpu_custom_call" | custom-call | tf_op jit(solution)/shard_map/mixer/pallas_call | solution.py:642
  40.5 5.0 %all-to-all-start.1 = ((bf16[16,168,128]{2,1,0:T(8,128)(2,1)}), bf16[16,168,128]{2,1,0:T(8,128)(2,1)S(1)}, u32[]{:S(2)}, u32[]{:S(2)}) async-start(bf16[16,168,128]{2,1,0:T(8,128)(2,1)} %get-tuple-element.17), calls=%async_computation.1 | async-start | bytes 1376256 | tf_op jit(solution)/shard_map/all_to_all | solution.py:526
  45.4 0.0 copy-start.5
  45.5 1.2 %copy-done.5 = bf16[2,4,256,256]{3,2,1,0:T(8,128)(2,1)S(1)} copy-done((bf16[2,4,256,256]{3,2,1,0:T(8,128)(2,1)S(1)}, bf16[2,4,256,256]{3,2,1,0:T(8,128)(2,1)}, u32[]{:S(2)}) %copy-start.5) | copy-done | bytes 1048600
  46.7 1.9 %lagged.1 = f32[2,64,2048]{2,1,0:T(8,128)} custom-call(bf16[2,4,256,256]{3,2,1,0:T(8,128)(2,1)S(1)} %copy-done.5, bf16[512,256]{1,0:T(8,128)(2,1)S(1)} %copy-done.9, bf16[256,512]{1,0:T(8,128)(2,1)S(1)} %copy-done.8, bf16[256,256]{1,0:T(8,128)(2,1)S(1)} %copy-done.13, bf16[256,256]{1,0:T(8,128)(2,1)S(1)} %copy-done.12, f32[256,128]{1,0:T(8,128)S(1)} %copy-done.11, ...), custom_call_target="tpu_custom_call" | custom-call | flops 10000000000 | bytes 30000000 | tf_op jit(solution)/shard_map/lagged/pallas_call | solution.py:661
  48.6 14.0 %all-to-all-done.1.packed = bf16[16,168,128]{2,1,0:T(8,128)(2,1)S(1)} async-done(((bf16[16,168,128]{2,1,0:T(8,128)(2,1)}), bf16[16,168,128]{2,1,0:T(8,128)(2,1)S(1)}, u32[]{:S(2)}, u32[]{:S(2)}) %all-to-all-start.1) | async-done | bytes 688160 | tf_op jit(solution)/shard_map/all_to_all | solution.py:526
  62.6 1.2 %unpack.1 = (bf16[128,1024]{1,0:T(8,128)(2,1)}, f32[64,3072]{1,0:T(8,128)}, f32[3,3072]{1,0:T(4,128)}) custom-call(bf16[16,168,128]{2,1,0:T(8,128)(2,1)S(1)} %all-to-all-done.1.packed), custom_call_target="tpu_custom_call" | custom-call | tf_op jit(solution)/shard_map/unpack/pallas_call | solution.py:671
  (1 shorter events, 0.0 us)
Async XLA Ops:
  0.6 11.0 %copy-start.10 = (f32[256,128]{1,0:T(8,128)S(1)}, f32[256,128]{1,0:T(8,128)}, u32[]{:S(2)}) copy-start(f32[256,128]{1,0:T(8,128)} %constant.27.clone.rest_5_) | copy-start | bytes 393220
  0.6 11.0 %copy-start.11 = (f32[256,128]{1,0:T(8,128)S(1)}, f32[256,128]{1,0:T(8,128)}, u32[]{:S(2)}) copy-start(f32[256,128]{1,0:T(8,128)} %constant.26.clone.rest_4_) | copy-start | bytes 393220
  0.7 11.0 %copy-start.12 = (bf16[256,256]{1,0:T(8,128)(2,1)S(1)}, bf16[256,256]{1,0:T(8,128)(2,1)}, u32[]{:S(2)}) copy-start(bf16[256,256]{1,0:T(8,128)(2,1)} %constant.25.clone.rest_3_) | copy-start | bytes 393220
  0.7 10.9 %copy-start.13 = (bf16[256,256]{1,0:T(8,128)(2,1)S(1)}, bf16[256,256]{1,0:T(8,128)(2,1)}, u32[]{:S(2)}) copy-start(bf16[256,256]{1,0:T(8,128)(2,1)} %constant.24.clone.rest_2_) | copy-start | bytes 393220
  0.7 10.9 %copy-start.8 = (bf16[256,512]{1,0:T(8,128)(2,1)S(1)}, bf16[256,512]{1,0:T(8,128)(2,1)}, u32[]{:S(2)}) copy-start(bf16[256,512]{1,0:T(8,128)(2,1)} %constant.23.clone.rest_1_) | copy-start | bytes 786436
  0.7 10.9 %copy-start.9 = (bf16[512,256]{1,0:T(8,128)(2,1)S(1)}, bf16[512,256]{1,0:T(8,128)(2,1)}, u32[]{:S(2)}) copy-start(bf16[512,256]{1,0:T(8,128)(2,1)} %constant.22.clone.rest_0_) | copy-start | bytes 786436
  0.7 10.5 %copy-start.14 = (f32[3,3072]{1,0:T(4,128)S(1)}, f32[3,3072]{1,0:T(4,128)}, u32[]{:S(2)}) copy-start(f32[3,3072]{1,0:T(4,128)} %param.17) | copy-start | bytes 110596
  0.7 10.9 %copy-start.6 = (bf16[2,64,2048]{2,1,0:T(8,128)(2,1)S(1)}, bf16[2,64,2048]{2,1,0:T(8,128)(2,1)}, u32[]{:S(2)}) copy-start(bf16[2,64,2048]{2,1,0:T(8,128)(2,1)} %filters.1) | copy-start | bytes 1572868
  0.7 10.9 %copy-start.7 = (s32[8]{0:T(128)S(1)}, s32[8]{0:T(128)}, u32[]{:S(2)}) copy-start(s32[8]{0:T(128)} %offsets.1) | copy-start | bytes 100
  3.7 24.6 %all-to-all-start = ((bf16[16,168,128]{2,1,0:T(8,128)(2,1)}), bf16[16,168,128]{2,1,0:T(8,128)(2,1)}, u32[]{:S(2)}, u32[]{:S(2)}) async-start(bf16[16,168,128]{2,1,0:T(8,128)(2,1)} %pack.1), calls=%async_computation | async-start | bytes 1376256 | tf_op jit(solution)/shard_map/all_to_all | solution.py:526
  11.7 1.6 %copy-start.4 = (bf16[1024,1024]{1,0:T(8,128)(2,1)S(1)}, bf16[1024,1024]{1,0:T(8,128)(2,1)}, u32[]{:S(2)}) copy-start(bf16[1024,1024]{1,0:T(8,128)(2,1)} %table.1) | copy-start | bytes 6291460
  15.4 1.3 %copy-start = (f32[2,4,256,256]{3,2,1,0:T(8,128)}, f32[2,4,256,256]{3,2,1,0:T(8,128)S(1)}, u32[]{:S(2)}) copy-start(f32[2,4,256,256]{3,2,1,0:T(8,128)S(1)} %get-tuple-element.14.refs_2_) | copy-start | bytes 6291460
  16.7 1.3 %copy-start.1 = (bf16[1024,1024]{1,0:T(8,128)(2,1)}, bf16[1024,1024]{1,0:T(8,128)(2,1)S(1)}, u32[]{:S(2)}) copy-start(bf16[1024,1024]{1,0:T(8,128)(2,1)S(1)} %get-tuple-element.13.refs_1_) | copy-start | bytes 6291460
  18.0 0.9 %copy-start.2 = (bf16[1536,256]{1,0:T(8,128)(2,1)}, bf16[1536,256]{1,0:T(8,128)(2,1)S(1)}, u32[]{:S(2)}) copy-start(bf16[1536,256]{1,0:T(8,128)(2,1)S(1)} %get-tuple-element.15.refs_3_) | copy-start | bytes 2359300
  18.9 0.8 %copy-start.3 = (f32[1088,128]{1,0:T(8,128)}, f32[1088,128]{1,0:T(8,128)S(1)}, u32[]{:S(2)}) copy-start(f32[1088,128]{1,0:T(8,128)S(1)} %get-tuple-element.16.refs_4_) | copy-start | bytes 1671172
  40.5 22.1 %all-to-all-start.1 = ((bf16[16,168,128]{2,1,0:T(8,128)(2,1)}), bf16[16,168,128]{2,1,0:T(8,128)(2,1)S(1)}, u32[]{:S(2)}, u32[]{:S(2)}) async-start(bf16[16,168,128]{2,1,0:T(8,128)(2,1)} %get-tuple-element.17), calls=%async_computation.1 | async-start | bytes 1376256 | tf_op jit(solution)/shard_map/all_to_all | solution.py:526
  45.4 1.2 %copy-start.5 = (bf16[2,4,256,256]{3,2,1,0:T(8,128)(2,1)S(1)}, bf16[2,4,256,256]{3,2,1,0:T(8,128)(2,1)}, u32[]{:S(2)}) copy-start(bf16[2,4,256,256]{3,2,1,0:T(8,128)(2,1)} %get-tuple-element.21.lagged_spec) | copy-start | bytes 3145732
